TPU v7x, 32 devices: a whole 2x2x4 slice. The times are simulated.
32 devices in a mesh: dp: 8 (over y, x, core), expert: 4 (over z), tensor: 1.
Axes of the slice: x: 2, y: 2, z: 4, core: 2. Of those that a mesh axis runs over, the one named last changes fastest.
Arguments:
- tokens: bfloat16 [2048, 4096], P(('dp', 'expert'), 'tensor'), may hold values from -6 to 6
- expert_ids: int32 [2048, 8], P(('dp', 'expert')), may hold values from 0 to 31, all different within a row; in each aligned block of 64 rows (0 to 63, 64 to 127, ...) at most 24 rows name the same one
- combine_weights: float32 [2048, 8], P(('dp', 'expert')), may hold values from 0.05 to 1
- topology: int32 [32, 12, 12], P(('dp', 'expert'), 'tensor'), may hold values from 0 to 31, all different within a row
- gate_blocks: bfloat16 [32, 12, 12, 128, 128], P(('dp', 'expert'), 'tensor'), may hold values from -0.15625 to 0.15625
- up_blocks: bfloat16 [32, 12, 12, 128, 128], P(('dp', 'expert'), 'tensor'), may hold values from -0.15625 to 0.15625
- down_blocks: bfloat16 [32, 12, 12, 128, 128], P(('dp', 'expert'), 'tensor'), may hold values from -0.25 to 0.25
Outputs:
- layer_out: bfloat16 [2048, 4096], P(('dp', 'expert'), 'tensor')
Inputs may be any that keep to these rules, and one draw needn't show every extreme that they name: `expert_ids`: in each aligned block of 64 tokens (the tokens of one index of dp+expert), no expert is named more than 24 times, a bound that some block reaches; a token names 8 different experts. `topology`: each row names 12 different blocks; every block is named by some row.
All inputs are finite; a program needn't handle non-finite values.
Results may differ from a plain program's by a relative error of at most 0.0058.
Values may be sent and summed in bfloat16 or wider, within the bound.
No kernel may reach another device: no remote copies, remote signals or barrier semaphores. Data moves between devices by JAX's collectives and lax.ppermute only.
A program may use at most 256 MiB of HBM per device.

v0:
```python
import jax
import jax.numpy as jnp
from jax import lax
from jax.sharding import PartitionSpec as P

D = 4096
TOP = 8
BLK = 128


def slot_numbers(expert_ids, experts):
    flat_ids = expert_ids.reshape(-1)
    onehot = (flat_ids[:, None] == jnp.arange(experts, dtype=jnp.int32)[None, :]).astype(jnp.int32)
    before = jnp.cumsum(onehot, axis=0) - onehot
    return jnp.sum(before * onehot, axis=1).reshape(expert_ids.shape)


def combine_rows(flat_rows, target, combine_weights):
    total = jnp.zeros((target.shape[0], flat_rows.shape[1]), jnp.float32)
    for pick in range(target.shape[1]):
        chosen = jnp.take(flat_rows, target[:, pick], axis=0)
        total = total + combine_weights[:, pick][:, None] * chosen
    return total


def per_device(tokens, expert_ids, combine_weights, topology, gate_blocks, up_blocks, down_blocks):
    experts = lax.axis_size(("dp", "expert"))
    tok_rows = tokens.shape[0]
    capacity = min(tok_rows, 3 * tok_rows * TOP // (2 * experts))
    slot_index = slot_numbers(expert_ids, experts)
    target = expert_ids * capacity + slot_index
    places = jnp.arange(experts * capacity, dtype=jnp.int32)
    matches = target[None, :, :] == places[:, None, None]
    dispatch = jnp.any(matches, axis=2).astype(jnp.bfloat16)
    outgoing = jnp.dot(dispatch, tokens, preferred_element_type=jnp.float32).astype(jnp.bfloat16)
    outgoing = outgoing.reshape(experts, capacity, tokens.shape[1])
    arrived = lax.all_to_all(outgoing, ("dp", "expert"), split_axis=0, concat_axis=0, tiled=True)
    expert_in = lax.all_gather(arrived, "tensor", axis=2, tiled=True)
    row_count = experts * capacity
    layout_ids = topology[0]
    local_blocks = layout_ids.shape[0]
    blocked = expert_in.reshape(row_count, D // BLK, BLK)
    width_ids = jnp.arange(D // BLK, dtype=jnp.int32)
    partial_value = jnp.zeros((row_count, D // BLK, BLK), jnp.float32)
    for block in range(local_blocks):
        chosen = layout_ids[block]
        picked = jnp.take(blocked, chosen, axis=1)
        gate_proj = jnp.einsum(
            "rkc,kcf->rf", picked, gate_blocks[0, block], preferred_element_type=jnp.float32
        )
        up_proj = jnp.einsum(
            "rkc,kcf->rf", picked, up_blocks[0, block], preferred_element_type=jnp.float32
        )
        hidden = (jax.nn.silu(gate_proj) * up_proj).astype(jnp.bfloat16)
        pieces = jnp.einsum(
            "rf,kfc->rkc", hidden, down_blocks[0, block], preferred_element_type=jnp.float32
        )
        placer = (chosen[:, None] == width_ids[None, :]).astype(jnp.float32)
        partial_value = partial_value + jnp.einsum(
            "rkc,kb->rbc", pieces, placer, precision=lax.Precision.HIGHEST
        )
    partial_low = lax.optimization_barrier(
        partial_value.reshape(experts, capacity, D).astype(jnp.bfloat16)
    )
    shares = lax.all_to_all(
        partial_low.reshape(1, experts, capacity, D),
        "tensor",
        split_axis=3,
        concat_axis=0,
        tiled=True,
    )
    summed = jnp.sum(shares.astype(jnp.float32), axis=0)
    returned_rows = lax.all_to_all(
        summed, ("dp", "expert"), split_axis=0, concat_axis=0, tiled=True
    )
    flat_rows = returned_rows.reshape(row_count, returned_rows.shape[2])
    combined = combine_rows(flat_rows, target, combine_weights)
    return combined.astype(jnp.bfloat16)


def solution(mesh):
    return jax.shard_map(
        per_device,
        mesh=mesh,
        in_specs=(
            P(("dp", "expert"), "tensor"),
            P(("dp", "expert"), None),
            P(("dp", "expert"), None),
            P(("dp", "expert"), "tensor", None),
            P(("dp", "expert"), "tensor", None, None, None),
            P(("dp", "expert"), "tensor", None, None, None),
            P(("dp", "expert"), "tensor", None, None, None),
        ),
        out_specs=P(("dp", "expert"), "tensor"),
        check_vma=False,
    )
```

profile of v0, /device:TPU:0, one launch (start us, length us, event | category | flops | bytes accessed | tf_op | source)
XLA Modules:
  0.0 850.2 jit_solution(1513225719281895106)
XLA Ops:
  4.1 4.5 convolution_convert_fusion
  8.6 7.9 all-to-all-start
  16.7 136.2 %all-to-all-done = bf16[32,24,4096]{2,1,0:T(8,128)(2,1)} async-done(((bf16[32,24,4096]{2,1,0:T(8,128)(2,1)}), bf16[32,24,4096]{2,1,0:T(8,128)(2,1)}, u32[]{:S(2)}, u32[]{:S(2)}) %all-to-all-start) | async-done | bytes 6291488 | tf_op jit(solution)/shard_map/all_to_all | solution.py:37
  152.9 4.8 copy.102
  157.7 5.1 copy.77
  162.9 5.2 gather_fusion.6
  168.0 3.8 gather_fusion.5
  171.8 2.5 fusion.112
  174.3 1.8 fusion.106
  176.1 6.6 fusion.283
  182.8 5.8 fusion.280
  188.5 3.8 gather_fusion.4
  192.3 1.8 fusion.100
  194.1 5.9 fusion.277
  200.1 4.0 gather_fusion.3
  204.0 1.8 fusion.94
  205.8 5.8 fusion.274
  211.6 3.8 gather_fusion.2
  215.4 1.8 fusion.88
  217.2 5.9 fusion.271
  223.1 3.8 gather_fusion.1
  226.9 1.8 fusion.82
  228.7 5.9 fusion.268
  234.6 3.8 gather_fusion.9
  240.2 5.9 fusion.292
  246.1 3.8 gather_fusion.8
  249.9 1.8 fusion.124
  251.7 6.0 fusion.289
  257.7 3.8 gather_fusion.7
  261.5 1.8 fusion.118
  263.3 5.8 fusion.286
  269.1 3.8 gather_fusion.10
  272.8 1.8 fusion.136
  274.6 5.8 fusion.295
  280.4 3.8 gather_fusion.11
  284.2 1.8 fusion.142
  286.0 5.8 fusion.298
  291.9 3.8 gather_fusion
  297.5 6.3 fusion.265
  303.8 13.7 %fusion.10 = f32[32,768,128]{2,0,1:T(8,128)} fusion(f32[768,12,128]{2,0,1:T(8,128)} %fusion.283, s32[12]{0:T(128)S(1)} %get-tuple-element.51), kind=kOutput, calls=%fused_computation.32 | convolution fusion | flops 452985216 | bytes 17301552 | tf_op jit(solution)/shard_map/rkc,kb->rbc/dot_general | solution.py:59
  317.5 12.8 %fusion.12 = f32[32,768,128]{2,0,1:T(8,128)} fusion(f32[768,12,128]{2,0,1:T(8,128)S(1)} %bitcast.685, s32[12]{0:T(128)S(1)} %get-tuple-element.52), kind=kOutput, calls=%fused_computation.34 | convolution fusion | flops 452985216 | bytes 17301552 | tf_op jit(solution)/shard_map/rkc,kb->rbc/dot_general | solution.py:59
  330.3 12.8 %fusion.14 = f32[32,768,128]{2,0,1:T(8,128)} fusion(f32[768,12,128]{2,0,1:T(8,128)S(1)} %bitcast.687, s32[12]{0:T(128)S(1)} %get-tuple-element.53), kind=kOutput, calls=%fused_computation.36 | convolution fusion | flops 452985216 | bytes 17301552 | tf_op jit(solution)/shard_map/rkc,kb->rbc/dot_general | solution.py:59
  343.2 12.9 %fusion.16 = f32[32,768,128]{2,0,1:T(8,128)} fusion(f32[768,12,128]{2,0,1:T(8,128)S(1)} %bitcast.689, s32[12]{0:T(128)S(1)} %get-tuple-element.54), kind=kOutput, calls=%fused_computation.38 | convolution fusion | flops 452985216 | bytes 17301552 | tf_op jit(solution)/shard_map/rkc,kb->rbc/dot_general | solution.py:59
  356.2 12.8 %fusion.18 = f32[32,768,128]{2,0,1:T(8,128)} fusion(f32[768,12,128]{2,0,1:T(8,128)S(1)} %bitcast.691, s32[12]{0:T(128)S(1)} %get-tuple-element.55), kind=kOutput, calls=%fused_computation.40 | convolution fusion | flops 452985216 | bytes 17301552 | tf_op jit(solution)/shard_map/rkc,kb->rbc/dot_general | solution.py:59
  368.9 12.7 %fusion.20 = f32[32,768,128]{2,0,1:T(8,128)} fusion(f32[768,12,128]{2,0,1:T(8,128)S(1)} %bitcast.693, s32[12]{0:T(128)S(1)} %get-tuple-element.56), kind=kOutput, calls=%fused_computation.42 | convolution fusion | flops 452985216 | bytes 17301552 | tf_op jit(solution)/shard_map/rkc,kb->rbc/dot_general | solution.py:59
  381.7 13.0 %fusion.4 = f32[32,768,128]{2,0,1:T(8,128)} fusion(f32[768,12,128]{2,0,1:T(8,128)S(1)} %bitcast.695, s32[12]{0:T(128)S(1)} %get-tuple-element.48), kind=kOutput, calls=%fused_computation.26 | convolution fusion | flops 452985216 | bytes 17301552 | tf_op jit(solution)/shard_map/rkc,kb->rbc/dot_general | solution.py:59
  394.7 12.8 %fusion.6 = f32[32,768,128]{2,0,1:T(8,128)} fusion(f32[768,12,128]{2,0,1:T(8,128)S(1)} %bitcast.697, s32[12]{0:T(128)S(1)} %get-tuple-element.49), kind=kOutput, calls=%fused_computation.28 | convolution fusion | flops 452985216 | bytes 17301552 | tf_op jit(solution)/shard_map/rkc,kb->rbc/dot_general | solution.py:59
  407.5 12.7 %fusion.8 = f32[32,768,128]{2,0,1:T(8,128)} fusion(f32[768,12,128]{2,0,1:T(8,128)S(1)} %bitcast.699, s32[12]{0:T(128)S(1)} %get-tuple-element.50), kind=kOutput, calls=%fused_computation.30 | convolution fusion | flops 452985216 | bytes 17301552 | tf_op jit(solution)/shard_map/rkc,kb->rbc/dot_general | solution.py:59
  420.2 13.2 %fusion.2 = f32[32,768,128]{2,0,1:T(8,128)} fusion(f32[768,12,128]{2,0,1:T(8,128)S(1)} %bitcast.701, s32[12]{0:T(128)S(1)} %get-tuple-element.58), kind=kOutput, calls=%fused_computation.24 | convolution fusion | flops 452985216 | bytes 17301552 | tf_op jit(solution)/shard_map/rkc,kb->rbc/dot_general | solution.py:59
  433.4 12.7 %fusion = f32[32,768,128]{2,0,1:T(8,128)} fusion(f32[768,12,128]{2,0,1:T(8,128)S(1)} %bitcast.703, s32[12]{0:T(128)S(1)} %get-tuple-element.57), kind=kOutput, calls=%fused_computation.22 | convolution fusion | flops 452985216 | bytes 17301552 | tf_op jit(solution)/shard_map/rkc,kb->rbc/dot_general | solution.py:59
  446.2 47.8 %fusion.24 = bf16[768,32,128]{2,1,0:T(8,128)(2,1)} fusion(f32[32,768,128]{2,0,1:T(8,128)} %fusion, f32[32,768,128]{2,0,1:T(8,128)} %fusion.2, f32[32,768,128]{2,0,1:T(8,128)} %fusion.4, f32[32,768,128]{2,0,1:T(8,128)} %fusion.6, f32[32,768,128]{2,0,1:T(8,128)} %fusion.8, f32[32,768,128]{2,0,1:T(8,128)} %fusion.10, f32[32,768,128]{2,0,1:T(8,128)} %fusion.12, ...), kind=kOutput, calls=%fused_computation.46 | convolution fusion | flops 490733952 | bytes 149422128 | tf_op jit(solution)/shard_map/rkc,kb->rbc/dot_general | solution.py:59
  494.0 10.3 %convert_element_type.88 = bf16[32,24,4096]{2,1,0:T(8,128)(2,1)} reshape(bf16[768,32,128]{2,1,0:T(8,128)(2,1)} %fusion.24) | data formatting | bytes 12582912 | tf_op jit(solution)/shard_map/convert_element_type | solution.py:63
  504.3 9.1 %convert_element_type.89 = f32[32,24,4096]{2,1,0:T(8,128)} convert(bf16[32,24,4096]{2,1,0:T(8,128)(2,1)} %convert_element_type.88) | non-fusion elementwise | flops 3145728 | bytes 18874368 | tf_op jit(solution)/shard_map/convert_element_type | solution.py:72
  513.4 7.3 all-to-all-start.1
  520.8 270.8 %all-to-all-done.1 = f32[32,24,4096]{2,1,0:T(8,128)} async-done(((f32[32,24,4096]{2,1,0:T(8,128)}), f32[32,24,4096]{2,1,0:T(8,128)}, u32[]{:S(2)}, u32[]{:S(2)}) %all-to-all-start.1) | async-done | bytes 12582944 | tf_op jit(solution)/shard_map/all_to_all | solution.py:73
  791.5 6.0 gather_fusion.12
  797.5 6.0 gather_fusion.13
  803.5 6.9 gather_fusion.14
  810.4 6.9 gather_fusion.15
  817.3 6.9 gather_fusion.16
  824.1 6.9 gather_fusion.17
  831.0 6.9 gather_fusion.18
  837.9 6.9 gather_fusion.19
  844.9 5.1 fusion.257
  (92 shorter events, 7.9 us)
Async XLA Ops:
  0.0 4.1 copy-start
  3.4 5.2 copy-start.2
  8.6 7.9 copy-start.4
  8.6 144.3 %all-to-all-start = ((bf16[32,24,4096]{2,1,0:T(8,128)(2,1)}), bf16[32,24,4096]{2,1,0:T(8,128)(2,1)}, u32[]{:S(2)}, u32[]{:S(2)}) async-start(bf16[32,24,4096]{2,1,0:T(8,128)(2,1)} %bitcast.683), calls=%async_computation | async-start | bytes 12582912 | tf_op jit(solution)/shard_map/all_to_all | solution.py:37
  297.5 20.0 %slice-start = ((s8[4718592]{0:T(1024)(128)(4,1)}), s8[524288]{0:T(1024)(128)(4,1)S(1)}, s32[]{:S(2)}) async-start(s8[4718592]{0:T(1024)(128)(4,1)} %bitcast.684), calls=%async_computation.2 | async-start | bytes 1048576
  303.8 13.7 %slice-start.1 = ((s8[4718592]{0:T(1024)(128)(4,1)}), s8[4194304]{0:T(1024)(128)(4,1)S(1)}, s32[]{:S(2)}) async-start(s8[4718592]{0:T(1024)(128)(4,1)} %bitcast.684), calls=%async_computation.3 | async-start | bytes 8388608
  303.8 26.5 %slice-start.2 = ((s8[4718592]{0:T(1024)(128)(4,1)}), s8[4194304]{0:T(1024)(128)(4,1)S(1)}, s32[]{:S(2)}) async-start(s8[4718592]{0:T(1024)(128)(4,1)} %bitcast.686), calls=%async_computation.4 | async-start | bytes 8388608
  317.5 12.8 %slice-start.3 = ((s8[4718592]{0:T(1024)(128)(4,1)}), s8[524288]{0:T(1024)(128)(4,1)S(1)}, s32[]{:S(2)}) async-start(s8[4718592]{0:T(1024)(128)(4,1)} %bitcast.686), calls=%async_computation.5 | async-start | bytes 1048576
  317.5 25.7 %slice-start.4 = ((s8[4718592]{0:T(1024)(128)(4,1)}), s8[4194304]{0:T(1024)(128)(4,1)S(1)}, s32[]{:S(2)}) async-start(s8[4718592]{0:T(1024)(128)(4,1)} %bitcast.688), calls=%async_computation.6 | async-start | bytes 8388608
  330.3 12.9 %slice-start.5 = ((s8[4718592]{0:T(1024)(128)(4,1)}), s8[524288]{0:T(1024)(128)(4,1)S(1)}, s32[]{:S(2)}) async-start(s8[4718592]{0:T(1024)(128)(4,1)} %bitcast.688), calls=%async_computation.7 | async-start | bytes 1048576
  330.3 25.8 %slice-start.6 = ((s8[4718592]{0:T(1024)(128)(4,1)}), s8[4194304]{0:T(1024)(128)(4,1)S(1)}, s32[]{:S(2)}) async-start(s8[4718592]{0:T(1024)(128)(4,1)} %bitcast.690), calls=%async_computation.8 | async-start | bytes 8388608
  343.2 13.0 %slice-start.7 = ((s8[4718592]{0:T(1024)(128)(4,1)}), s8[524288]{0:T(1024)(128)(4,1)S(1)}, s32[]{:S(2)}) async-start(s8[4718592]{0:T(1024)(128)(4,1)} %bitcast.690), calls=%async_computation.9 | async-start | bytes 1048576
  343.2 25.7 %slice-start.8 = ((s8[4718592]{0:T(1024)(128)(4,1)}), s8[4194304]{0:T(1024)(128)(4,1)S(1)}, s32[]{:S(2)}) async-start(s8[4718592]{0:T(1024)(128)(4,1)} %bitcast.692), calls=%async_computation.10 | async-start | bytes 8388608
  356.1 12.8 %slice-start.9 = ((s8[4718592]{0:T(1024)(128)(4,1)}), s8[524288]{0:T(1024)(128)(4,1)S(1)}, s32[]{:S(2)}) async-start(s8[4718592]{0:T(1024)(128)(4,1)} %bitcast.692), calls=%async_computation.11 | async-start | bytes 1048576
  356.1 25.5 %slice-start.10 = ((s8[4718592]{0:T(1024)(128)(4,1)}), s8[4194304]{0:T(1024)(128)(4,1)S(1)}, s32[]{:S(2)}) async-start(s8[4718592]{0:T(1024)(128)(4,1)} %bitcast.694), calls=%async_computation.12 | async-start | bytes 8388608
  368.9 12.8 %slice-start.11 = ((s8[4718592]{0:T(1024)(128)(4,1)}), s8[524288]{0:T(1024)(128)(4,1)S(1)}, s32[]{:S(2)}) async-start(s8[4718592]{0:T(1024)(128)(4,1)} %bitcast.694), calls=%async_computation.13 | async-start | bytes 1048576
  368.9 25.7 %slice-start.12 = ((s8[4718592]{0:T(1024)(128)(4,1)}), s8[4194304]{0:T(1024)(128)(4,1)S(1)}, s32[]{:S(2)}) async-start(s8[4718592]{0:T(1024)(128)(4,1)} %bitcast.696), calls=%async_computation.14 | async-start | bytes 8388608
  381.7 13.0 %slice-start.13 = ((s8[4718592]{0:T(1024)(128)(4,1)}), s8[524288]{0:T(1024)(128)(4,1)S(1)}, s32[]{:S(2)}) async-start(s8[4718592]{0:T(1024)(128)(4,1)} %bitcast.696), calls=%async_computation.15 | async-start | bytes 1048576
  381.7 25.8 %slice-start.14 = ((s8[4718592]{0:T(1024)(128)(4,1)}), s8[4194304]{0:T(1024)(128)(4,1)S(1)}, s32[]{:S(2)}) async-start(s8[4718592]{0:T(1024)(128)(4,1)} %bitcast.698), calls=%async_computation.16 | async-start | bytes 8388608
  394.7 12.8 %slice-start.15 = ((s8[4718592]{0:T(1024)(128)(4,1)}), s8[524288]{0:T(1024)(128)(4,1)S(1)}, s32[]{:S(2)}) async-start(s8[4718592]{0:T(1024)(128)(4,1)} %bitcast.698), calls=%async_computation.17 | async-start | bytes 1048576
  394.7 25.5 %slice-start.16 = ((s8[4718592]{0:T(1024)(128)(4,1)}), s8[4194304]{0:T(1024)(128)(4,1)S(1)}, s32[]{:S(2)}) async-start(s8[4718592]{0:T(1024)(128)(4,1)} %bitcast.700), calls=%async_computation.18 | async-start | bytes 8388608
  407.5 12.8 %slice-start.17 = ((s8[4718592]{0:T(1024)(128)(4,1)}), s8[524288]{0:T(1024)(128)(4,1)S(1)}, s32[]{:S(2)}) async-start(s8[4718592]{0:T(1024)(128)(4,1)} %bitcast.700), calls=%async_computation.19 | async-start | bytes 1048576
  407.5 26.0 %slice-start.18 = ((s8[4718592]{0:T(1024)(128)(4,1)}), s8[4194304]{0:T(1024)(128)(4,1)S(1)}, s32[]{:S(2)}) async-start(s8[4718592]{0:T(1024)(128)(4,1)} %bitcast.702), calls=%async_computation.20 | async-start | bytes 8388608
  420.2 13.2 %slice-start.19 = ((s8[4718592]{0:T(1024)(128)(4,1)}), s8[524288]{0:T(1024)(128)(4,1)S(1)}, s32[]{:S(2)}) async-start(s8[4718592]{0:T(1024)(128)(4,1)} %bitcast.702), calls=%async_computation.21 | async-start | bytes 1048576
  513.4 7.3 copy-start.3
  513.4 7.4 copy-start.5
  513.4 278.1 %all-to-all-start.1 = ((f32[32,24,4096]{2,1,0:T(8,128)}), f32[32,24,4096]{2,1,0:T(8,128)}, u32[]{:S(2)}, u32[]{:S(2)}) async-start(f32[32,24,4096]{2,1,0:T(8,128)} %convert_element_type.89), calls=%async_computation.1 | async-start | bytes 25165824 | tf_op jit(solution)/shard_map/all_to_all | solution.py:73
  837.9 12.1 %copy-start.1 = (bf16[64,4096]{1,0:T(8,128)(2,1)S(1)}, bf16[64,4096]{1,0:T(8,128)(2,1)}, u32[]{:S(2)}) copy-start(bf16[64,4096]{1,0:T(8,128)(2,1)} %param.11) | copy-start | bytes 1572868
where the time goes:
time: 861 us; the launch traced here: 850 us
  waiting for transfers between devices  407 us (47%)
  matrix products  288 us (33%)
  local copies, waits for them, and re-layouts  122 us (14%)
  other arithmetic  16.9 us (2%)
  starting transfers between devices  15.2 us (2%)
    all_to_all x1, waiting for transfers between devices, per_device(): lax.all_to_all(summed, ('dp', 'expert'), split_axis=0, concat_axis=0, til...  271 us
    dot_general x12, matrix products, per_device(): jnp.einsum('rkc,kb->rbc', pieces, placer, precision=lax.Precision.HIGHEST)  190 us
    all_to_all x1, waiting for transfers between devices, per_device(): lax.all_to_all(outgoing, ('dp', 'expert'), split_axis=0, concat_axis=0, t...  136 us
    dot_general x12, matrix products, per_device(): jnp.einsum('rf,kfc->rkc', hidden, down_blocks[0, block], preferred_elemen...  71.5 us
    gather x8, local copies, waits for them, and re-layouts, combine_rows(): chosen = jnp.take(flat_rows, target[:, pick], axis=0)  53.3 us
    gather x12, local copies, waits for them, and re-layouts, per_device(): picked = jnp.take(blocked, chosen, axis=1)  47 us
    dot_general x12, matrix products, per_device(): jnp.einsum('rkc,kcf->rf', picked, gate_blocks[0, block], preferred_elemen...  22.4 us
  transfers between devices with their start and end apart: 2, of which 2 were waited for; matrix products, arithmetic and copies ran while one was open for 0% of the time, Pallas kernels for 0%

commit v1 on v0

v1 whole, which is shorter than its diff:
```python
import functools

import jax
import jax.numpy as jnp
from jax import lax
from jax.experimental import pallas as pl
from jax.experimental.pallas import tpu as pltpu
from jax.sharding import PartitionSpec as P

TOP = 8
BLK = 128
BF16 = jnp.bfloat16
F32 = jnp.float32
VMEM_LIMIT = 48 * 1024 * 1024


def slot_numbers(expert_ids, experts):
    flat_ids = expert_ids.reshape(-1)
    onehot = (flat_ids[:, None] == jnp.arange(experts, dtype=jnp.int32)[None, :]).astype(jnp.int32)
    before = jnp.cumsum(onehot, axis=0) - onehot
    return jnp.sum(before * onehot, axis=1).reshape(expert_ids.shape)


def combine_rows(flat_rows, target, combine_weights):
    total = jnp.zeros((target.shape[0], flat_rows.shape[1]), jnp.float32)
    for pick in range(target.shape[1]):
        chosen = jnp.take(flat_rows, target[:, pick], axis=0)
        total = total + combine_weights[:, pick][:, None] * chosen
    return total


def general_device(tokens, expert_ids, combine_weights, topology, gate_blocks, up_blocks, down_blocks):
    experts = lax.axis_size(("dp", "expert"))
    width = tokens.shape[1] * lax.axis_size("tensor")
    tok_rows = tokens.shape[0]
    capacity = min(tok_rows, 3 * tok_rows * TOP // (2 * experts))
    slot_index = slot_numbers(expert_ids, experts)
    target = expert_ids * capacity + slot_index
    places = jnp.arange(experts * capacity, dtype=jnp.int32)
    matches = target[None, :, :] == places[:, None, None]
    dispatch = jnp.any(matches, axis=2).astype(BF16)
    outgoing = jnp.dot(dispatch, tokens, preferred_element_type=F32).astype(BF16)
    outgoing = outgoing.reshape(experts, capacity, tokens.shape[1])
    arrived = lax.all_to_all(outgoing, ("dp", "expert"), split_axis=0, concat_axis=0, tiled=True)
    expert_in = lax.all_gather(arrived, "tensor", axis=2, tiled=True)
    row_count = experts * capacity
    layout_ids = topology[0]
    blocked = expert_in.reshape(row_count, width // BLK, BLK)
    width_ids = jnp.arange(width // BLK, dtype=jnp.int32)
    partial_value = jnp.zeros((row_count, width // BLK, BLK), F32)
    for block in range(layout_ids.shape[0]):
        chosen = layout_ids[block]
        picked = jnp.take(blocked, chosen, axis=1)
        gate_proj = jnp.einsum("rkc,kcf->rf", picked, gate_blocks[0, block], preferred_element_type=F32)
        up_proj = jnp.einsum("rkc,kcf->rf", picked, up_blocks[0, block], preferred_element_type=F32)
        hidden = (jax.nn.silu(gate_proj) * up_proj).astype(BF16)
        pieces = jnp.einsum("rf,kfc->rkc", hidden, down_blocks[0, block], preferred_element_type=F32)
        placer = (chosen[:, None] == width_ids[None, :]).astype(F32)
        partial_value = partial_value + jnp.einsum(
            "rkc,kb->rbc", pieces, placer, precision=lax.Precision.HIGHEST
        )
    partial_low = lax.optimization_barrier(partial_value.reshape(experts, capacity, width).astype(BF16))
    shares = lax.all_to_all(
        partial_low.reshape(1, experts, capacity, width), "tensor", split_axis=3, concat_axis=0, tiled=True
    )
    summed = jnp.sum(shares.astype(F32), axis=0)
    returned_rows = lax.all_to_all(summed, ("dp", "expert"), split_axis=0, concat_axis=0, tiled=True)
    flat_rows = returned_rows.reshape(row_count, returned_rows.shape[2])
    return combine_rows(flat_rows, target, combine_weights).astype(BF16)


CORE, XBIT, YBIT = 1, 2, 4
PAIRS = [(0, 1), (1, 0), (2, 3), (3, 2)]
MIDDLES = [(1, 2), (2, 1)]
OUTWARD = [(1, 0), (2, 3)]
INWARD = [(0, 1), (3, 2)]


def flip(value, bit):
    return lax.ppermute(value, "dp", [(i, i ^ bit) for i in range(lax.axis_size("dp"))])


def along(value, pairs):
    return lax.ppermute(value, "expert", pairs)


def add(*values):
    return functools.reduce(lambda a, b: a + b, [v.astype(F32) for v in values]).astype(BF16)


def select_kernel(width, experts, cap, ids, a, b, c, d, own, send, hot):
    rows = a.shape[0]
    slots = 4 * cap
    lane = lax.broadcasted_iota(jnp.int32, (rows, BLK), 1)
    place = lax.broadcasted_iota(jnp.int32, (rows, 2 * slots), 1)
    parts = []
    for n, ref in enumerate((a, b, c, d)):
        meta = ref[:, width:].astype(F32)
        match = None
        for which in range(2):
            rank = jnp.sum(jnp.where(lane == 3 * experts + ids[which], meta, 0.0), axis=1, keepdims=True).astype(jnp.int32)
            goal = jnp.where(rank >= 0, rank + (which * slots + n * cap), -1)
            here = place == goal
            match = here if match is None else match | here
        parts.append(jnp.where(match, 1.0, 0.0))
    hot_t = jnp.concatenate(parts, axis=0).astype(BF16)
    hot[...] = hot_t
    step = 3 * BLK
    for at in range(0, own.shape[1], step):
        cols = slice(at, at + step)
        block = jnp.concatenate([a[:, cols], b[:, cols], c[:, cols], d[:, cols]], axis=0)
        picked = lax.dot_general(hot_t, block, (((0,), (0,)), ((), ())), preferred_element_type=F32).astype(BF16)
        own[:, cols] = picked[:slots]
        send[:, cols] = picked[slots:]


def select(ids, blocks, width, experts, cap):
    rows, full = blocks[0].shape
    return pl.pallas_call(
        functools.partial(select_kernel, width, experts, cap),
        out_shape=(
            jax.ShapeDtypeStruct((4 * cap, full), BF16),
            jax.ShapeDtypeStruct((4 * cap, full), BF16),
            jax.ShapeDtypeStruct((4 * rows, 8 * cap), BF16),
        ),
        in_specs=[pl.BlockSpec(memory_space=pltpu.SMEM)] + [pl.BlockSpec(memory_space=pltpu.VMEM)] * 4,
        out_specs=(pl.BlockSpec(memory_space=pltpu.VMEM),) * 3,
        compiler_params=pltpu.CompilerParams(vmem_limit_bytes=VMEM_LIMIT),
        name="select_rows",
    )(ids, *blocks)


def expert_kernel(count, width, experts, ids, topo, *refs):
    inputs, (gate, up, down) = refs[:count], refs[count : count + 3]
    outputs, (x, total) = refs[count + 3 : 2 * count + 3], refs[2 * count + 3 :]
    h = pl.program_id(0)
    rows = inputs[0].shape[0]

    @pl.when(h == 0)
    def _():
        for n, ref in enumerate(inputs):
            x[n * rows : (n + 1) * rows, :] = ref[:, :width]
        total[...] = jnp.zeros_like(total)

    kb = gate.shape[2]
    cols = [pl.ds(pl.multiple_of(topo[h, i] * BLK, BLK), BLK) for i in range(kb)]
    picked = jnp.concatenate([x[:, c] for c in cols], axis=1)
    weights = jnp.concatenate(
        [gate[0, 0].reshape(kb * BLK, BLK), up[0, 0].reshape(kb * BLK, BLK)], axis=1
    )
    both = jnp.dot(picked, weights, preferred_element_type=F32)
    gate_proj, up_proj = both[:, :BLK], both[:, BLK:]
    hidden = (gate_proj / (1.0 + jnp.exp(-gate_proj)) * up_proj).astype(BF16)
    for i in range(0, kb, 2):
        pair = jnp.concatenate([down[0, 0, i], down[0, 0, i + 1]], axis=1)
        pieces = jnp.dot(hidden, pair, preferred_element_type=F32)
        total[:, cols[i]] += pieces[:, :BLK]
        total[:, cols[i + 1]] += pieces[:, BLK:]

    @pl.when(h == pl.num_programs(0) - 1)
    def _():
        lane = lax.broadcasted_iota(jnp.int32, (rows, BLK), 1)
        mine = (lax.rem(lane, experts) == ids[0]) & (lane < 3 * experts)
        for n, (ref, out) in enumerate(zip(inputs, outputs)):
            meta = ref[:, width:].astype(F32)
            weight = jnp.sum(jnp.where(mine, meta, 0.0), axis=1, keepdims=True)
            out[...] = (total[n * rows : (n + 1) * rows, :] * weight).astype(BF16)


def expert(ids, topo, inputs, gate, up, down, width, experts):
    count, rows = len(inputs), inputs[0].shape[0]
    _, blocks, kb, _, _ = gate.shape
    spec = pl.BlockSpec((1, 1, kb, BLK, BLK), lambda h: (0, h, 0, 0, 0))
    return pl.pallas_call(
        functools.partial(expert_kernel, count, width, experts),
        grid=(blocks,),
        out_shape=[jax.ShapeDtypeStruct((rows, width), BF16)] * count,
        in_specs=[pl.BlockSpec(memory_space=pltpu.SMEM)] * 2
        + [pl.BlockSpec(v.shape, lambda h: (0, 0)) for v in inputs]
        + [spec] * 3,
        out_specs=[pl.BlockSpec((rows, width), lambda h: (0, 0))] * count,
        scratch_shapes=[pltpu.VMEM((count * rows, width), BF16), pltpu.VMEM((count * rows, width), F32)],
        compiler_params=pltpu.CompilerParams(vmem_limit_bytes=VMEM_LIMIT),
        name="expert_rows",
    )(ids, topo, *inputs, gate, up, down)


def spread_kernel(hot, own, back, a, b, c, d):
    rows = a.shape[0]
    step = 4 * BLK
    for at in range(0, own.shape[1], step):
        cols = slice(at, at + step)
        both = jnp.concatenate([own[:, cols], back[:, cols]], axis=0)
        sums = jnp.dot(hot[...], both, preferred_element_type=F32).astype(BF16)
        for n, ref in enumerate((a, b, c, d)):
            ref[:, cols] = sums[n * rows : (n + 1) * rows]


def spread(hot, own, back):
    rows, width = hot.shape[0] // 4, own.shape[1]
    return pl.pallas_call(
        spread_kernel,
        out_shape=[jax.ShapeDtypeStruct((rows, width), BF16)] * 4,
        in_specs=[pl.BlockSpec(memory_space=pltpu.VMEM)] * 3,
        out_specs=[pl.BlockSpec(memory_space=pltpu.VMEM)] * 4,
        compiler_params=pltpu.CompilerParams(vmem_limit_bytes=VMEM_LIMIT),
        name="spread_rows",
    )(hot, own, back)


def with_meta(tokens, expert_ids, combine_weights, experts):
    rows = tokens.shape[0]
    named = expert_ids[:, :, None] == jnp.arange(experts, dtype=jnp.int32)[None, None, :]
    weight = jnp.sum(jnp.where(named, combine_weights[:, :, None], 0.0), axis=1)
    chosen = jnp.any(named, axis=1)
    earlier = jnp.tril(jnp.ones((rows, rows), BF16), -1)
    rank = jnp.dot(earlier, chosen.astype(BF16), preferred_element_type=F32)
    rank = jnp.where(chosen, rank, -1.0)
    high = lax.reduce_precision(weight, 8, 7)
    middle = lax.reduce_precision(weight - high, 8, 7)
    low = weight - high - middle
    return jnp.concatenate([tokens] + [v.astype(BF16) for v in (high, middle, low, rank)], axis=1)


GROUPS = ((0, 1), (2, 3))


def line_device(tokens, expert_ids, combine_weights, topology, gate_blocks, up_blocks, down_blocks):
    experts = lax.axis_size(("dp", "expert"))
    rows, width = tokens.shape
    cap = min(rows, 3 * rows * TOP // (2 * experts))
    dp, z = lax.axis_index("dp"), lax.axis_index("expert")
    line = lax.axis_size("expert")
    ids = jnp.stack([dp * line + z, (dp ^ CORE) * line + z]).astype(jnp.int32)
    middle = (z == 1) | (z == 2)
    topo = topology[0]

    own = with_meta(tokens, expert_ids, combine_weights, experts)
    from_pair = along(own, PAIRS)
    from_middle = along(own, MIDDLES)
    second = jnp.where(middle, along(from_pair, MIDDLES), along(from_middle, OUTWARD))
    third = jnp.where(middle, from_middle, along(second, OUTWARD))
    layers = [own, from_pair, second, third]

    returned = {}
    for group in GROUPS:
        hots, mine, theirs = [], [], []
        for k in group:
            here = layers[k]
            by_x, by_y = flip(here, XBIT), flip(here, YBIT)
            across = flip(by_y, XBIT) if k % 2 == 0 else flip(by_x, YBIT)
            kept, sent, hot = select(ids, [here, by_x, by_y, across], width, experts, cap)
            hots.append(hot)
            mine.append(kept)
            theirs.append(flip(sent, CORE))
        results = expert(ids, topo, mine + theirs, gate_blocks, up_blocks, down_blocks, width, experts)
        count = len(group)
        for n, k in reversed(list(enumerate(group))):
            back = flip(results[count + n], CORE)
            here, to_x, to_y, across = spread(hots[n], results[n], back)
            if k % 2 == 0:
                to_y = add(to_y, flip(across, XBIT))
            else:
                to_x = add(to_x, flip(across, YBIT))
            returned[k] = (here, flip(to_x, XBIT), flip(to_y, YBIT))

    third = add(*returned[3])
    second = add(*returned[2])
    end_third, end_second = along(third, INWARD), along(second, INWARD)
    second = add(second, end_third)
    third = add(third, end_second)
    first = add(*returned[1], along(second, MIDDLES))
    last = along(third, MIDDLES)
    return add(*returned[0], last, along(first, PAIRS))


def solution(mesh):
    line = mesh.shape["dp"] == 8 and mesh.shape["expert"] == 4 and mesh.shape["tensor"] == 1
    return jax.shard_map(
        line_device if line else general_device,
        mesh=mesh,
        in_specs=(
            P(("dp", "expert"), "tensor"),
            P(("dp", "expert"), None),
            P(("dp", "expert"), None),
            P(("dp", "expert"), "tensor", None),
            P(("dp", "expert"), "tensor", None, None, None),
            P(("dp", "expert"), "tensor", None, None, None),
            P(("dp", "expert"), "tensor", None, None, None),
        ),
        out_specs=P(("dp", "expert"), "tensor"),
        check_vma=False,
    )
```

time: 861 us -> 254 us (0.30); the launches traced: 850 us -> 254 us
  matrix products: 288 us -> 0.19 us
  waiting for transfers between devices: 407 us -> 143 us
  local copies, waits for them, and re-layouts: 122 us -> 3.21 us
  Pallas kernels: 0 us -> 54.2 us
  starting transfers between devices: 15.2 us -> 48.7 us
  other arithmetic: 16.9 us -> 4.15 us
    all_to_all x2 -> x0, waiting for transfers between devices: 407 us -> none  [the longest x1 271 us: per_device(): lax.all_to_all(summed, ('dp', 'expert'), split_axis=0, concat_axis=0, til...]
    dot_general x37 -> x1, matrix products: 288 us -> 0.19 us  [with_meta(): rank = jnp.dot(earlier, chosen.astype(BF16), preferred_element_type=F32)]
    ppermute x0 -> x42, waiting for transfers between devices: none -> 143 us  [the longest x32 93.6 us: flip(): lax.ppermute(value, 'dp', [(i, i ^ bit) for i in range(lax.axis_size('dp'...]
    gather x20 -> x0, local copies, waits for them, and re-layouts: 100 us -> none  [the longest x8 53.3 us: combine_rows(): chosen = jnp.take(flat_rows, target[:, pick], axis=0)]
    pallas_call x0 -> x10, Pallas kernels: none -> 54.2 us  [the longest x2 44.2 us: expert(): pl.pallas_call(functools.partial(expert_kernel, count, width, experts), g...]
    ppermute x0 -> x42, starting transfers between devices: none -> 48.7 us  [the longest x32 29.4 us: flip(): lax.ppermute(value, 'dp', [(i, i ^ bit) for i in range(lax.axis_size('dp'...]
    all_to_all x2 -> x0, starting transfers between devices: 15.2 us -> none  [the longest x1 7.94 us: per_device(): lax.all_to_all(outgoing, ('dp', 'expert'), split_axis=0, concat_axis=0, t...]
    convert_element_type x3 -> x10, other arithmetic: 14.2 us -> 2.49 us  [the longest x9 2.48 us: add(): functools.reduce(lambda a, b: a + b, [v.astype(F32) for v in values])]
  transfers between devices with their start and end apart: 2 -> 42, of which waited for: 2 -> 14; matrix products, arithmetic and copies ran while one was open for 0% -> 1% of each run, Pallas kernels for 0% -> 21%
where the time goes in v1:
time: 254 us
  waiting for transfers between devices  143 us (56%)
  Pallas kernels  54.2 us (21%)
  starting transfers between devices  48.7 us (19%)
  other arithmetic  4.15 us (2%)
  local copies, waits for them, and re-layouts  3.21 us (1%)
    ppermute x32, waiting for transfers between devices, flip(): lax.ppermute(value, 'dp', [(i, i ^ bit) for i in range(lax.axis_size('dp'...  93.6 us
    ppermute x10, waiting for transfers between devices, along(): return lax.ppermute(value, 'expert', pairs)  49.3 us
    pallas_call x2, Pallas kernels, expert(): pl.pallas_call(functools.partial(expert_kernel, count, width, experts), g...  44.2 us
    ppermute x32, starting transfers between devices, flip(): lax.ppermute(value, 'dp', [(i, i ^ bit) for i in range(lax.axis_size('dp'...  29.4 us
    ppermute x10, starting transfers between devices, along(): return lax.ppermute(value, 'expert', pairs)  19.3 us
    pallas_call x4, Pallas kernels, select(): pl.pallas_call(functools.partial(select_kernel, width, experts, cap), out...  7.19 us
  transfers between devices with their start and end apart: 42, of which 14 were waited for; matrix products, arithmetic and copies ran while one was open for 1% of the time, Pallas kernels for 21%

profile of v1, /device:TPU:0, one launch (start us, length us, event | category | flops | bytes accessed | tf_op | source)
XLA Modules:
  0.0 253.7 jit_solution(6141475199865026680)
XLA Ops:
  0.0 0.7 select_reduce_fusion
  0.8 0.7 fusion.1
  1.9 1.1 concatenate.3.a
  3.1 3.1 %collective-permute-start.3 = (bf16[64,4224]{1,0:T(8,128)(2,1)S(1)}, bf16[64,4224]{1,0:T(8,128)(2,1)S(1)}, u32[]{:S(2)}, u32[]{:S(2)}) collective-permute-start(bf16[64,4224]{1,0:T(8,128)(2,1)S(1)} %concatenate.3.a), channel_id=1, source_target_pairs={{0,1},{1,0},{2,3},{3,2},{4,5},{5,4},{6,7},{7,6},{8,9},{9,8},{10,11... | collective-permute-start | bytes 1622024 | tf_op jit(solution)/shard_map/ppermute | solution.py:84
  6.2 0.7 collective-permute-start.13
  6.9 11.6 %collective-permute-done.3.a = bf16[64,4224]{1,0:T(8,128)(2,1)S(1)} collective-permute-done((bf16[64,4224]{1,0:T(8,128)(2,1)S(1)}, bf16[64,4224]{1,0:T(8,128)(2,1)S(1)}, u32[]{:S(2)}, u32[]{:S(2)}) %collective-permute-start.3) | collective-permute-done | bytes 540704 | tf_op jit(solution)/shard_map/ppermute | solution.py:84
  18.5 0.7 collective-permute-start.14
  19.2 1.3 collective-permute-start.15
  20.5 15.6 %collective-permute-done.15 = bf16[64,4224]{1,0:T(8,128)(2,1)S(1)} collective-permute-done((bf16[64,4224]{1,0:T(8,128)(2,1)S(1)}, bf16[64,4224]{1,0:T(8,128)(2,1)S(1)}, u32[]{:S(2)}, u32[]{:S(2)}) %collective-permute-start.15) | collective-permute-done | bytes 540704 | tf_op jit(solution)/shard_map/ppermute | solution.py:84
  36.2 1.3 collective-permute-start.16
  37.5 1.6 collective-permute-start.21
  39.0 11.2 %collective-permute-done.16 = bf16[64,4224]{1,0:T(8,128)(2,1)S(1)} collective-permute-done((bf16[64,4224]{1,0:T(8,128)(2,1)S(1)}, bf16[64,4224]{1,0:T(8,128)(2,1)S(1)}, u32[]{:S(2)}, u32[]{:S(2)}) %collective-permute-start.16) | collective-permute-done | bytes 540704 | tf_op jit(solution)/shard_map/ppermute | solution.py:84
  50.3 1.6 collective-permute-start.17
  51.9 0.5 collective-permute-start.20
  52.4 1.5 collective-permute-start.22
  53.9 1.5 collective-permute-start.18
  55.5 10.2 %collective-permute-done.17.b = bf16[64,4224]{1,0:T(8,128)(2,1)S(1)} collective-permute-done((bf16[64,4224]{1,0:T(8,128)(2,1)S(1)}, bf16[64,4224]{1,0:T(8,128)(2,1)S(1)}, u32[]{:S(2)}, u32[]{:S(2)}) %collective-permute-start.17) | collective-permute-done | bytes 540704 | tf_op jit(solution)/shard_map/ppermute | solution.py:80
  65.6 1.5 collective-permute-start.19
  67.2 10.1 %collective-permute-done.20.b = bf16[64,4224]{1,0:T(8,128)(2,1)} collective-permute-done((bf16[64,4224]{1,0:T(8,128)(2,1)S(1)}, bf16[64,4224]{1,0:T(8,128)(2,1)}, u32[]{:S(2)}, u32[]{:S(2)}) %collective-permute-start.20) | collective-permute-done | bytes 540704 | tf_op jit(solution)/shard_map/ppermute | solution.py:80
  77.3 7.7 %collective-permute-done.22.d = bf16[64,4224]{1,0:T(8,128)(2,1)} collective-permute-done((bf16[64,4224]{1,0:T(8,128)(2,1)S(1)}, bf16[64,4224]{1,0:T(8,128)(2,1)}, u32[]{:S(2)}, u32[]{:S(2)}) %collective-permute-start.22) | collective-permute-done | bytes 540704 | tf_op jit(solution)/shard_map/ppermute | solution.py:80
  85.0 2.1 select_rows.7
  87.2 2.1 select_rows.6
  89.4 0.5 collective-permute-start.24
  89.9 1.5 collective-permute-start.1
  91.4 1.5 collective-permute-start.4
  92.9 0.5 collective-permute-start
  93.5 10.7 %collective-permute-done.1.c = bf16[64,4224]{1,0:T(8,128)(2,1)S(1)} collective-permute-done((bf16[64,4224]{1,0:T(8,128)(2,1)S(1)}, bf16[64,4224]{1,0:T(8,128)(2,1)S(1)}, u32[]{:S(2)}, u32[]{:S(2)}) %collective-permute-start.1) | collective-permute-done | bytes 540704 | tf_op jit(solution)/shard_map/ppermute | solution.py:80
  104.2 1.5 collective-permute-start.2
  105.7 0.9 collective-permute-done.4.b
  106.6 0.6 collective-permute-start.5
  107.2 1.4 collective-permute-start.6
  108.7 0.9 copy-done
  109.6 22.1 %expert_rows.3 = (bf16[96,4096]{1,0:T(8,128)(2,1)S(1)}, bf16[96,4096]{1,0:T(8,128)(2,1)S(1)}, bf16[96,4096]{1,0:T(8,128)(2,1)S(1)}, bf16[96,4096]{1,0:T(8,128)(2,1)S(1)}) custom-call(s32[2]{0:T(128)S(1)} %pad_add_fusion.ids, s32[12,12]{1,0:T(8,128)S(1)} %bitcast.6, bf16[96,4224]{1,0:T(8,128)(2,1)S(1)} %get-tuple-element.53.refs_0_, ...), custom_call_target="tpu_custom_call" | custom-call | tf_op jit(solution)/shard_map/expert_rows/pallas_call | solution.py:174
  131.7 1.4 select_rows.4
  133.2 0.6 collective-permute-start.7
  133.8 1.5 select_rows.5
  135.8 0.7 spread_rows.6
  136.5 1.6 collective-permute-start.31
  138.1 0.9 copy-done.1
  139.0 22.1 %expert_rows.2 = (bf16[96,4096]{1,0:T(8,128)(2,1)S(1)}, bf16[96,4096]{1,0:T(8,128)(2,1)S(1)}, bf16[96,4096]{1,0:T(8,128)(2,1)S(1)}, bf16[96,4096]{1,0:T(8,128)(2,1)S(1)}) custom-call(s32[2]{0:T(128)S(1)} %pad_add_fusion.ids, s32[12,12]{1,0:T(8,128)S(1)} %bitcast.7, bf16[96,4224]{1,0:T(8,128)(2,1)S(1)} %get-tuple-element.42.refs_0_, ...), custom_call_target="tpu_custom_call" | custom-call | tf_op jit(solution)/shard_map/expert_rows/pallas_call | solution.py:174
  161.7 1.0 collective-permute-start.30
  162.7 0.7 spread_rows.5
  164.0 1.6 collective-permute-start.26
  165.6 22.8 %collective-permute-done.26 = bf16[64,4096]{1,0:T(8,128)(2,1)S(1)} collective-permute-done((bf16[64,4096]{1,0:T(8,128)(2,1)S(1)}, bf16[64,4096]{1,0:T(8,128)(2,1)S(1)}, u32[]{:S(2)}, u32[]{:S(2)}) %collective-permute-start.26) | collective-permute-done | bytes 524320 | tf_op jit(solution)/shard_map/ppermute | solution.py:80
  189.0 1.0 collective-permute-start.27
  190.0 11.2 %collective-permute-done.32 = bf16[64,4096]{1,0:T(8,128)(2,1)S(1)} collective-permute-done((bf16[64,4096]{1,0:T(8,128)(2,1)S(1)}, bf16[64,4096]{1,0:T(8,128)(2,1)S(1)}, u32[]{:S(2)}, u32[]{:S(2)}) %collective-permute-start.32) | collective-permute-done | bytes 524320 | tf_op jit(solution)/shard_map/ppermute | solution.py:80
  201.4 1.6 collective-permute-start.33
  203.1 0.7 spread_rows.7
  203.8 0.6 collective-permute-start.38
  204.4 1.5 collective-permute-start.36
  205.9 0.7 spread_rows.4
  206.6 0.9 collective-permute-start.11
  207.6 1.1 collective-permute-start.10
  208.7 3.7 %collective-permute-done.33 = bf16[64,4096]{1,0:T(8,128)(2,1)S(1)} collective-permute-done((bf16[64,4096]{1,0:T(8,128)(2,1)S(1)}, bf16[64,4096]{1,0:T(8,128)(2,1)S(1)}, u32[]{:S(2)}, u32[]{:S(2)}) %collective-permute-start.33) | collective-permute-done | bytes 524320 | tf_op jit(solution)/shard_map/ppermute | solution.py:84
  212.7 4.4 %collective-permute-start.39 = (bf16[64,4096]{1,0:T(8,128)(2,1)S(1)}, bf16[64,4096]{1,0:T(8,128)(2,1)S(1)}, u32[]{:S(2)}, u32[]{:S(2)}) collective-permute-start(bf16[64,4096]{1,0:T(8,128)(2,1)S(1)} %get-tuple-element.78), channel_id=1, source_target_pairs={{0,1},{3,2},{4,5},{7,6},{8,9},{11,10},{12,13},{15,14},{16,17},{19,... | collective-permute-start | bytes 1572872 | tf_op jit(solution)/shard_map/ppermute | solution.py:84
  217.1 9.7 %collective-permute-done.36 = bf16[64,4096]{1,0:T(8,128)(2,1)S(1)} collective-permute-done((bf16[64,4096]{1,0:T(8,128)(2,1)S(1)}, bf16[64,4096]{1,0:T(8,128)(2,1)S(1)}, u32[]{:S(2)}, u32[]{:S(2)}) %collective-permute-start.36) | collective-permute-done | bytes 524320 | tf_op jit(solution)/shard_map/ppermute | solution.py:80
  227.0 0.8 collective-permute-start.37
  227.9 0.7 collective-permute-start.40
  228.8 0.6 collective-permute-start.12
  229.4 0.7 collective-permute-start.34
  230.1 10.3 %collective-permute-done.37 = bf16[64,4096]{1,0:T(8,128)(2,1)S(1)} collective-permute-done((bf16[64,4096]{1,0:T(8,128)(2,1)S(1)}, bf16[64,4096]{1,0:T(8,128)(2,1)S(1)}, u32[]{:S(2)}, u32[]{:S(2)}) %collective-permute-start.37) | collective-permute-done | bytes 524320 | tf_op jit(solution)/shard_map/ppermute | solution.py:80
  240.6 4.8 %collective-permute-start.41 = (bf16[64,4096]{1,0:T(8,128)(2,1)S(1)}, bf16[64,4096]{1,0:T(8,128)(2,1)S(1)}, u32[]{:S(2)}, u32[]{:S(2)}) collective-permute-start(bf16[64,4096]{1,0:T(8,128)(2,1)S(1)} %add_convert_fusion.1), channel_id=1, source_target_pairs={{0,1},{1,0},{2,3},{3,2},{4,5},{5,4},{6,7},{7,6},{8,9},{9,8},{10,11... | collective-permute-start | bytes 1572872 | tf_op jit(solution)/shard_map/ppermute | solution.py:84
  245.4 7.1 %collective-permute-done.41 = bf16[64,4096]{1,0:T(8,128)(2,1)S(1)} collective-permute-done((bf16[64,4096]{1,0:T(8,128)(2,1)S(1)}, bf16[64,4096]{1,0:T(8,128)(2,1)S(1)}, u32[]{:S(2)}, u32[]{:S(2)}) %collective-permute-start.41) | collective-permute-done | bytes 524320 | tf_op jit(solution)/shard_map/ppermute | solution.py:84
  252.6 1.1 add_convert_fusion
  (59 shorter events, 4.4 us)
Async XLA Ops:
  0.0 108.6 %copy-start.2 = (s32[1,12,12]{2,0,1:T(1,128)S(1)}, s32[1,12,12]{2,0,1:T(1,128)}, u32[]{:S(2)}) copy-start(s32[1,12,12]{2,0,1:T(1,128)} %param.10) | copy-start | bytes 1732
  3.1 15.4 %collective-permute-start.3 = (bf16[64,4224]{1,0:T(8,128)(2,1)S(1)}, bf16[64,4224]{1,0:T(8,128)(2,1)S(1)}, u32[]{:S(2)}, u32[]{:S(2)}) collective-permute-start(bf16[64,4224]{1,0:T(8,128)(2,1)S(1)} %concatenate.3.a), channel_id=1, source_target_pairs={{0,1},{1,0},{2,3},{3,2},{4,5},{5,4},{6,7},{7,6},{8,9},{9,8},{10,11... | collective-permute-start | bytes 1622024 | tf_op jit(solution)/shard_map/ppermute | solution.py:84
  6.2 13.0 %collective-permute-start.13 = (bf16[64,4224]{1,0:T(8,128)(2,1)S(1)}, bf16[64,4224]{1,0:T(8,128)(2,1)S(1)}, u32[]{:S(2)}, u32[]{:S(2)}) collective-permute-start(bf16[64,4224]{1,0:T(8,128)(2,1)S(1)} %concatenate.3.a), channel_id=1, source_target_pairs={{1,2},{2,1},{5,6},{6,5},{9,10},{10,9},{13,14},{14,13},{17,18},{18,... | collective-permute-start | bytes 1622024 | tf_op jit(solution)/shard_map/ppermute | solution.py:84
  18.5 2.0 collective-permute-start.14
  19.2 16.9 %collective-permute-start.15 = (bf16[64,4224]{1,0:T(8,128)(2,1)S(1)}, bf16[64,4224]{1,0:T(8,128)(2,1)S(1)}, u32[]{:S(2)}, u32[]{:S(2)}) collective-permute-start(bf16[64,4224]{1,0:T(8,128)(2,1)S(1)} %collective-permute-done.13), channel_id=1, source_target_pairs={{1,0},{2,3},{5,4},{6,7},{9,8},{10,11},{13,12},{14,15},{17,16},{18,... | collective-permute-start | bytes 1622024 | tf_op jit(solution)/shard_map/ppermute | solution.py:84
  36.2 14.1 %collective-permute-start.16 = (bf16[64,4224]{1,0:T(8,128)(2,1)S(1)}, bf16[64,4224]{1,0:T(8,128)(2,1)S(1)}, u32[]{:S(2)}, u32[]{:S(2)}) collective-permute-start(bf16[64,4224]{1,0:T(8,128)(2,1)S(1)} %broadcast_select_fusion.1.a), channel_id=1, source_target_pairs={{1,0},{2,3},{5,4},{6,7},{9,8},{10,11},{13,12},{14,15},{17,16},{18,... | collective-permute-start | bytes 1622024 | tf_op jit(solution)/shard_map/ppermute | solution.py:84
  37.5 15.0 %collective-permute-start.21 = (bf16[64,4224]{1,0:T(8,128)(2,1)S(1)}, bf16[64,4224]{1,0:T(8,128)(2,1)S(1)}, u32[]{:S(2)}, u32[]{:S(2)}) collective-permute-start(bf16[64,4224]{1,0:T(8,128)(2,1)S(1)} %broadcast_select_fusion.1.a), channel_id=1, source_target_pairs={{0,16},{4,20},{8,24},{12,28},{16,0},{20,4},{24,8},{28,12},{1,17},{... | collective-permute-start | bytes 1622024 | tf_op jit(solution)/shard_map/ppermute | solution.py:80
  50.3 15.3 %collective-permute-start.17 = (bf16[64,4224]{1,0:T(8,128)(2,1)S(1)}, bf16[64,4224]{1,0:T(8,128)(2,1)S(1)}, u32[]{:S(2)}, u32[]{:S(2)}) collective-permute-start(bf16[64,4224]{1,0:T(8,128)(2,1)S(1)} %broadcast_select_fusion.a), channel_id=1, source_target_pairs={{0,8},{4,12},{8,0},{12,4},{16,24},{20,28},{24,16},{28,20},{1,9},{5... | collective-permute-start | bytes 1622024 | tf_op jit(solution)/shard_map/ppermute | solution.py:80
  51.9 25.4 %collective-permute-start.20 = (bf16[64,4224]{1,0:T(8,128)(2,1)S(1)}, bf16[64,4224]{1,0:T(8,128)(2,1)}, u32[]{:S(2)}, u32[]{:S(2)}) collective-permute-start(bf16[64,4224]{1,0:T(8,128)(2,1)S(1)} %broadcast_select_fusion.1.a), channel_id=1, source_target_pairs={{0,8},{4,12},{8,0},{12,4},{16,24},{20,28},{24,16},{28,20},{1,9},{5... | collective-permute-start | bytes 1622024 | tf_op jit(solution)/shard_map/ppermute | solution.py:80
  52.4 32.5 %collective-permute-start.22 = (bf16[64,4224]{1,0:T(8,128)(2,1)S(1)}, bf16[64,4224]{1,0:T(8,128)(2,1)}, u32[]{:S(2)}, u32[]{:S(2)}) collective-permute-start(bf16[64,4224]{1,0:T(8,128)(2,1)S(1)} %collective-permute-done.21.c), channel_id=1, source_target_pairs={{0,8},{4,12},{8,0},{12,4},{16,24},{20,28},{24,16},{28,20},{1,9},{5... | collective-permute-start | bytes 1622024 | tf_op jit(solution)/shard_map/ppermute | solution.py:80
  53.9 33.3 %collective-permute-start.18 = (bf16[64,4224]{1,0:T(8,128)(2,1)S(1)}, bf16[64,4224]{1,0:T(8,128)(2,1)}, u32[]{:S(2)}, u32[]{:S(2)}) collective-permute-start(bf16[64,4224]{1,0:T(8,128)(2,1)S(1)} %broadcast_select_fusion.a), channel_id=1, source_target_pairs={{0,16},{4,20},{8,24},{12,28},{16,0},{20,4},{24,8},{28,12},{1,17},{... | collective-permute-start | bytes 1622024 | tf_op jit(solution)/shard_map/ppermute | solution.py:80
  65.6 21.6 %collective-permute-start.19 = (bf16[64,4224]{1,0:T(8,128)(2,1)S(1)}, bf16[64,4224]{1,0:T(8,128)(2,1)}, u32[]{:S(2)}, u32[]{:S(2)}) collective-permute-start(bf16[64,4224]{1,0:T(8,128)(2,1)S(1)} %collective-permute-done.17.b), channel_id=1, source_target_pairs={{0,16},{4,20},{8,24},{12,28},{16,0},{20,4},{24,8},{28,12},{1,17},{... | collective-permute-start | bytes 1622024 | tf_op jit(solution)/shard_map/ppermute | solution.py:80
  87.1 20.1 %collective-permute-start.23 = (bf16[96,4224]{1,0:T(8,128)(2,1)S(1)}, bf16[96,4224]{1,0:T(8,128)(2,1)S(1)}, u32[]{:S(2)}, u32[]{:S(2)}) collective-permute-start(bf16[96,4224]{1,0:T(8,128)(2,1)S(1)} %get-tuple-element.55), channel_id=1, source_target_pairs={{0,4},{4,0},{8,12},{12,8},{16,20},{20,16},{24,28},{28,24},{1,5},{5... | collective-permute-start | bytes 2433032 | tf_op jit(solution)/shard_map/ppermute | solution.py:80
  89.4 19.3 %collective-permute-start.24 = (bf16[96,4224]{1,0:T(8,128)(2,1)S(1)}, bf16[96,4224]{1,0:T(8,128)(2,1)S(1)}, u32[]{:S(2)}, u32[]{:S(2)}) collective-permute-start(bf16[96,4224]{1,0:T(8,128)(2,1)S(1)} %get-tuple-element.56), channel_id=1, source_target_pairs={{0,4},{4,0},{8,12},{12,8},{16,20},{20,16},{24,28},{28,24},{1,5},{5... | collective-permute-start | bytes 2433032 | tf_op jit(solution)/shard_map/ppermute | solution.py:80
  89.9 14.3 %collective-permute-start.1 = (bf16[64,4224]{1,0:T(8,128)(2,1)S(1)}, bf16[64,4224]{1,0:T(8,128)(2,1)S(1)}, u32[]{:S(2)}, u32[]{:S(2)}) collective-permute-start(bf16[64,4224]{1,0:T(8,128)(2,1)S(1)} %concatenate.3.a), channel_id=1, source_target_pairs={{0,16},{4,20},{8,24},{12,28},{16,0},{20,4},{24,8},{28,12},{1,17},{... | collective-permute-start | bytes 1622024 | tf_op jit(solution)/shard_map/ppermute | solution.py:80
  91.4 15.2 %collective-permute-start.4 = (bf16[64,4224]{1,0:T(8,128)(2,1)S(1)}, bf16[64,4224]{1,0:T(8,128)(2,1)S(1)}, u32[]{:S(2)}, u32[]{:S(2)}) collective-permute-start(bf16[64,4224]{1,0:T(8,128)(2,1)S(1)} %collective-permute-done.3.a), channel_id=1, source_target_pairs={{0,8},{4,12},{8,0},{12,4},{16,24},{20,28},{24,16},{28,20},{1,9},{5... | collective-permute-start | bytes 1622024 | tf_op jit(solution)/shard_map/ppermute | solution.py:80
  92.9 38.8 %collective-permute-start = (bf16[64,4224]{1,0:T(8,128)(2,1)S(1)}, bf16[64,4224]{1,0:T(8,128)(2,1)S(1)}, u32[]{:S(2)}, u32[]{:S(2)}) collective-permute-start(bf16[64,4224]{1,0:T(8,128)(2,1)S(1)} %concatenate.3.a), channel_id=1, source_target_pairs={{0,8},{4,12},{8,0},{12,4},{16,24},{20,28},{24,16},{28,20},{1,9},{5... | collective-permute-start | bytes 1622024 | tf_op jit(solution)/shard_map/ppermute | solution.py:80
  104.2 27.6 %collective-permute-start.2 = (bf16[64,4224]{1,0:T(8,128)(2,1)S(1)}, bf16[64,4224]{1,0:T(8,128)(2,1)S(1)}, u32[]{:S(2)}, u32[]{:S(2)}) collective-permute-start(bf16[64,4224]{1,0:T(8,128)(2,1)S(1)} %collective-permute-done.1.c), channel_id=1, source_target_pairs={{0,8},{4,12},{8,0},{12,4},{16,24},{20,28},{24,16},{28,20},{1,9},{5... | collective-permute-start | bytes 1622024 | tf_op jit(solution)/shard_map/ppermute | solution.py:80
  106.6 27.1 %collective-permute-start.5 = (bf16[64,4224]{1,0:T(8,128)(2,1)S(1)}, bf16[64,4224]{1,0:T(8,128)(2,1)S(1)}, u32[]{:S(2)}, u32[]{:S(2)}) collective-permute-start(bf16[64,4224]{1,0:T(8,128)(2,1)S(1)} %collective-permute-done.3.a), channel_id=1, source_target_pairs={{0,16},{4,20},{8,24},{12,28},{16,0},{20,4},{24,8},{28,12},{1,17},{... | collective-permute-start | bytes 1622024 | tf_op jit(solution)/shard_map/ppermute | solution.py:80
  107.2 26.6 %collective-permute-start.6 = (bf16[64,4224]{1,0:T(8,128)(2,1)S(1)}, bf16[64,4224]{1,0:T(8,128)(2,1)S(1)}, u32[]{:S(2)}, u32[]{:S(2)}) collective-permute-start(bf16[64,4224]{1,0:T(8,128)(2,1)S(1)} %collective-permute-done.4.b), channel_id=1, source_target_pairs={{0,16},{4,20},{8,24},{12,28},{16,0},{20,4},{24,8},{28,12},{1,17},{... | collective-permute-start | bytes 1622024 | tf_op jit(solution)/shard_map/ppermute | solution.py:80
  108.6 0.9 copy-start
  131.6 4.2 %collective-permute-start.29 = (bf16[96,4096]{1,0:T(8,128)(2,1)S(1)}, bf16[96,4096]{1,0:T(8,128)(2,1)S(1)}, u32[]{:S(2)}, u32[]{:S(2)}) collective-permute-start(bf16[96,4096]{1,0:T(8,128)(2,1)S(1)} %get-tuple-element.65), channel_id=1, source_target_pairs={{0,4},{4,0},{8,12},{12,8},{16,20},{20,16},{24,28},{28,24},{1,5},{5... | collective-permute-start | bytes 2359304 | tf_op jit(solution)/shard_map/ppermute | solution.py:80
  133.2 4.9 %collective-permute-start.7 = (bf16[96,4224]{1,0:T(8,128)(2,1)S(1)}, bf16[96,4224]{1,0:T(8,128)(2,1)S(1)}, u32[]{:S(2)}, u32[]{:S(2)}) collective-permute-start(bf16[96,4224]{1,0:T(8,128)(2,1)S(1)} %get-tuple-element.44), channel_id=1, source_target_pairs={{0,4},{4,0},{8,12},{12,8},{16,20},{20,16},{24,28},{28,24},{1,5},{5... | collective-permute-start | bytes 2433032 | tf_op jit(solution)/shard_map/ppermute | solution.py:80
  135.2 2.9 %collective-permute-start.8 = (bf16[96,4224]{1,0:T(8,128)(2,1)S(1)}, bf16[96,4224]{1,0:T(8,128)(2,1)S(1)}, u32[]{:S(2)}, u32[]{:S(2)}) collective-permute-start(bf16[96,4224]{1,0:T(8,128)(2,1)S(1)} %get-tuple-element.45), channel_id=1, source_target_pairs={{0,4},{4,0},{8,12},{12,8},{16,20},{20,16},{24,28},{28,24},{1,5},{5... | collective-permute-start | bytes 2433032 | tf_op jit(solution)/shard_map/ppermute | solution.py:80
  135.3 27.4 %collective-permute-start.25 = (bf16[96,4096]{1,0:T(8,128)(2,1)S(1)}, bf16[96,4096]{1,0:T(8,128)(2,1)S(1)}, u32[]{:S(2)}, u32[]{:S(2)}) collective-permute-start(bf16[96,4096]{1,0:T(8,128)(2,1)S(1)} %get-tuple-element.58), channel_id=1, source_target_pairs={{0,4},{4,0},{8,12},{12,8},{16,20},{20,16},{24,28},{28,24},{1,5},{5... | collective-permute-start | bytes 2359304 | tf_op jit(solution)/shard_map/ppermute | solution.py:80
  136.5 27.4 %collective-permute-start.31 = (bf16[64,4096]{1,0:T(8,128)(2,1)S(1)}, bf16[64,4096]{1,0:T(8,128)(2,1)S(1)}, u32[]{:S(2)}, u32[]{:S(2)}) collective-permute-start(bf16[64,4096]{1,0:T(8,128)(2,1)S(1)} %get-tuple-element.69), channel_id=1, source_target_pairs={{0,8},{4,12},{8,0},{12,4},{16,24},{20,28},{24,16},{28,20},{1,9},{5... | collective-permute-start | bytes 1572872 | tf_op jit(solution)/shard_map/ppermute | solution.py:80
  138.1 0.9 copy-start.1
  161.1 42.0 %collective-permute-start.35 = (bf16[96,4096]{1,0:T(8,128)(2,1)S(1)}, bf16[96,4096]{1,0:T(8,128)(2,1)S(1)}, u32[]{:S(2)}, u32[]{:S(2)}) collective-permute-start(bf16[96,4096]{1,0:T(8,128)(2,1)S(1)} %get-tuple-element.72), channel_id=1, source_target_pairs={{0,4},{4,0},{8,12},{12,8},{16,20},{20,16},{24,28},{28,24},{1,5},{5... | collective-permute-start | bytes 2359304 | tf_op jit(solution)/shard_map/ppermute | solution.py:80
  161.2 43.2 %collective-permute-start.9 = (bf16[96,4096]{1,0:T(8,128)(2,1)S(1)}, bf16[96,4096]{1,0:T(8,128)(2,1)S(1)}, u32[]{:S(2)}, u32[]{:S(2)}) collective-permute-start(bf16[96,4096]{1,0:T(8,128)(2,1)S(1)} %get-tuple-element.47), channel_id=1, source_target_pairs={{0,4},{4,0},{8,12},{12,8},{16,20},{20,16},{24,28},{28,24},{1,5},{5... | collective-permute-start | bytes 2359304 | tf_op jit(solution)/shard_map/ppermute | solution.py:80
  161.7 27.4 %collective-permute-start.30 = (bf16[64,4096]{1,0:T(8,128)(2,1)S(1)}, bf16[64,4096]{1,0:T(8,128)(2,1)S(1)}, u32[]{:S(2)}, u32[]{:S(2)}) collective-permute-start(bf16[64,4096]{1,0:T(8,128)(2,1)S(1)} %get-tuple-element.67), channel_id=1, source_target_pairs={{0,8},{4,12},{8,0},{12,4},{16,24},{20,28},{24,16},{28,20},{1,9},{5... | collective-permute-start | bytes 1572872 | tf_op jit(solution)/shard_map/ppermute | solution.py:80
  163.4 43.2 %collective-permute-start.28 = (bf16[64,4096]{1,0:T(8,128)(2,1)S(1)}, bf16[64,4096]{1,0:T(8,128)(2,1)S(1)}, u32[]{:S(2)}, u32[]{:S(2)}) collective-permute-start(bf16[64,4096]{1,0:T(8,128)(2,1)S(1)} %get-tuple-element.62), channel_id=1, source_target_pairs={{0,16},{4,20},{8,24},{12,28},{16,0},{20,4},{24,8},{28,12},{1,17},{... | collective-permute-start | bytes 1572872 | tf_op jit(solution)/shard_map/ppermute | solution.py:80
  164.0 24.5 %collective-permute-start.26 = (bf16[64,4096]{1,0:T(8,128)(2,1)S(1)}, bf16[64,4096]{1,0:T(8,128)(2,1)S(1)}, u32[]{:S(2)}, u32[]{:S(2)}) collective-permute-start(bf16[64,4096]{1,0:T(8,128)(2,1)S(1)} %get-tuple-element.61), channel_id=1, source_target_pairs={{0,16},{4,20},{8,24},{12,28},{16,0},{20,4},{24,8},{28,12},{1,17},{... | collective-permute-start | bytes 1572872 | tf_op jit(solution)/shard_map/ppermute | solution.py:80
  188.4 12.8 %collective-permute-start.32 = (bf16[64,4096]{1,0:T(8,128)(2,1)S(1)}, bf16[64,4096]{1,0:T(8,128)(2,1)S(1)}, u32[]{:S(2)}, u32[]{:S(2)}) collective-permute-start(bf16[64,4096]{1,0:T(8,128)(2,1)S(1)} %add_convert_fusion.6), channel_id=1, source_target_pairs={{0,16},{4,20},{8,24},{12,28},{16,0},{20,4},{24,8},{28,12},{1,17},{... | collective-permute-start | bytes 1572872 | tf_op jit(solution)/shard_map/ppermute | solution.py:80
  189.0 18.5 %collective-permute-start.27 = (bf16[64,4096]{1,0:T(8,128)(2,1)S(1)}, bf16[64,4096]{1,0:T(8,128)(2,1)S(1)}, u32[]{:S(2)}, u32[]{:S(2)}) collective-permute-start(bf16[64,4096]{1,0:T(8,128)(2,1)S(1)} %add_convert_fusion.8), channel_id=1, source_target_pairs={{0,8},{4,12},{8,0},{12,4},{16,24},{20,28},{24,16},{28,20},{1,9},{5... | collective-permute-start | bytes 1572872 | tf_op jit(solution)/shard_map/ppermute | solution.py:80
  201.4 11.0 %collective-permute-start.33 = (bf16[64,4096]{1,0:T(8,128)(2,1)S(1)}, bf16[64,4096]{1,0:T(8,128)(2,1)S(1)}, u32[]{:S(2)}, u32[]{:S(2)}) collective-permute-start(bf16[64,4096]{1,0:T(8,128)(2,1)S(1)} %add_convert_fusion.5), channel_id=1, source_target_pairs={{0,1},{3,2},{4,5},{7,6},{8,9},{11,10},{12,13},{15,14},{16,17},{19,... | collective-permute-start | bytes 1572872 | tf_op jit(solution)/shard_map/ppermute | solution.py:84
  203.8 25.6 %collective-permute-start.38 = (bf16[64,4096]{1,0:T(8,128)(2,1)S(1)}, bf16[64,4096]{1,0:T(8,128)(2,1)S(1)}, u32[]{:S(2)}, u32[]{:S(2)}) collective-permute-start(bf16[64,4096]{1,0:T(8,128)(2,1)S(1)} %get-tuple-element.76), channel_id=1, source_target_pairs={{0,16},{4,20},{8,24},{12,28},{16,0},{20,4},{24,8},{28,12},{1,17},{... | collective-permute-start | bytes 1572872 | tf_op jit(solution)/shard_map/ppermute | solution.py:80
  204.4 22.5 %collective-permute-start.36 = (bf16[64,4096]{1,0:T(8,128)(2,1)S(1)}, bf16[64,4096]{1,0:T(8,128)(2,1)S(1)}, u32[]{:S(2)}, u32[]{:S(2)}) collective-permute-start(bf16[64,4096]{1,0:T(8,128)(2,1)S(1)} %get-tuple-element.75), channel_id=1, source_target_pairs={{0,16},{4,20},{8,24},{12,28},{16,0},{20,4},{24,8},{28,12},{1,17},{... | collective-permute-start | bytes 1572872 | tf_op jit(solution)/shard_map/ppermute | solution.py:80
  206.6 22.0 %collective-permute-start.11 = (bf16[64,4096]{1,0:T(8,128)(2,1)S(1)}, bf16[64,4096]{1,0:T(8,128)(2,1)S(1)}, u32[]{:S(2)}, u32[]{:S(2)}) collective-permute-start(bf16[64,4096]{1,0:T(8,128)(2,1)S(1)} %get-tuple-element.51), channel_id=1, source_target_pairs={{0,8},{4,12},{8,0},{12,4},{16,24},{20,28},{24,16},{28,20},{1,9},{5... | collective-permute-start | bytes 1572872 | tf_op jit(solution)/shard_map/ppermute | solution.py:80
  207.6 37.9 %collective-permute-start.10 = (bf16[64,4096]{1,0:T(8,128)(2,1)S(1)}, bf16[64,4096]{1,0:T(8,128)(2,1)S(1)}, u32[]{:S(2)}, u32[]{:S(2)}) collective-permute-start(bf16[64,4096]{1,0:T(8,128)(2,1)S(1)} %get-tuple-element.49), channel_id=1, source_target_pairs={{0,8},{4,12},{8,0},{12,4},{16,24},{20,28},{24,16},{28,20},{1,9},{5... | collective-permute-start | bytes 1572872 | tf_op jit(solution)/shard_map/ppermute | solution.py:80
  212.7 15.1 %collective-permute-start.39 = (bf16[64,4096]{1,0:T(8,128)(2,1)S(1)}, bf16[64,4096]{1,0:T(8,128)(2,1)S(1)}, u32[]{:S(2)}, u32[]{:S(2)}) collective-permute-start(bf16[64,4096]{1,0:T(8,128)(2,1)S(1)} %get-tuple-element.78), channel_id=1, source_target_pairs={{0,1},{3,2},{4,5},{7,6},{8,9},{11,10},{12,13},{15,14},{16,17},{19,... | collective-permute-start | bytes 1572872 | tf_op jit(solution)/shard_map/ppermute | solution.py:84
  227.0 13.4 %collective-permute-start.37 = (bf16[64,4096]{1,0:T(8,128)(2,1)S(1)}, bf16[64,4096]{1,0:T(8,128)(2,1)S(1)}, u32[]{:S(2)}, u32[]{:S(2)}) collective-permute-start(bf16[64,4096]{1,0:T(8,128)(2,1)S(1)} %add_convert_fusion.3), channel_id=1, source_target_pairs={{0,8},{4,12},{8,0},{12,4},{16,24},{20,28},{24,16},{28,20},{1,9},{5... | collective-permute-start | bytes 1572872 | tf_op jit(solution)/shard_map/ppermute | solution.py:80
  227.9 12.4 %collective-permute-start.40 = (bf16[64,4096]{1,0:T(8,128)(2,1)S(1)}, bf16[64,4096]{1,0:T(8,128)(2,1)S(1)}, u32[]{:S(2)}, u32[]{:S(2)}) collective-permute-start(bf16[64,4096]{1,0:T(8,128)(2,1)S(1)} %add_convert_fusion.2), channel_id=1, source_target_pairs={{1,2},{2,1},{5,6},{6,5},{9,10},{10,9},{13,14},{14,13},{17,18},{18,... | collective-permute-start | bytes 1572872 | tf_op jit(solution)/shard_map/ppermute | solution.py:84
  228.8 16.6 %collective-permute-start.12 = (bf16[64,4096]{1,0:T(8,128)(2,1)S(1)}, bf16[64,4096]{1,0:T(8,128)(2,1)S(1)}, u32[]{:S(2)}, u32[]{:S(2)}) collective-permute-start(bf16[64,4096]{1,0:T(8,128)(2,1)S(1)} %add_convert_fusion.9), channel_id=1, source_target_pairs={{0,16},{4,20},{8,24},{12,28},{16,0},{20,4},{24,8},{28,12},{1,17},{... | collective-permute-start | bytes 1572872 | tf_op jit(solution)/shard_map/ppermute | solution.py:80
  229.4 16.0 %collective-permute-start.34 = (bf16[64,4096]{1,0:T(8,128)(2,1)S(1)}, bf16[64,4096]{1,0:T(8,128)(2,1)S(1)}, u32[]{:S(2)}, u32[]{:S(2)}) collective-permute-start(bf16[64,4096]{1,0:T(8,128)(2,1)S(1)} %get-tuple-element.77), channel_id=1, source_target_pairs={{1,2},{2,1},{5,6},{6,5},{9,10},{10,9},{13,14},{14,13},{17,18},{18,... | collective-permute-start | bytes 1572872 | tf_op jit(solution)/shard_map/ppermute | solution.py:84
  240.6 11.9 %collective-permute-start.41 = (bf16[64,4096]{1,0:T(8,128)(2,1)S(1)}, bf16[64,4096]{1,0:T(8,128)(2,1)S(1)}, u32[]{:S(2)}, u32[]{:S(2)}) collective-permute-start(bf16[64,4096]{1,0:T(8,128)(2,1)S(1)} %add_convert_fusion.1), channel_id=1, source_target_pairs={{0,1},{1,0},{2,3},{3,2},{4,5},{5,4},{6,7},{7,6},{8,9},{9,8},{10,11... | collective-permute-start | bytes 1572872 | tf_op jit(solution)/shard_map/ppermute | solution.py:84

commit v2 on v0

v2 whole, which is shorter than its diff:
```python
import functools

import jax
import jax.numpy as jnp
from jax import lax
from jax.experimental import pallas as pl
from jax.experimental.pallas import tpu as pltpu
from jax.sharding import PartitionSpec as P

TOP = 8
BLK = 128
BF16 = jnp.bfloat16
F32 = jnp.float32
VMEM_LIMIT = 48 * 1024 * 1024


def slot_numbers(expert_ids, experts):
    flat_ids = expert_ids.reshape(-1)
    onehot = (flat_ids[:, None] == jnp.arange(experts, dtype=jnp.int32)[None, :]).astype(jnp.int32)
    before = jnp.cumsum(onehot, axis=0) - onehot
    return jnp.sum(before * onehot, axis=1).reshape(expert_ids.shape)


def combine_rows(flat_rows, target, combine_weights):
    total = jnp.zeros((target.shape[0], flat_rows.shape[1]), jnp.float32)
    for pick in range(target.shape[1]):
        chosen = jnp.take(flat_rows, target[:, pick], axis=0)
        total = total + combine_weights[:, pick][:, None] * chosen
    return total


def general_device(tokens, expert_ids, combine_weights, topology, gate_blocks, up_blocks, down_blocks):
    experts = lax.axis_size(("dp", "expert"))
    width = tokens.shape[1] * lax.axis_size("tensor")
    tok_rows = tokens.shape[0]
    capacity = min(tok_rows, 3 * tok_rows * TOP // (2 * experts))
    slot_index = slot_numbers(expert_ids, experts)
    target = expert_ids * capacity + slot_index
    places = jnp.arange(experts * capacity, dtype=jnp.int32)
    matches = target[None, :, :] == places[:, None, None]
    dispatch = jnp.any(matches, axis=2).astype(BF16)
    outgoing = jnp.dot(dispatch, tokens, preferred_element_type=F32).astype(BF16)
    outgoing = outgoing.reshape(experts, capacity, tokens.shape[1])
    arrived = lax.all_to_all(outgoing, ("dp", "expert"), split_axis=0, concat_axis=0, tiled=True)
    expert_in = lax.all_gather(arrived, "tensor", axis=2, tiled=True)
    row_count = experts * capacity
    layout_ids = topology[0]
    blocked = expert_in.reshape(row_count, width // BLK, BLK)
    width_ids = jnp.arange(width // BLK, dtype=jnp.int32)
    partial_value = jnp.zeros((row_count, width // BLK, BLK), F32)
    for block in range(layout_ids.shape[0]):
        chosen = layout_ids[block]
        picked = jnp.take(blocked, chosen, axis=1)
        gate_proj = jnp.einsum("rkc,kcf->rf", picked, gate_blocks[0, block], preferred_element_type=F32)
        up_proj = jnp.einsum("rkc,kcf->rf", picked, up_blocks[0, block], preferred_element_type=F32)
        hidden = (jax.nn.silu(gate_proj) * up_proj).astype(BF16)
        pieces = jnp.einsum("rf,kfc->rkc", hidden, down_blocks[0, block], preferred_element_type=F32)
        placer = (chosen[:, None] == width_ids[None, :]).astype(F32)
        partial_value = partial_value + jnp.einsum(
            "rkc,kb->rbc", pieces, placer, precision=lax.Precision.HIGHEST
        )
    partial_low = lax.optimization_barrier(partial_value.reshape(experts, capacity, width).astype(BF16))
    shares = lax.all_to_all(
        partial_low.reshape(1, experts, capacity, width), "tensor", split_axis=3, concat_axis=0, tiled=True
    )
    summed = jnp.sum(shares.astype(F32), axis=0)
    returned_rows = lax.all_to_all(summed, ("dp", "expert"), split_axis=0, concat_axis=0, tiled=True)
    flat_rows = returned_rows.reshape(row_count, returned_rows.shape[2])
    return combine_rows(flat_rows, target, combine_weights).astype(BF16)


CORE, XBIT, YBIT = 1, 2, 4
FLIPS = (0, XBIT, YBIT, XBIT | YBIT)
XOR = {k: [(i, i ^ k) for i in range(4)] for k in (1, 2, 3)}
HALVES = 2


def flip(value, bit):
    return lax.ppermute(value, "dp", [(i, i ^ bit) for i in range(lax.axis_size("dp"))])


def along(value, pairs):
    return lax.ppermute(value, "expert", pairs)


def exchange(messages):
    across = flip(messages[3], FLIPS[3])
    return [messages[0], flip(messages[1], FLIPS[1]), flip(messages[2], FLIPS[2]), across]


def hold(values, after):
    return list(lax.optimization_barrier(tuple(values) + tuple(after))[: len(values)])


def both(arrived, others):
    held = hold([arrived[3], arrived[1], arrived[2], arrived[0]] + list(others), [])
    return [held[3], held[1], held[2], held[0]], held[4:]


def add(*values):
    return functools.reduce(lambda a, b: a + b, [v.astype(F32) for v in values]).astype(BF16)


def column(meta, lane):
    at = lax.broadcasted_iota(jnp.int32, meta.shape, 1)
    return jnp.sum(jnp.where(at == lane, meta, 0.0), axis=1, keepdims=True)


def slots_of(meta, half, ids, experts, cap, weighted):
    place = lax.broadcasted_iota(jnp.int32, (meta.shape[0], len(FLIPS) * HALVES * cap), 1)
    terms = [0.0] * (3 if weighted else 1)
    for n in range(len(FLIPS)):
        rank = column(meta, 3 * experts + ids[n]).astype(jnp.int32)
        here = place == jnp.where(rank >= 0, rank + (n * HALVES + half) * cap, -1)
        for t in range(len(terms)):
            terms[t] = jnp.where(here, column(meta, t * experts + ids[n]) if weighted else 1.0, terms[t])
    return terms


def select_kernel(width, experts, cap, ids, near, far, *outs):
    hot = jnp.concatenate(
        [slots_of(ref[:, width:].astype(F32), half, ids, experts, cap, False)[0] for half, ref in enumerate((near, far))],
        axis=0,
    ).astype(BF16)
    each = HALVES * cap
    step = 4 * BLK
    for at in range(0, width, step):
        cols = slice(at, at + step)
        block = jnp.concatenate([near[:, cols], far[:, cols]], axis=0)
        picked = lax.dot_general(hot, block, (((0,), (0,)), ((), ())), preferred_element_type=F32).astype(BF16)
        for n, out in enumerate(outs):
            out[:, cols] = picked[n * each : (n + 1) * each]


def select(ids, near, far, width, experts, cap):
    return pl.pallas_call(
        functools.partial(select_kernel, width, experts, cap),
        out_shape=[jax.ShapeDtypeStruct((HALVES * cap, width), BF16)] * len(FLIPS),
        in_specs=[pl.BlockSpec(memory_space=pltpu.SMEM)] + [pl.BlockSpec(memory_space=pltpu.VMEM)] * 2,
        out_specs=[pl.BlockSpec(memory_space=pltpu.VMEM)] * len(FLIPS),
        compiler_params=pltpu.CompilerParams(vmem_limit_bytes=VMEM_LIMIT),
        name="select_rows",
    )(ids, near, far)


def combine_kernel(width, experts, cap, ids, near, far, *refs):
    rows, (mine, theirs) = refs[:4], refs[4:]
    halves = [slots_of(ref[:, width:].astype(F32), half, ids, experts, cap, True) for half, ref in enumerate((near, far))]
    terms = [jnp.concatenate(pair, axis=0).astype(BF16) for pair in zip(*halves)]
    tokens = near.shape[0]
    step = 4 * BLK
    for at in range(0, width, step):
        cols = slice(at, at + step)
        block = jnp.concatenate([ref[:, cols] for ref in rows], axis=0)
        total = functools.reduce(
            lambda a, b: a + b, [jnp.dot(term, block, preferred_element_type=F32) for term in terms]
        )
        mine[:, cols] = total[:tokens]
        theirs[:, cols] = total[tokens:].astype(BF16)


def combine(ids, near, far, rows, width, experts, cap):
    tokens = near.shape[0]
    return pl.pallas_call(
        functools.partial(combine_kernel, width, experts, cap),
        out_shape=[jax.ShapeDtypeStruct((tokens, width), F32), jax.ShapeDtypeStruct((tokens, width), BF16)],
        in_specs=[pl.BlockSpec(memory_space=pltpu.SMEM)] + [pl.BlockSpec(memory_space=pltpu.VMEM)] * 6,
        out_specs=[pl.BlockSpec(memory_space=pltpu.VMEM)] * 2,
        compiler_params=pltpu.CompilerParams(vmem_limit_bytes=VMEM_LIMIT),
        name="combine_rows",
    )(ids, near, far, *rows)


def expert_kernel(count, topo, *refs):
    inputs, (gate, up, down) = refs[:count], refs[count : count + 3]
    outputs, (x, total) = refs[count + 3 : 2 * count + 3], refs[2 * count + 3 :]
    h = pl.program_id(0)
    rows = inputs[0].shape[0]

    @pl.when(h == 0)
    def _():
        for n, ref in enumerate(inputs):
            x[n * rows : (n + 1) * rows, :] = ref[...]
        total[...] = jnp.zeros_like(total)

    _, each, kb, _, _ = gate.shape
    cols = [[pl.ds(pl.multiple_of(topo[h * each + n, i] * BLK, BLK), BLK) for i in range(kb)] for n in range(each)]
    hidden = []
    for n in range(each):
        picked = jnp.concatenate([x[:, c] for c in cols[n]], axis=1)
        weights = jnp.concatenate([gate[0, n].reshape(kb * BLK, BLK), up[0, n].reshape(kb * BLK, BLK)], axis=1)
        both = jnp.dot(picked, weights, preferred_element_type=F32)
        gate_proj, up_proj = both[:, :BLK], both[:, BLK:]
        hidden.append((gate_proj / (1.0 + jnp.exp(-gate_proj)) * up_proj).astype(BF16))
    for n in range(each):
        for i in range(0, kb, 2):
            pair = jnp.concatenate([down[0, n, i], down[0, n, i + 1]], axis=1)
            pieces = jnp.dot(hidden[n], pair, preferred_element_type=F32)
            total[:, cols[n][i]] += pieces[:, :BLK]
            total[:, cols[n][i + 1]] += pieces[:, BLK:]

    @pl.when(h == pl.num_programs(0) - 1)
    def _():
        for n, out in enumerate(outputs):
            out[...] = total[n * rows : (n + 1) * rows, :].astype(BF16)


def expert(topo, inputs, weights):
    count, (rows, width) = len(inputs), inputs[0].shape
    _, blocks, kb, _, _ = weights[0].shape
    each = 3
    spec = pl.BlockSpec((1, each, kb, BLK, BLK), lambda h: (0, h, 0, 0, 0))
    whole = pl.BlockSpec((rows, width), lambda h: (0, 0))
    return pl.pallas_call(
        functools.partial(expert_kernel, count),
        grid=(blocks // each,),
        out_shape=[jax.ShapeDtypeStruct((rows, width), BF16)] * count,
        in_specs=[pl.BlockSpec(memory_space=pltpu.SMEM)] + [whole] * count + [spec] * 3,
        out_specs=[whole] * count,
        scratch_shapes=[pltpu.VMEM((count * rows, width), BF16), pltpu.VMEM((count * rows, width), F32)],
        compiler_params=pltpu.CompilerParams(vmem_limit_bytes=VMEM_LIMIT),
        name="expert_rows",
    )(topo, *inputs, *weights)


def with_meta(tokens, expert_ids, combine_weights, experts):
    rows = tokens.shape[0]
    named = expert_ids[:, :, None] == jnp.arange(experts, dtype=jnp.int32)[None, None, :]
    weight = jnp.sum(jnp.where(named, combine_weights[:, :, None], 0.0), axis=1)
    chosen = jnp.any(named, axis=1)
    earlier = jnp.tril(jnp.ones((rows, rows), BF16), -1)
    rank = jnp.dot(earlier, chosen.astype(BF16), preferred_element_type=F32)
    rank = jnp.where(chosen, rank, -1.0)
    high = lax.reduce_precision(weight, 8, 7)
    middle = lax.reduce_precision(weight - high, 8, 7)
    low = weight - high - middle
    return jnp.concatenate([tokens] + [v.astype(BF16) for v in (high, middle, low, rank)], axis=1)


def line_device(tokens, expert_ids, combine_weights, topology, gate_blocks, up_blocks, down_blocks):
    experts = lax.axis_size(("dp", "expert"))
    rows, width = tokens.shape
    cap = min(rows, 3 * rows * TOP // (2 * experts))
    dp, z = lax.axis_index("dp"), lax.axis_index("expert")
    ids = jnp.stack([(dp ^ bit) * lax.axis_size("expert") + z for bit in FLIPS]).astype(jnp.int32)
    topo = topology[0]
    weights = (gate_blocks, up_blocks, down_blocks)

    def chosen(near):
        far = flip(near, CORE)
        return (near, far), list(select(ids, near, far, width, experts, cap))

    def joined(pair, rows):
        mine, theirs = combine(ids, *pair, rows, width, experts, cap)
        return mine, flip(theirs, CORE)

    own = with_meta(tokens, expert_ids, combine_weights, experts)
    first, second = along(own, XOR[1]), along(own, XOR[2])
    pair0, out0 = chosen(own)

    in0 = exchange(out0)
    in0, (first, second, late) = both(in0, [first, second, own])
    pair1, out1 = chosen(first)

    in1 = exchange(out1)
    third = along(late, XOR[3])
    pair2, out2 = chosen(second)
    in0, out2 = both(in0, out2)
    back0 = expert(topo, in0, weights)
    in1, (third, *rest) = both(in1, [third] + list(out2) + list(back0))
    out2, back0 = rest[:4], rest[4:]

    in2 = exchange(out2)
    pair3, out3 = chosen(third)
    in1, out3 = both(in1, out3)
    back1 = expert(topo, in1, weights)
    in2, rest = both(in2, list(out3) + list(back1))
    out3, back1 = rest[:4], rest[4:]

    in3 = exchange(out3)
    back2 = expert(topo, in2, weights)
    in3, back2 = both(in3, back2)

    got2 = exchange(back2)
    back3 = expert(topo, in3, weights)
    got2, back3 = both(got2, back3)

    got3 = exchange(back3)
    mine2, theirs2 = joined(pair2, got2)
    sum2 = add(mine2, theirs2)
    got3, back1 = both(got3, back1)

    got1 = exchange(back1)
    far2 = along(sum2, XOR[2])
    mine3, theirs3 = joined(pair3, got3)
    mine3, theirs3, far2 = hold([mine3, theirs3, far2], [])
    sum3 = add(mine3, theirs3)
    got1, back0 = both(got1, back0)

    got0 = exchange(back0)
    far3 = along(sum3, XOR[3])
    mine1, theirs1 = joined(pair1, got1)
    mine1, theirs1, far3 = hold([mine1, theirs1, far3], [])
    sum1 = add(mine1, theirs1)
    far1 = along(sum1, XOR[1])
    mine0, theirs0 = joined(pair0, got0)
    return add(mine0, theirs0, far1, far2, far3)


def solution(mesh):
    line = mesh.shape["dp"] == 8 and mesh.shape["expert"] == 4 and mesh.shape["tensor"] == 1
    return jax.shard_map(
        line_device if line else general_device,
        mesh=mesh,
        in_specs=(
            P(("dp", "expert"), "tensor"),
            P(("dp", "expert"), None),
            P(("dp", "expert"), None),
            P(("dp", "expert"), "tensor", None),
            P(("dp", "expert"), "tensor", None, None, None),
            P(("dp", "expert"), "tensor", None, None, None),
            P(("dp", "expert"), "tensor", None, None, None),
        ),
        out_specs=P(("dp", "expert"), "tensor"),
        check_vma=False,
    )
```

time: 861 us -> 211 us (0.25); the launches traced: 850 us -> 211 us
  waiting for transfers between devices: 407 us -> 112 us
  matrix products: 288 us -> 0.19 us
  local copies, waits for them, and re-layouts: 122 us -> 2.1 us
  Pallas kernels: 0 us -> 50 us
  starting transfers between devices: 15.2 us -> 43.2 us
  other arithmetic: 16.9 us -> 2.93 us
    all_to_all x2 -> x0, waiting for transfers between devices: 407 us -> none  [the longest x1 271 us: per_device(): lax.all_to_all(summed, ('dp', 'expert'), split_axis=0, concat_axis=0, til...]
    dot_general x37 -> x1, matrix products: 288 us -> 0.19 us  [with_meta(): rank = jnp.dot(earlier, chosen.astype(BF16), preferred_element_type=F32)]
    ppermute x0 -> x38, waiting for transfers between devices: none -> 112 us  [the longest x32 79.6 us: flip(): lax.ppermute(value, 'dp', [(i, i ^ bit) for i in range(lax.axis_size('dp'...]
    gather x20 -> x0, local copies, waits for them, and re-layouts: 100 us -> none  [the longest x8 53.3 us: combine_rows(): chosen = jnp.take(flat_rows, target[:, pick], axis=0)]
    pallas_call x0 -> x12, Pallas kernels: none -> 50 us  [the longest x4 37.9 us: expert(): pl.pallas_call(functools.partial(expert_kernel, count), grid=(blocks // e...]
    ppermute x0 -> x38, starting transfers between devices: none -> 43.2 us  [the longest x32 29.5 us: flip(): lax.ppermute(value, 'dp', [(i, i ^ bit) for i in range(lax.axis_size('dp'...]
    all_to_all x2 -> x0, starting transfers between devices: 15.2 us -> none  [the longest x1 7.94 us: per_device(): lax.all_to_all(outgoing, ('dp', 'expert'), split_axis=0, concat_axis=0, t...]
    convert_element_type x3 -> x5, other arithmetic: 14.2 us -> 1.4 us  [the longest x4 1.39 us: add(): functools.reduce(lambda a, b: a + b, [v.astype(F32) for v in values])]
  transfers between devices with their start and end apart: 2 -> 38, of which waited for: 2 -> 15; matrix products, arithmetic and copies ran while one was open for 0% -> 1% of each run, Pallas kernels for 0% -> 23%
where the time goes in v2:
time: 211 us
  waiting for transfers between devices  112 us (53%)
  Pallas kernels  50 us (24%)
  starting transfers between devices  43.2 us (20%)
  other arithmetic  2.93 us (1%)
    ppermute x32, waiting for transfers between devices, flip(): lax.ppermute(value, 'dp', [(i, i ^ bit) for i in range(lax.axis_size('dp'...  79.6 us
    pallas_call x4, Pallas kernels, expert(): pl.pallas_call(functools.partial(expert_kernel, count), grid=(blocks // e...  37.9 us
    ppermute x6, waiting for transfers between devices, along(): return lax.ppermute(value, 'expert', pairs)  32.3 us
    ppermute x32, starting transfers between devices, flip(): lax.ppermute(value, 'dp', [(i, i ^ bit) for i in range(lax.axis_size('dp'...  29.5 us
    ppermute x6, starting transfers between devices, along(): return lax.ppermute(value, 'expert', pairs)  13.7 us
    pallas_call x4, Pallas kernels, combine(): pl.pallas_call(functools.partial(combine_kernel, width, experts, cap), ou...  7.02 us
    pallas_call x4, Pallas kernels, select(): pl.pallas_call(functools.partial(select_kernel, width, experts, cap), out...  5.09 us
  transfers between devices with their start and end apart: 38, of which 15 were waited for; matrix products, arithmetic and copies ran while one was open for 1% of the time, Pallas kernels for 23%

profile of v2, /device:TPU:0, one launch (start us, length us, event | category | flops | bytes accessed | tf_op | source)
XLA Modules:
  0.0 210.5 jit_solution(10140828021017116013)
XLA Ops:
  0.0 0.7 fusion.1
  0.7 0.7 select_reduce_fusion
  1.7 0.2 fusion
  1.9 1.2 concatenate.3.near
  3.1 0.5 collective-permute-start
  3.6 3.7 %collective-permute-start.5 = (bf16[64,4224]{1,0:T(8,128)(2,1)S(1)}, bf16[64,4224]{1,0:T(8,128)(2,1)S(1)}, u32[]{:S(2)}, u32[]{:S(2)}) collective-permute-start(bf16[64,4224]{1,0:T(8,128)(2,1)S(1)} %concatenate.3.near), channel_id=1, source_target_pairs={{0,2},{1,3},{2,0},{3,1},{4,6},{5,7},{6,4},{7,5},{8,10},{9,11},{10,... | collective-permute-start | bytes 1622024 | tf_op jit(solution)/shard_map/ppermute | solution.py:83
  7.3 1.6 collective-permute-start.4
  8.9 1.3 select_rows.4
  10.2 2.5 %collective-permute-start.1 = (bf16[48,4096]{1,0:T(8,128)(2,1)S(1)}, bf16[48,4096]{1,0:T(8,128)(2,1)S(1)}, u32[]{:S(2)}, u32[]{:S(2)}) collective-permute-start(bf16[48,4096]{1,0:T(8,128)(2,1)S(1)} %get-tuple-element.131), channel_id=1, source_target_pairs={{0,24},{4,28},{8,16},{12,20},{16,8},{20,12},{24,0},{28,4},{1,25},{... | collective-permute-start | bytes 1179656 | tf_op jit(solution)/shard_map/ppermute | solution.py:79
  12.7 0.5 collective-permute-start.2
  13.3 0.5 collective-permute-start.3
  13.8 18.1 %collective-permute-done.5.near = bf16[64,4224]{1,0:T(8,128)(2,1)S(1)} collective-permute-done((bf16[64,4224]{1,0:T(8,128)(2,1)S(1)}, bf16[64,4224]{1,0:T(8,128)(2,1)S(1)}, u32[]{:S(2)}, u32[]{:S(2)}) %collective-permute-start.5) | collective-permute-done | bytes 540704 | tf_op jit(solution)/shard_map/ppermute | solution.py:83
  31.8 0.2 collective-permute-done.4.near
  32.1 0.5 collective-permute-start.11
  32.6 3.3 %collective-permute-start.10 = (bf16[64,4224]{1,0:T(8,128)(2,1)S(1)}, bf16[64,4224]{1,0:T(8,128)(2,1)S(1)}, u32[]{:S(2)}, u32[]{:S(2)}) collective-permute-start(bf16[64,4224]{1,0:T(8,128)(2,1)S(1)} %concatenate.3.near), channel_id=1, source_target_pairs={{0,3},{1,2},{2,1},{3,0},{4,7},{5,6},{6,5},{7,4},{8,11},{9,10},{10,... | collective-permute-start | bytes 1622024 | tf_op jit(solution)/shard_map/ppermute | solution.py:83
  35.9 1.3 select_rows.5
  37.2 2.5 %collective-permute-start.7 = (bf16[48,4096]{1,0:T(8,128)(2,1)S(1)}, bf16[48,4096]{1,0:T(8,128)(2,1)S(1)}, u32[]{:S(2)}, u32[]{:S(2)}) collective-permute-start(bf16[48,4096]{1,0:T(8,128)(2,1)S(1)} %get-tuple-element.136), channel_id=1, source_target_pairs={{0,24},{4,28},{8,16},{12,20},{16,8},{20,12},{24,0},{28,4},{1,25},{... | collective-permute-start | bytes 1179656 | tf_op jit(solution)/shard_map/ppermute | solution.py:79
  39.7 0.5 collective-permute-start.8
  40.2 0.5 collective-permute-start.9
  40.7 0.7 copy.23
  41.4 1.3 select_rows.6
  42.7 9.4 %expert_rows.4 = (bf16[48,4096]{1,0:T(8,128)(2,1)S(1)}, bf16[48,4096]{1,0:T(8,128)(2,1)S(1)}, bf16[48,4096]{1,0:T(8,128)(2,1)S(1)}, bf16[48,4096]{1,0:T(8,128)(2,1)S(1)}) custom-call(s32[12,12]{1,0:T(8,128)S(1)} %bitcast.8, bf16[48,4096]{1,0:T(8,128)(2,1)S(1)} %get-tuple-element.154.refs_0_, bf16[48,4096]{1,0:T(8,128)(2,1)S(1)} %collective-permute-done.2.refs_1_, ...), custom_call_target="tpu_custom_call" | custom-call | tf_op jit(solution)/shard_map/expert_rows/pallas_call | solution.py:214
  52.2 5.3 %collective-permute-done.8.refs_1_ = bf16[48,4096]{1,0:T(8,128)(2,1)S(1)} collective-permute-done((bf16[48,4096]{1,0:T(8,128)(2,1)S(1)}, bf16[48,4096]{1,0:T(8,128)(2,1)S(1)}, u32[]{:S(2)}, u32[]{:S(2)}) %collective-permute-start.8) | collective-permute-done | bytes 393248 | tf_op jit(solution)/shard_map/ppermute | solution.py:79
  57.5 2.4 %collective-permute-start.12 = (bf16[48,4096]{1,0:T(8,128)(2,1)S(1)}, bf16[48,4096]{1,0:T(8,128)(2,1)S(1)}, u32[]{:S(2)}, u32[]{:S(2)}) collective-permute-start(bf16[48,4096]{1,0:T(8,128)(2,1)S(1)} %get-tuple-element.162), channel_id=1, source_target_pairs={{0,24},{4,28},{8,16},{12,20},{16,8},{20,12},{24,0},{28,4},{1,25},{... | collective-permute-start | bytes 1179656 | tf_op jit(solution)/shard_map/ppermute | solution.py:79
  59.8 0.5 collective-permute-start.13
  60.4 0.6 collective-permute-start.14
  61.0 1.3 select_rows.7
  62.3 9.4 %expert_rows.5 = (bf16[48,4096]{1,0:T(8,128)(2,1)S(1)}, bf16[48,4096]{1,0:T(8,128)(2,1)S(1)}, bf16[48,4096]{1,0:T(8,128)(2,1)S(1)}, bf16[48,4096]{1,0:T(8,128)(2,1)S(1)}) custom-call(s32[12,12]{1,0:T(8,128)S(1)} %bitcast.9, bf16[48,4096]{1,0:T(8,128)(2,1)S(1)} %get-tuple-element.179.refs_0_, bf16[48,4096]{1,0:T(8,128)(2,1)S(1)} %collective-permute-done.8.refs_1_, ...), custom_call_target="tpu_custom_call" | custom-call | tf_op jit(solution)/shard_map/expert_rows/pallas_call | solution.py:214
  71.7 6.6 %collective-permute-done.13.refs_1_ = bf16[48,4096]{1,0:T(8,128)(2,1)S(1)} collective-permute-done((bf16[48,4096]{1,0:T(8,128)(2,1)S(1)}, bf16[48,4096]{1,0:T(8,128)(2,1)S(1)}, u32[]{:S(2)}, u32[]{:S(2)}) %collective-permute-start.13) | collective-permute-done | bytes 393248 | tf_op jit(solution)/shard_map/ppermute | solution.py:79
  78.3 2.3 %collective-permute-start.16 = (bf16[48,4096]{1,0:T(8,128)(2,1)S(1)}, bf16[48,4096]{1,0:T(8,128)(2,1)S(1)}, u32[]{:S(2)}, u32[]{:S(2)}) collective-permute-start(bf16[48,4096]{1,0:T(8,128)(2,1)S(1)} %get-tuple-element.187), channel_id=1, source_target_pairs={{0,24},{4,28},{8,16},{12,20},{16,8},{20,12},{24,0},{28,4},{1,25},{... | collective-permute-start | bytes 1179656 | tf_op jit(solution)/shard_map/ppermute | solution.py:79
  80.7 0.5 collective-permute-start.17
  81.2 0.6 collective-permute-start.18
  81.8 9.4 %expert_rows.6 = (bf16[48,4096]{1,0:T(8,128)(2,1)S(1)}, bf16[48,4096]{1,0:T(8,128)(2,1)S(1)}, bf16[48,4096]{1,0:T(8,128)(2,1)S(1)}, bf16[48,4096]{1,0:T(8,128)(2,1)S(1)}) custom-call(s32[12,12]{1,0:T(8,128)S(1)} %bitcast.10, bf16[48,4096]{1,0:T(8,128)(2,1)S(1)} %get-tuple-element.191.refs_0_, bf16[48,4096]{1,0:T(8,128)(2,1)S(1)} %collective-permute-done.13.refs_1_, ...), custom_call_target="tpu_custom_call" | custom-call | tf_op jit(solution)/shard_map/expert_rows/pallas_call | solution.py:214
  91.3 7.4 %collective-permute-done.17.refs_1_ = bf16[48,4096]{1,0:T(8,128)(2,1)S(1)} collective-permute-done((bf16[48,4096]{1,0:T(8,128)(2,1)S(1)}, bf16[48,4096]{1,0:T(8,128)(2,1)S(1)}, u32[]{:S(2)}, u32[]{:S(2)}) %collective-permute-start.17) | collective-permute-done | bytes 393248 | tf_op jit(solution)/shard_map/ppermute | solution.py:79
  98.7 2.3 %collective-permute-start.19 = (bf16[48,4096]{1,0:T(8,128)(2,1)S(1)}, bf16[48,4096]{1,0:T(8,128)(2,1)S(1)}, u32[]{:S(2)}, u32[]{:S(2)}) collective-permute-start(bf16[48,4096]{1,0:T(8,128)(2,1)S(1)} %get-tuple-element.199), channel_id=1, source_target_pairs={{0,24},{4,28},{8,16},{12,20},{16,8},{20,12},{24,0},{28,4},{1,25},{... | collective-permute-start | bytes 1179656 | tf_op jit(solution)/shard_map/ppermute | solution.py:79
  101.0 0.5 collective-permute-start.20
  101.6 0.6 collective-permute-start.21
  102.2 9.6 %expert_rows.7 = (bf16[48,4096]{1,0:T(8,128)(2,1)S(1)}, bf16[48,4096]{1,0:T(8,128)(2,1)S(1)}, bf16[48,4096]{1,0:T(8,128)(2,1)S(1)}, bf16[48,4096]{1,0:T(8,128)(2,1)S(1)}) custom-call(s32[12,12]{1,0:T(8,128)S(1)} %bitcast.11, bf16[48,4096]{1,0:T(8,128)(2,1)S(1)} %get-tuple-element.203.refs_0_, bf16[48,4096]{1,0:T(8,128)(2,1)S(1)} %collective-permute-done.17.refs_1_, ...), custom_call_target="tpu_custom_call" | custom-call | tf_op jit(solution)/shard_map/expert_rows/pallas_call | solution.py:214
  111.8 7.3 %collective-permute-done.20.refs_1_ = bf16[48,4096]{1,0:T(8,128)(2,1)S(1)} collective-permute-done((bf16[48,4096]{1,0:T(8,128)(2,1)S(1)}, bf16[48,4096]{1,0:T(8,128)(2,1)S(1)}, u32[]{:S(2)}, u32[]{:S(2)}) %collective-permute-start.20) | collective-permute-done | bytes 393248 | tf_op jit(solution)/shard_map/ppermute | solution.py:79
  119.1 1.8 combine_rows.7
  120.9 2.4 %collective-permute-start.22 = (bf16[48,4096]{1,0:T(8,128)(2,1)S(1)}, bf16[48,4096]{1,0:T(8,128)(2,1)S(1)}, u32[]{:S(2)}, u32[]{:S(2)}) collective-permute-start(bf16[48,4096]{1,0:T(8,128)(2,1)S(1)} %get-tuple-element.211), channel_id=1, source_target_pairs={{0,24},{4,28},{8,16},{12,20},{16,8},{20,12},{24,0},{28,4},{1,25},{... | collective-permute-start | bytes 1179656 | tf_op jit(solution)/shard_map/ppermute | solution.py:79
  123.3 0.5 collective-permute-start.23
  123.8 0.6 collective-permute-start.24
  124.5 9.4 %collective-permute-done.22.refs_3_ = bf16[48,4096]{1,0:T(8,128)(2,1)S(1)} collective-permute-done((bf16[48,4096]{1,0:T(8,128)(2,1)S(1)}, bf16[48,4096]{1,0:T(8,128)(2,1)S(1)}, u32[]{:S(2)}, u32[]{:S(2)}) %collective-permute-start.22) | collective-permute-done | bytes 393248 | tf_op jit(solution)/shard_map/ppermute | solution.py:79
  133.8 7.9 %collective-permute-done.23.refs_1_ = bf16[48,4096]{1,0:T(8,128)(2,1)S(1)} collective-permute-done((bf16[48,4096]{1,0:T(8,128)(2,1)S(1)}, bf16[48,4096]{1,0:T(8,128)(2,1)S(1)}, u32[]{:S(2)}, u32[]{:S(2)}) %collective-permute-start.23) | collective-permute-done | bytes 393248 | tf_op jit(solution)/shard_map/ppermute | solution.py:79
  141.8 1.8 combine_rows.6
  143.7 2.6 %collective-permute-start.35 = (bf16[64,4096]{1,0:T(8,128)(2,1)S(1)}, bf16[64,4096]{1,0:T(8,128)(2,1)S(1)}, u32[]{:S(2)}, u32[]{:S(2)}) collective-permute-start(bf16[64,4096]{1,0:T(8,128)(2,1)S(1)} %add_convert_fusion.3), channel_id=1, source_target_pairs={{0,2},{1,3},{2,0},{3,1},{4,6},{5,7},{6,4},{7,5},{8,10},{9,11},{10,... | collective-permute-start | bytes 1572872 | tf_op jit(solution)/shard_map/ppermute | solution.py:83
  146.3 2.3 %collective-permute-start.25 = (bf16[48,4096]{1,0:T(8,128)(2,1)S(1)}, bf16[48,4096]{1,0:T(8,128)(2,1)S(1)}, u32[]{:S(2)}, u32[]{:S(2)}) collective-permute-start(bf16[48,4096]{1,0:T(8,128)(2,1)S(1)} %get-tuple-element.219), channel_id=1, source_target_pairs={{0,24},{4,28},{8,16},{12,20},{16,8},{20,12},{24,0},{28,4},{1,25},{... | collective-permute-start | bytes 1179656 | tf_op jit(solution)/shard_map/ppermute | solution.py:79
  148.7 0.5 collective-permute-start.26
  149.2 0.6 collective-permute-start.27
  149.8 9.4 %collective-permute-done.25.refs_3_ = bf16[48,4096]{1,0:T(8,128)(2,1)S(1)} collective-permute-done((bf16[48,4096]{1,0:T(8,128)(2,1)S(1)}, bf16[48,4096]{1,0:T(8,128)(2,1)S(1)}, u32[]{:S(2)}, u32[]{:S(2)}) %collective-permute-start.25) | collective-permute-done | bytes 393248 | tf_op jit(solution)/shard_map/ppermute | solution.py:79
  159.2 7.6 %collective-permute-done.26.refs_1_ = bf16[48,4096]{1,0:T(8,128)(2,1)S(1)} collective-permute-done((bf16[48,4096]{1,0:T(8,128)(2,1)S(1)}, bf16[48,4096]{1,0:T(8,128)(2,1)S(1)}, u32[]{:S(2)}, u32[]{:S(2)}) %collective-permute-start.26) | collective-permute-done | bytes 393248 | tf_op jit(solution)/shard_map/ppermute | solution.py:79
  166.9 1.8 combine_rows.5
  168.7 1.5 collective-permute-done.35
  170.3 2.5 %collective-permute-start.36 = (bf16[64,4096]{1,0:T(8,128)(2,1)S(1)}, bf16[64,4096]{1,0:T(8,128)(2,1)S(1)}, u32[]{:S(2)}, u32[]{:S(2)}) collective-permute-start(bf16[64,4096]{1,0:T(8,128)(2,1)S(1)} %add_convert_fusion.2), channel_id=1, source_target_pairs={{0,3},{1,2},{2,1},{3,0},{4,7},{5,6},{6,5},{7,4},{8,11},{9,10},{10,... | collective-permute-start | bytes 1572872 | tf_op jit(solution)/shard_map/ppermute | solution.py:83
  172.8 1.5 collective-permute-start.28
  174.3 1.4 collective-permute-start.29
  175.7 0.6 collective-permute-start.30
  176.3 8.5 %collective-permute-done.28.refs_1_ = bf16[48,4096]{1,0:T(8,128)(2,1)S(1)} collective-permute-done((bf16[48,4096]{1,0:T(8,128)(2,1)S(1)}, bf16[48,4096]{1,0:T(8,128)(2,1)S(1)}, u32[]{:S(2)}, u32[]{:S(2)}) %collective-permute-start.28) | collective-permute-done | bytes 393248 | tf_op jit(solution)/shard_map/ppermute | solution.py:79
  184.8 8.3 %collective-permute-done.29.refs_2_ = bf16[48,4096]{1,0:T(8,128)(2,1)S(1)} collective-permute-done((bf16[48,4096]{1,0:T(8,128)(2,1)S(1)}, bf16[48,4096]{1,0:T(8,128)(2,1)S(1)}, u32[]{:S(2)}, u32[]{:S(2)}) %collective-permute-start.29) | collective-permute-done | bytes 393248 | tf_op jit(solution)/shard_map/ppermute | solution.py:79
  193.1 1.8 combine_rows.4
  195.1 1.7 collective-permute-done.31
  196.8 12.6 %collective-permute-done.37 = bf16[64,4096]{1,0:T(8,128)(2,1)S(1)} collective-permute-done((bf16[64,4096]{1,0:T(8,128)(2,1)S(1)}, bf16[64,4096]{1,0:T(8,128)(2,1)S(1)}, u32[]{:S(2)}, u32[]{:S(2)}) %collective-permute-start.37) | collective-permute-done | bytes 524320 | tf_op jit(solution)/shard_map/ppermute | solution.py:83
  209.4 1.1 add_convert_fusion
  (40 shorter events, 1.2 us)
Async XLA Ops:
  3.1 5.8 %collective-permute-start = (bf16[64,4224]{1,0:T(8,128)(2,1)S(1)}, bf16[64,4224]{1,0:T(8,128)(2,1)S(1)}, u32[]{:S(2)}, u32[]{:S(2)}) collective-permute-start(bf16[64,4224]{1,0:T(8,128)(2,1)S(1)} %concatenate.3.near), channel_id=1, source_target_pairs={{0,4},{4,0},{8,12},{12,8},{16,20},{20,16},{24,28},{28,24},{1,5},{5... | collective-permute-start | bytes 1622024 | tf_op jit(solution)/shard_map/ppermute | solution.py:79
  3.6 28.2 %collective-permute-start.5 = (bf16[64,4224]{1,0:T(8,128)(2,1)S(1)}, bf16[64,4224]{1,0:T(8,128)(2,1)S(1)}, u32[]{:S(2)}, u32[]{:S(2)}) collective-permute-start(bf16[64,4224]{1,0:T(8,128)(2,1)S(1)} %concatenate.3.near), channel_id=1, source_target_pairs={{0,2},{1,3},{2,0},{3,1},{4,6},{5,7},{6,4},{7,5},{8,10},{9,11},{10,... | collective-permute-start | bytes 1622024 | tf_op jit(solution)/shard_map/ppermute | solution.py:83
  7.3 24.8 %collective-permute-start.4 = (bf16[64,4224]{1,0:T(8,128)(2,1)S(1)}, bf16[64,4224]{1,0:T(8,128)(2,1)S(1)}, u32[]{:S(2)}, u32[]{:S(2)}) collective-permute-start(bf16[64,4224]{1,0:T(8,128)(2,1)S(1)} %concatenate.3.near), channel_id=1, source_target_pairs={{0,1},{1,0},{2,3},{3,2},{4,5},{5,4},{6,7},{7,6},{8,9},{9,8},{10,11... | collective-permute-start | bytes 1622024 | tf_op jit(solution)/shard_map/ppermute | solution.py:83
  10.2 21.8 %collective-permute-start.1 = (bf16[48,4096]{1,0:T(8,128)(2,1)S(1)}, bf16[48,4096]{1,0:T(8,128)(2,1)S(1)}, u32[]{:S(2)}, u32[]{:S(2)}) collective-permute-start(bf16[48,4096]{1,0:T(8,128)(2,1)S(1)} %get-tuple-element.131), channel_id=1, source_target_pairs={{0,24},{4,28},{8,16},{12,20},{16,8},{20,12},{24,0},{28,4},{1,25},{... | collective-permute-start | bytes 1179656 | tf_op jit(solution)/shard_map/ppermute | solution.py:79
  12.7 19.3 %collective-permute-start.2 = (bf16[48,4096]{1,0:T(8,128)(2,1)S(1)}, bf16[48,4096]{1,0:T(8,128)(2,1)S(1)}, u32[]{:S(2)}, u32[]{:S(2)}) collective-permute-start(bf16[48,4096]{1,0:T(8,128)(2,1)S(1)} %get-tuple-element.132), channel_id=1, source_target_pairs={{0,8},{4,12},{8,0},{12,4},{16,24},{20,28},{24,16},{28,20},{1,9},{5... | collective-permute-start | bytes 1179656 | tf_op jit(solution)/shard_map/ppermute | solution.py:79
  13.3 18.8 %collective-permute-start.3 = (bf16[48,4096]{1,0:T(8,128)(2,1)S(1)}, bf16[48,4096]{1,0:T(8,128)(2,1)S(1)}, u32[]{:S(2)}, u32[]{:S(2)}) collective-permute-start(bf16[48,4096]{1,0:T(8,128)(2,1)S(1)} %get-tuple-element.133), channel_id=1, source_target_pairs={{0,16},{4,20},{8,24},{12,28},{16,0},{20,4},{24,8},{28,12},{1,17},{... | collective-permute-start | bytes 1179656 | tf_op jit(solution)/shard_map/ppermute | solution.py:79
  32.0 3.8 %collective-permute-start.6 = (bf16[64,4224]{1,0:T(8,128)(2,1)S(1)}, bf16[64,4224]{1,0:T(8,128)(2,1)S(1)}, u32[]{:S(2)}, u32[]{:S(2)}) collective-permute-start(bf16[64,4224]{1,0:T(8,128)(2,1)S(1)} %collective-permute-done.4.near), channel_id=1, source_target_pairs={{0,4},{4,0},{8,12},{12,8},{16,20},{20,16},{24,28},{28,24},{1,5},{5... | collective-permute-start | bytes 1622024 | tf_op jit(solution)/shard_map/ppermute | solution.py:79
  32.1 9.3 %collective-permute-start.11 = (bf16[64,4224]{1,0:T(8,128)(2,1)S(1)}, bf16[64,4224]{1,0:T(8,128)(2,1)S(1)}, u32[]{:S(2)}, u32[]{:S(2)}) collective-permute-start(bf16[64,4224]{1,0:T(8,128)(2,1)S(1)} %collective-permute-done.5.near), channel_id=1, source_target_pairs={{0,4},{4,0},{8,12},{12,8},{16,20},{20,16},{24,28},{28,24},{1,5},{5... | collective-permute-start | bytes 1622024 | tf_op jit(solution)/shard_map/ppermute | solution.py:79
  32.6 19.5 %collective-permute-start.10 = (bf16[64,4224]{1,0:T(8,128)(2,1)S(1)}, bf16[64,4224]{1,0:T(8,128)(2,1)S(1)}, u32[]{:S(2)}, u32[]{:S(2)}) collective-permute-start(bf16[64,4224]{1,0:T(8,128)(2,1)S(1)} %concatenate.3.near), channel_id=1, source_target_pairs={{0,3},{1,2},{2,1},{3,0},{4,7},{5,6},{6,5},{7,4},{8,11},{9,10},{10,... | collective-permute-start | bytes 1622024 | tf_op jit(solution)/shard_map/ppermute | solution.py:83
  37.2 15.0 %collective-permute-start.7 = (bf16[48,4096]{1,0:T(8,128)(2,1)S(1)}, bf16[48,4096]{1,0:T(8,128)(2,1)S(1)}, u32[]{:S(2)}, u32[]{:S(2)}) collective-permute-start(bf16[48,4096]{1,0:T(8,128)(2,1)S(1)} %get-tuple-element.136), channel_id=1, source_target_pairs={{0,24},{4,28},{8,16},{12,20},{16,8},{20,12},{24,0},{28,4},{1,25},{... | collective-permute-start | bytes 1179656 | tf_op jit(solution)/shard_map/ppermute | solution.py:79
  39.7 17.8 %collective-permute-start.8 = (bf16[48,4096]{1,0:T(8,128)(2,1)S(1)}, bf16[48,4096]{1,0:T(8,128)(2,1)S(1)}, u32[]{:S(2)}, u32[]{:S(2)}) collective-permute-start(bf16[48,4096]{1,0:T(8,128)(2,1)S(1)} %get-tuple-element.137), channel_id=1, source_target_pairs={{0,8},{4,12},{8,0},{12,4},{16,24},{20,28},{24,16},{28,20},{1,9},{5... | collective-permute-start | bytes 1179656 | tf_op jit(solution)/shard_map/ppermute | solution.py:79
  40.2 17.3 %collective-permute-start.9 = (bf16[48,4096]{1,0:T(8,128)(2,1)S(1)}, bf16[48,4096]{1,0:T(8,128)(2,1)S(1)}, u32[]{:S(2)}, u32[]{:S(2)}) collective-permute-start(bf16[48,4096]{1,0:T(8,128)(2,1)S(1)} %get-tuple-element.138), channel_id=1, source_target_pairs={{0,16},{4,20},{8,24},{12,28},{16,0},{20,4},{24,8},{28,12},{1,17},{... | collective-permute-start | bytes 1179656 | tf_op jit(solution)/shard_map/ppermute | solution.py:79
  57.5 3.5 %collective-permute-start.15 = (bf16[64,4224]{1,0:T(8,128)(2,1)S(1)}, bf16[64,4224]{1,0:T(8,128)(2,1)S(1)}, u32[]{:S(2)}, u32[]{:S(2)}) collective-permute-start(bf16[64,4224]{1,0:T(8,128)(2,1)S(1)} %collective-permute-done.10.near), channel_id=1, source_target_pairs={{0,4},{4,0},{8,12},{12,8},{16,20},{20,16},{24,28},{28,24},{1,5},{5... | collective-permute-start | bytes 1622024 | tf_op jit(solution)/shard_map/ppermute | solution.py:79
  57.5 14.2 %collective-permute-start.12 = (bf16[48,4096]{1,0:T(8,128)(2,1)S(1)}, bf16[48,4096]{1,0:T(8,128)(2,1)S(1)}, u32[]{:S(2)}, u32[]{:S(2)}) collective-permute-start(bf16[48,4096]{1,0:T(8,128)(2,1)S(1)} %get-tuple-element.162), channel_id=1, source_target_pairs={{0,24},{4,28},{8,16},{12,20},{16,8},{20,12},{24,0},{28,4},{1,25},{... | collective-permute-start | bytes 1179656 | tf_op jit(solution)/shard_map/ppermute | solution.py:79
  59.8 18.5 %collective-permute-start.13 = (bf16[48,4096]{1,0:T(8,128)(2,1)S(1)}, bf16[48,4096]{1,0:T(8,128)(2,1)S(1)}, u32[]{:S(2)}, u32[]{:S(2)}) collective-permute-start(bf16[48,4096]{1,0:T(8,128)(2,1)S(1)} %get-tuple-element.163), channel_id=1, source_target_pairs={{0,8},{4,12},{8,0},{12,4},{16,24},{20,28},{24,16},{28,20},{1,9},{5... | collective-permute-start | bytes 1179656 | tf_op jit(solution)/shard_map/ppermute | solution.py:79
  60.4 18.0 %collective-permute-start.14 = (bf16[48,4096]{1,0:T(8,128)(2,1)S(1)}, bf16[48,4096]{1,0:T(8,128)(2,1)S(1)}, u32[]{:S(2)}, u32[]{:S(2)}) collective-permute-start(bf16[48,4096]{1,0:T(8,128)(2,1)S(1)} %get-tuple-element.164), channel_id=1, source_target_pairs={{0,16},{4,20},{8,24},{12,28},{16,0},{20,4},{24,8},{28,12},{1,17},{... | collective-permute-start | bytes 1179656 | tf_op jit(solution)/shard_map/ppermute | solution.py:79
  78.3 12.9 %collective-permute-start.16 = (bf16[48,4096]{1,0:T(8,128)(2,1)S(1)}, bf16[48,4096]{1,0:T(8,128)(2,1)S(1)}, u32[]{:S(2)}, u32[]{:S(2)}) collective-permute-start(bf16[48,4096]{1,0:T(8,128)(2,1)S(1)} %get-tuple-element.187), channel_id=1, source_target_pairs={{0,24},{4,28},{8,16},{12,20},{16,8},{20,12},{24,0},{28,4},{1,25},{... | collective-permute-start | bytes 1179656 | tf_op jit(solution)/shard_map/ppermute | solution.py:79
  80.7 18.0 %collective-permute-start.17 = (bf16[48,4096]{1,0:T(8,128)(2,1)S(1)}, bf16[48,4096]{1,0:T(8,128)(2,1)S(1)}, u32[]{:S(2)}, u32[]{:S(2)}) collective-permute-start(bf16[48,4096]{1,0:T(8,128)(2,1)S(1)} %get-tuple-element.188), channel_id=1, source_target_pairs={{0,8},{4,12},{8,0},{12,4},{16,24},{20,28},{24,16},{28,20},{1,9},{5... | collective-permute-start | bytes 1179656 | tf_op jit(solution)/shard_map/ppermute | solution.py:79
  81.2 17.5 %collective-permute-start.18 = (bf16[48,4096]{1,0:T(8,128)(2,1)S(1)}, bf16[48,4096]{1,0:T(8,128)(2,1)S(1)}, u32[]{:S(2)}, u32[]{:S(2)}) collective-permute-start(bf16[48,4096]{1,0:T(8,128)(2,1)S(1)} %get-tuple-element.189), channel_id=1, source_target_pairs={{0,16},{4,20},{8,24},{12,28},{16,0},{20,4},{24,8},{28,12},{1,17},{... | collective-permute-start | bytes 1179656 | tf_op jit(solution)/shard_map/ppermute | solution.py:79
  98.7 13.1 %collective-permute-start.19 = (bf16[48,4096]{1,0:T(8,128)(2,1)S(1)}, bf16[48,4096]{1,0:T(8,128)(2,1)S(1)}, u32[]{:S(2)}, u32[]{:S(2)}) collective-permute-start(bf16[48,4096]{1,0:T(8,128)(2,1)S(1)} %get-tuple-element.199), channel_id=1, source_target_pairs={{0,24},{4,28},{8,16},{12,20},{16,8},{20,12},{24,0},{28,4},{1,25},{... | collective-permute-start | bytes 1179656 | tf_op jit(solution)/shard_map/ppermute | solution.py:79
  101.0 18.0 %collective-permute-start.20 = (bf16[48,4096]{1,0:T(8,128)(2,1)S(1)}, bf16[48,4096]{1,0:T(8,128)(2,1)S(1)}, u32[]{:S(2)}, u32[]{:S(2)}) collective-permute-start(bf16[48,4096]{1,0:T(8,128)(2,1)S(1)} %get-tuple-element.200), channel_id=1, source_target_pairs={{0,8},{4,12},{8,0},{12,4},{16,24},{20,28},{24,16},{28,20},{1,9},{5... | collective-permute-start | bytes 1179656 | tf_op jit(solution)/shard_map/ppermute | solution.py:79
  101.6 17.5 %collective-permute-start.21 = (bf16[48,4096]{1,0:T(8,128)(2,1)S(1)}, bf16[48,4096]{1,0:T(8,128)(2,1)S(1)}, u32[]{:S(2)}, u32[]{:S(2)}) collective-permute-start(bf16[48,4096]{1,0:T(8,128)(2,1)S(1)} %get-tuple-element.201), channel_id=1, source_target_pairs={{0,16},{4,20},{8,24},{12,28},{16,0},{20,4},{24,8},{28,12},{1,17},{... | collective-permute-start | bytes 1179656 | tf_op jit(solution)/shard_map/ppermute | solution.py:79
  120.8 22.8 %collective-permute-start.34 = (bf16[64,4096]{1,0:T(8,128)(2,1)S(1)}, bf16[64,4096]{1,0:T(8,128)(2,1)S(1)}, u32[]{:S(2)}, u32[]{:S(2)}) collective-permute-start(bf16[64,4096]{1,0:T(8,128)(2,1)S(1)} %get-tuple-element.250), channel_id=1, source_target_pairs={{0,4},{4,0},{8,12},{12,8},{16,20},{20,16},{24,28},{28,24},{1,5},{5... | collective-permute-start | bytes 1572872 | tf_op jit(solution)/shard_map/ppermute | solution.py:79
  120.9 12.9 %collective-permute-start.22 = (bf16[48,4096]{1,0:T(8,128)(2,1)S(1)}, bf16[48,4096]{1,0:T(8,128)(2,1)S(1)}, u32[]{:S(2)}, u32[]{:S(2)}) collective-permute-start(bf16[48,4096]{1,0:T(8,128)(2,1)S(1)} %get-tuple-element.211), channel_id=1, source_target_pairs={{0,24},{4,28},{8,16},{12,20},{16,8},{20,12},{24,0},{28,4},{1,25},{... | collective-permute-start | bytes 1179656 | tf_op jit(solution)/shard_map/ppermute | solution.py:79
  123.3 18.4 %collective-permute-start.23 = (bf16[48,4096]{1,0:T(8,128)(2,1)S(1)}, bf16[48,4096]{1,0:T(8,128)(2,1)S(1)}, u32[]{:S(2)}, u32[]{:S(2)}) collective-permute-start(bf16[48,4096]{1,0:T(8,128)(2,1)S(1)} %get-tuple-element.212), channel_id=1, source_target_pairs={{0,8},{4,12},{8,0},{12,4},{16,24},{20,28},{24,16},{28,20},{1,9},{5... | collective-permute-start | bytes 1179656 | tf_op jit(solution)/shard_map/ppermute | solution.py:79
  123.8 17.9 %collective-permute-start.24 = (bf16[48,4096]{1,0:T(8,128)(2,1)S(1)}, bf16[48,4096]{1,0:T(8,128)(2,1)S(1)}, u32[]{:S(2)}, u32[]{:S(2)}) collective-permute-start(bf16[48,4096]{1,0:T(8,128)(2,1)S(1)} %get-tuple-element.213), channel_id=1, source_target_pairs={{0,16},{4,20},{8,24},{12,28},{16,0},{20,4},{24,8},{28,12},{1,17},{... | collective-permute-start | bytes 1179656 | tf_op jit(solution)/shard_map/ppermute | solution.py:79
  143.5 25.2 %collective-permute-start.33 = (bf16[64,4096]{1,0:T(8,128)(2,1)S(1)}, bf16[64,4096]{1,0:T(8,128)(2,1)S(1)}, u32[]{:S(2)}, u32[]{:S(2)}) collective-permute-start(bf16[64,4096]{1,0:T(8,128)(2,1)S(1)} %get-tuple-element.244), channel_id=1, source_target_pairs={{0,4},{4,0},{8,12},{12,8},{16,20},{20,16},{24,28},{28,24},{1,5},{5... | collective-permute-start | bytes 1572872 | tf_op jit(solution)/shard_map/ppermute | solution.py:79
  143.7 26.5 %collective-permute-start.35 = (bf16[64,4096]{1,0:T(8,128)(2,1)S(1)}, bf16[64,4096]{1,0:T(8,128)(2,1)S(1)}, u32[]{:S(2)}, u32[]{:S(2)}) collective-permute-start(bf16[64,4096]{1,0:T(8,128)(2,1)S(1)} %add_convert_fusion.3), channel_id=1, source_target_pairs={{0,2},{1,3},{2,0},{3,1},{4,6},{5,7},{6,4},{7,5},{8,10},{9,11},{10,... | collective-permute-start | bytes 1572872 | tf_op jit(solution)/shard_map/ppermute | solution.py:83
  146.3 12.9 %collective-permute-start.25 = (bf16[48,4096]{1,0:T(8,128)(2,1)S(1)}, bf16[48,4096]{1,0:T(8,128)(2,1)S(1)}, u32[]{:S(2)}, u32[]{:S(2)}) collective-permute-start(bf16[48,4096]{1,0:T(8,128)(2,1)S(1)} %get-tuple-element.219), channel_id=1, source_target_pairs={{0,24},{4,28},{8,16},{12,20},{16,8},{20,12},{24,0},{28,4},{1,25},{... | collective-permute-start | bytes 1179656 | tf_op jit(solution)/shard_map/ppermute | solution.py:79
  148.7 18.2 %collective-permute-start.26 = (bf16[48,4096]{1,0:T(8,128)(2,1)S(1)}, bf16[48,4096]{1,0:T(8,128)(2,1)S(1)}, u32[]{:S(2)}, u32[]{:S(2)}) collective-permute-start(bf16[48,4096]{1,0:T(8,128)(2,1)S(1)} %get-tuple-element.220), channel_id=1, source_target_pairs={{0,8},{4,12},{8,0},{12,4},{16,24},{20,28},{24,16},{28,20},{1,9},{5... | collective-permute-start | bytes 1179656 | tf_op jit(solution)/shard_map/ppermute | solution.py:79
  149.2 17.7 %collective-permute-start.27 = (bf16[48,4096]{1,0:T(8,128)(2,1)S(1)}, bf16[48,4096]{1,0:T(8,128)(2,1)S(1)}, u32[]{:S(2)}, u32[]{:S(2)}) collective-permute-start(bf16[48,4096]{1,0:T(8,128)(2,1)S(1)} %get-tuple-element.221), channel_id=1, source_target_pairs={{0,16},{4,20},{8,24},{12,28},{16,0},{20,4},{24,8},{28,12},{1,17},{... | collective-permute-start | bytes 1179656 | tf_op jit(solution)/shard_map/ppermute | solution.py:79
  168.7 26.3 %collective-permute-start.32 = (bf16[64,4096]{1,0:T(8,128)(2,1)S(1)}, bf16[64,4096]{1,0:T(8,128)(2,1)S(1)}, u32[]{:S(2)}, u32[]{:S(2)}) collective-permute-start(bf16[64,4096]{1,0:T(8,128)(2,1)S(1)} %get-tuple-element.238), channel_id=1, source_target_pairs={{0,4},{4,0},{8,12},{12,8},{16,20},{20,16},{24,28},{28,24},{1,5},{5... | collective-permute-start | bytes 1572872 | tf_op jit(solution)/shard_map/ppermute | solution.py:79
  170.3 24.6 %collective-permute-start.36 = (bf16[64,4096]{1,0:T(8,128)(2,1)S(1)}, bf16[64,4096]{1,0:T(8,128)(2,1)S(1)}, u32[]{:S(2)}, u32[]{:S(2)}) collective-permute-start(bf16[64,4096]{1,0:T(8,128)(2,1)S(1)} %add_convert_fusion.2), channel_id=1, source_target_pairs={{0,3},{1,2},{2,1},{3,0},{4,7},{5,6},{6,5},{7,4},{8,11},{9,10},{10,... | collective-permute-start | bytes 1572872 | tf_op jit(solution)/shard_map/ppermute | solution.py:83
  172.8 12.0 %collective-permute-start.28 = (bf16[48,4096]{1,0:T(8,128)(2,1)S(1)}, bf16[48,4096]{1,0:T(8,128)(2,1)S(1)}, u32[]{:S(2)}, u32[]{:S(2)}) collective-permute-start(bf16[48,4096]{1,0:T(8,128)(2,1)S(1)} %get-tuple-element.228), channel_id=1, source_target_pairs={{0,8},{4,12},{8,0},{12,4},{16,24},{20,28},{24,16},{28,20},{1,9},{5... | collective-permute-start | bytes 1179656 | tf_op jit(solution)/shard_map/ppermute | solution.py:79
  174.3 18.8 %collective-permute-start.29 = (bf16[48,4096]{1,0:T(8,128)(2,1)S(1)}, bf16[48,4096]{1,0:T(8,128)(2,1)S(1)}, u32[]{:S(2)}, u32[]{:S(2)}) collective-permute-start(bf16[48,4096]{1,0:T(8,128)(2,1)S(1)} %get-tuple-element.229), channel_id=1, source_target_pairs={{0,16},{4,20},{8,24},{12,28},{16,0},{20,4},{24,8},{28,12},{1,17},{... | collective-permute-start | bytes 1179656 | tf_op jit(solution)/shard_map/ppermute | solution.py:79
  175.7 17.4 %collective-permute-start.30 = (bf16[48,4096]{1,0:T(8,128)(2,1)S(1)}, bf16[48,4096]{1,0:T(8,128)(2,1)S(1)}, u32[]{:S(2)}, u32[]{:S(2)}) collective-permute-start(bf16[48,4096]{1,0:T(8,128)(2,1)S(1)} %get-tuple-element.230), channel_id=1, source_target_pairs={{0,24},{4,28},{8,16},{12,20},{16,8},{20,12},{24,0},{28,4},{1,25},{... | collective-permute-start | bytes 1179656 | tf_op jit(solution)/shard_map/ppermute | solution.py:79
  194.9 2.0 collective-permute-start.31
  195.1 14.4 %collective-permute-start.37 = (bf16[64,4096]{1,0:T(8,128)(2,1)S(1)}, bf16[64,4096]{1,0:T(8,128)(2,1)S(1)}, u32[]{:S(2)}, u32[]{:S(2)}) collective-permute-start(bf16[64,4096]{1,0:T(8,128)(2,1)S(1)} %add_convert_fusion.1), channel_id=1, source_target_pairs={{0,1},{1,0},{2,3},{3,2},{4,5},{5,4},{6,7},{7,6},{8,9},{9,8},{10,11... | collective-permute-start | bytes 1572872 | tf_op jit(solution)/shard_map/ppermute | solution.py:83

commit v3 on v2

--- a/solution.py
+++ b/solution.py
@@ -11,7 +11,8 @@
 BLK = 128
 BF16 = jnp.bfloat16
 F32 = jnp.float32
-VMEM_LIMIT = 48 * 1024 * 1024
+VMEM_LIMIT = 16 * 1024 * 1024
+EXPERT_VMEM_LIMIT = 28 * 1024 * 1024
 
 
 def slot_numbers(expert_ids, experts):
@@ -143,9 +144,46 @@
     )(ids, near, far)
 
 
+def gather_kernel(width, experts, cap, ids, *refs):
+    blocks, (mine, theirs) = refs[: len(FLIPS) * HALVES], refs[len(FLIPS) * HALVES :]
+    each = HALVES * cap
+    place = lax.broadcasted_iota(jnp.int32, (blocks[0].shape[0], HALVES * each), 1)
+    for n in range(len(FLIPS)):
+        pair = blocks[n * HALVES : (n + 1) * HALVES]
+        parts = []
+        for half, ref in enumerate(pair):
+            meta = ref[:, width:].astype(F32)
+            here = None
+            for which in range(2):
+                rank = column(meta, 3 * experts + ids[which]).astype(jnp.int32)
+                found = place == jnp.where(rank >= 0, rank + which * each + half * cap, -1)
+                here = found if here is None else here | found
+            parts.append(jnp.where(here, 1.0, 0.0))
+        hot = jnp.concatenate(parts, axis=0).astype(BF16)
+        step = 4 * BLK
+        for at in range(0, width, step):
+            cols = slice(at, at + step)
+            block = jnp.concatenate([ref[:, cols] for ref in pair], axis=0)
+            picked = lax.dot_general(hot, block, (((0,), (0,)), ((), ())), preferred_element_type=F32).astype(BF16)
+            mine[n * each : (n + 1) * each, cols] = picked[:each]
+            theirs[n * each : (n + 1) * each, cols] = picked[each:]
+
+
+def gather(ids, blocks, width, experts, cap):
+    shape = jax.ShapeDtypeStruct((len(FLIPS) * HALVES * cap, width), BF16)
+    return pl.pallas_call(
+        functools.partial(gather_kernel, width, experts, cap),
+        out_shape=[shape, shape],
+        in_specs=[pl.BlockSpec(memory_space=pltpu.SMEM)] + [pl.BlockSpec(memory_space=pltpu.VMEM)] * len(blocks),
+        out_specs=[pl.BlockSpec(memory_space=pltpu.VMEM)] * 2,
+        compiler_params=pltpu.CompilerParams(vmem_limit_bytes=VMEM_LIMIT),
+        name="gather_rows",
+    )(ids, *blocks)
+
+
 def combine_kernel(width, experts, cap, ids, near, far, *refs):
     rows, (mine, theirs) = refs[:4], refs[4:]
-    halves = [slots_of(ref[:, width:].astype(F32), half, ids, experts, cap, True) for half, ref in enumerate((near, far))]
+    halves = [slots_of(ref[:, ref.shape[1] - 4 * experts :].astype(F32), half, ids, experts, cap, True) for half, ref in enumerate((near, far))]
     terms = [jnp.concatenate(pair, axis=0).astype(BF16) for pair in zip(*halves)]
     tokens = near.shape[0]
     step = 4 * BLK
@@ -173,7 +211,7 @@
 
 def expert_kernel(count, topo, *refs):
     inputs, (gate, up, down) = refs[:count], refs[count : count + 3]
-    outputs, (x, total) = refs[count + 3 : 2 * count + 3], refs[2 * count + 3 :]
+    outputs, (x, total) = refs[count + 3 : -2], refs[-2:]
     h = pl.program_id(0)
     rows = inputs[0].shape[0]
 
@@ -201,8 +239,9 @@
 
     @pl.when(h == pl.num_programs(0) - 1)
     def _():
+        each = outputs[0].shape[0]
         for n, out in enumerate(outputs):
-            out[...] = total[n * rows : (n + 1) * rows, :].astype(BF16)
+            out[...] = total[n * each : (n + 1) * each, :].astype(BF16)
 
 
 def expert(topo, inputs, weights):
@@ -214,11 +253,11 @@
     return pl.pallas_call(
         functools.partial(expert_kernel, count),
         grid=(blocks // each,),
-        out_shape=[jax.ShapeDtypeStruct((rows, width), BF16)] * count,
+        out_shape=[jax.ShapeDtypeStruct((count * rows // len(FLIPS), width), BF16)] * len(FLIPS),
         in_specs=[pl.BlockSpec(memory_space=pltpu.SMEM)] + [whole] * count + [spec] * 3,
-        out_specs=[whole] * count,
+        out_specs=[pl.BlockSpec((count * rows // len(FLIPS), width), lambda h: (0, 0))] * len(FLIPS),
         scratch_shapes=[pltpu.VMEM((count * rows, width), BF16), pltpu.VMEM((count * rows, width), F32)],
-        compiler_params=pltpu.CompilerParams(vmem_limit_bytes=VMEM_LIMIT),
+        compiler_params=pltpu.CompilerParams(vmem_limit_bytes=EXPERT_VMEM_LIMIT),
         name="expert_rows",
     )(topo, *inputs, *weights)
 
@@ -234,7 +273,8 @@
     high = lax.reduce_precision(weight, 8, 7)
     middle = lax.reduce_precision(weight - high, 8, 7)
     low = weight - high - middle
-    return jnp.concatenate([tokens] + [v.astype(BF16) for v in (high, middle, low, rank)], axis=1)
+    meta = jnp.concatenate([v.astype(BF16) for v in (high, middle, low, rank)], axis=1)
+    return jnp.concatenate([tokens, meta], axis=1), meta
 
 
 def line_device(tokens, expert_ids, combine_weights, topology, gate_blocks, up_blocks, down_blocks):
@@ -254,57 +294,54 @@
         mine, theirs = combine(ids, *pair, rows, width, experts, cap)
         return mine, flip(theirs, CORE)
 
-    own = with_meta(tokens, expert_ids, combine_weights, experts)
-    first, second = along(own, XOR[1]), along(own, XOR[2])
-    pair0, out0 = chosen(own)
-
-    in0 = exchange(out0)
-    in0, (first, second, late) = both(in0, [first, second, own])
-    pair1, out1 = chosen(first)
-
-    in1 = exchange(out1)
-    third = along(late, XOR[3])
+    own, meta = with_meta(tokens, expert_ids, combine_weights, experts)
+    near_ids = jnp.stack([ids[0], ids[0] ^ 1])
+
+    own_far = flip(own, CORE)
+    third = along(own, XOR[3])
+    layer = exchange([own] * 4)
+    layer, (third,) = both(layer, [third])
+
+    pair3, out3 = chosen(third)
+    late, *rest = hold([own] + layer + out3, [])
+    layer, out3 = rest[:4], rest[4:]
+    in3 = exchange(out3)
+    second, first = along(late, XOR[2]), along(meta, XOR[1])
+    halves = [own, own_far] + [half for near in layer[1:] for half in (near, flip(near, CORE))]
+    in0, sent1 = gather(near_ids, halves, width, experts, cap)
+    in3, (second, in0, sent1) = both(in3, [second, in0, sent1])
+
     pair2, out2 = chosen(second)
-    in0, out2 = both(in0, out2)
-    back0 = expert(topo, in0, weights)
-    in1, (third, *rest) = both(in1, [third] + list(out2) + list(back0))
-    out2, back0 = rest[:4], rest[4:]
-
+    sent1, *out2 = hold([sent1] + out2, [])
     in2 = exchange(out2)
-    pair3, out3 = chosen(third)
-    in1, out3 = both(in1, out3)
-    back1 = expert(topo, in1, weights)
-    in2, rest = both(in2, list(out3) + list(back1))
-    out3, back1 = rest[:4], rest[4:]
-
-    in3 = exchange(out3)
+    in1 = along(sent1, XOR[1])
+    pair1 = first, flip(first, CORE)
+    back3 = expert(topo, in3, weights)
+    in2, back3 = both(in2, list(back3))
+
+    got3 = exchange(back3)
     back2 = expert(topo, in2, weights)
-    in3, back2 = both(in3, back2)
+    got3, back2 = both(got3, list(back2))
 
     got2 = exchange(back2)
-    back3 = expert(topo, in3, weights)
-    got2, back3 = both(got2, back3)
-
-    got3 = exchange(back3)
+    back0 = expert(topo, [in0], weights)
+    in1, *back0 = hold([in1] + list(back0), [])
+    back1 = expert(topo, [in1], weights)
+    got2[3], *got3 = hold([got2[3]] + got3, [])
+    mine3, theirs3 = combine(ids, *pair3, got3, width, experts, cap)
+    got2, (mine3, theirs3, *back1) = both(got2, [mine3, theirs3] + list(back1))
+
+    got1 = exchange(back1)
+    far3 = along(add(mine3, flip(theirs3, CORE)), XOR[1])
     mine2, theirs2 = joined(pair2, got2)
-    sum2 = add(mine2, theirs2)
-    got3, back1 = both(got3, back1)
-
-    got1 = exchange(back1)
-    far2 = along(sum2, XOR[2])
-    mine3, theirs3 = joined(pair3, got3)
-    mine3, theirs3, far2 = hold([mine3, theirs3, far2], [])
-    sum3 = add(mine3, theirs3)
-    got1, back0 = both(got1, back0)
+    got1, (far3, mine2, theirs2, *back0) = both(got1, [far3, mine2, theirs2] + back0)
 
     got0 = exchange(back0)
-    far3 = along(sum3, XOR[3])
-    mine1, theirs1 = joined(pair1, got1)
-    mine1, theirs1, far3 = hold([mine1, theirs1, far3], [])
-    sum1 = add(mine1, theirs1)
-    far1 = along(sum1, XOR[1])
-    mine0, theirs0 = joined(pair0, got0)
-    return add(mine0, theirs0, far1, far2, far3)
+    far2 = along(add(mine2, theirs2, far3), XOR[2])
+    far1 = along(add(*joined(pair1, got1)), XOR[1])
+    got0, (far1, far2) = both(got0, [far1, far2])
+    mine0, theirs0 = joined((meta, flip(meta, CORE)), got0)
+    return add(mine0, theirs0, far1, far2)
 
 
 def solution(mesh):

time: 211 us -> 194 us (0.919)
  waiting for transfers between devices: 112 us -> 91.4 us
  local copies, waits for them, and re-layouts: 2.1 us -> 11 us
  Pallas kernels: 50 us -> 44.5 us
    ppermute x6 -> x7, waiting for transfers between devices: 32.3 us -> 15.5 us  [along(): return lax.ppermute(value, 'expert', pairs)]
    unnamed x1 -> x21, local copies, waits for them, and re-layouts: 0.69 us -> 9.62 us
    pallas_call x4, Pallas kernels: 37.9 us -> 31.5 us  [expert(): pl.pallas_call(functools.partial(expert_kernel, count), grid=(blocks // e...]
    ppermute x32 -> x33, waiting for transfers between devices: 79.6 us -> 75.9 us  [flip(): lax.ppermute(value, 'dp', [(i, i ^ bit) for i in range(lax.axis_size('dp'...]
    pallas_call x0 -> x1, Pallas kernels: none -> 2.55 us  [gather(): pl.pallas_call(functools.partial(gather_kernel, width, experts, cap), out...]
    pallas_call x4 -> x2, Pallas kernels: 5.09 us -> 3.52 us  [select(): pl.pallas_call(functools.partial(select_kernel, width, experts, cap), out...]
    ppermute x32 -> x33, starting transfers between devices: 29.5 us -> 28.3 us  [flip(): lax.ppermute(value, 'dp', [(i, i ^ bit) for i in range(lax.axis_size('dp'...]
    ppermute x6 -> x7, starting transfers between devices: 13.7 us -> 14.6 us  [along(): return lax.ppermute(value, 'expert', pairs)]
  transfers between devices with their start and end apart: 38 -> 40, of which waited for: 15 -> 18; matrix products, arithmetic and copies ran while one was open for 1% -> 0% of each run, Pallas kernels for 23% -> 21%
where the time goes in v3:
time: 194 us; the launch traced here: 193 us
  waiting for transfers between devices  91.4 us (47%)
  Pallas kernels  44.5 us (23%)
  starting transfers between devices  42.9 us (22%)
  local copies, waits for them, and re-layouts  11 us (6%)
  other arithmetic  3.18 us (2%)
    ppermute x33, waiting for transfers between devices, flip(): lax.ppermute(value, 'dp', [(i, i ^ bit) for i in range(lax.axis_size('dp'...  75.9 us
    pallas_call x4, Pallas kernels, expert(): pl.pallas_call(functools.partial(expert_kernel, count), grid=(blocks // e...  31.5 us
    ppermute x33, starting transfers between devices, flip(): lax.ppermute(value, 'dp', [(i, i ^ bit) for i in range(lax.axis_size('dp'...  28.3 us
    ppermute x7, waiting for transfers between devices, along(): return lax.ppermute(value, 'expert', pairs)  15.5 us
    ppermute x7, starting transfers between devices, along(): return lax.ppermute(value, 'expert', pairs)  14.6 us
    unnamed x21, local copies, waits for them, and re-layouts  9.62 us
    pallas_call x4, Pallas kernels, combine(): pl.pallas_call(functools.partial(combine_kernel, width, experts, cap), ou...  7.01 us
  transfers between devices with their start and end apart: 40, of which 18 were waited for; matrix products, arithmetic and copies ran while one was open for 0% of the time, Pallas kernels for 21%

profile of v3, /device:TPU:0, one launch (start us, length us, event | category | flops | bytes accessed | tf_op | source)
XLA Modules:
  0.0 193.5 jit_solution(4647602613814775062)
XLA Ops:
  0.0 0.7 select_reduce_fusion
  0.8 0.7 fusion.1
  2.0 1.1 concatenate.8.refs_0_
  3.1 4.0 %collective-permute-start.1 = (bf16[64,4224]{1,0:T(8,128)(2,1)S(1)}, bf16[64,4224]{1,0:T(8,128)(2,1)S(1)}, u32[]{:S(2)}, u32[]{:S(2)}) collective-permute-start(bf16[64,4224]{1,0:T(8,128)(2,1)S(1)} %concatenate.8.refs_0_), channel_id=1, source_target_pairs={{0,24},{4,28},{8,16},{12,20},{16,8},{20,12},{24,0},{28,4},{1,25},{... | collective-permute-start | bytes 1622024 | tf_op jit(solution)/shard_map/ppermute | solution.py:80
  7.1 0.5 collective-permute-start.2
  7.7 4.0 %collective-permute-start.4 = (bf16[64,4224]{1,0:T(8,128)(2,1)S(1)}, bf16[64,4224]{1,0:T(8,128)(2,1)S(1)}, u32[]{:S(2)}, u32[]{:S(2)}) collective-permute-start(bf16[64,4224]{1,0:T(8,128)(2,1)S(1)} %concatenate.8.refs_0_), channel_id=1, source_target_pairs={{0,3},{1,2},{2,1},{3,0},{4,7},{5,6},{6,5},{7,4},{8,11},{9,10},{10,... | collective-permute-start | bytes 1622024 | tf_op jit(solution)/shard_map/ppermute | solution.py:84
  11.7 8.5 %collective-permute-done.1.refs_6_ = bf16[64,4224]{1,0:T(8,128)(2,1)S(1)} collective-permute-done((bf16[64,4224]{1,0:T(8,128)(2,1)S(1)}, bf16[64,4224]{1,0:T(8,128)(2,1)S(1)}, u32[]{:S(2)}, u32[]{:S(2)}) %collective-permute-start.1) | collective-permute-done | bytes 540704 | tf_op jit(solution)/shard_map/ppermute | solution.py:80
  20.2 11.0 %collective-permute-done.2.refs_2_ = bf16[64,4224]{1,0:T(8,128)(2,1)S(1)} collective-permute-done((bf16[64,4224]{1,0:T(8,128)(2,1)S(1)}, bf16[64,4224]{1,0:T(8,128)(2,1)S(1)}, u32[]{:S(2)}, u32[]{:S(2)}) %collective-permute-start.2) | collective-permute-done | bytes 540704 | tf_op jit(solution)/shard_map/ppermute | solution.py:80
  31.8 1.4 collective-permute-done.5.far
  33.2 2.2 %select_rows.2 = (bf16[48,4096]{1,0:T(8,128)(2,1)S(1)}, bf16[48,4096]{1,0:T(8,128)(2,1)}, bf16[48,4096]{1,0:T(8,128)(2,1)}, bf16[48,4096]{1,0:T(8,128)(2,1)}) custom-call(s32[4]{0:T(128)S(1)} %pad_add_fusion.ids, bf16[64,4224]{1,0:T(8,128)(2,1)S(1)} %collective-permute-done.4.near, bf16[64,4224]{1,0:T(8,128)(2,1)S(1)} %collective-permute-done.5.far), custom_call_target="tpu_custom_call" | custom-call | tf_op jit(solution)/shard_map/select_rows/pallas_call | solution.py:137
  35.5 0.8 copy-done.7
  36.9 4.9 %collective-permute-start.9 = (bf16[64,4224]{1,0:T(8,128)(2,1)S(1)}, bf16[64,4224]{1,0:T(8,128)(2,1)S(1)}, u32[]{:S(2)}, u32[]{:S(2)}) collective-permute-start(bf16[64,4224]{1,0:T(8,128)(2,1)S(1)} %concatenate.8.refs_0_), channel_id=1, source_target_pairs={{0,2},{1,3},{2,0},{3,1},{4,6},{5,7},{6,4},{7,5},{8,10},{9,11},{10,... | collective-permute-start | bytes 1622024 | tf_op jit(solution)/shard_map/ppermute | solution.py:84
  41.8 2.4 %collective-permute-start.6 = (bf16[48,4096]{1,0:T(8,128)(2,1)}, bf16[48,4096]{1,0:T(8,128)(2,1)}, u32[]{:S(2)}, u32[]{:S(2)}) collective-permute-start(bf16[48,4096]{1,0:T(8,128)(2,1)} %get-tuple-element.124), channel_id=1, source_target_pairs={{0,24},{4,28},{8,16},{12,20},{16,8},{20,12},{24,0},{28,4},{1,25},{... | collective-permute-start | bytes 1179656 | tf_op jit(solution)/shard_map/ppermute | solution.py:80
  44.3 0.8 copy-done.3
  45.1 0.5 collective-permute-start.7
  45.6 0.8 copy-done.5
  47.0 1.2 copy-done.4
  48.2 1.3 copy-done.6
  49.6 2.6 %gather_rows.1 = (bf16[192,4096]{1,0:T(8,128)(2,1)S(1)}, bf16[192,4096]{1,0:T(8,128)(2,1)S(1)}) custom-call(s32[2]{0:T(128)S(1)} %pad_add_fusion.1.ids, bf16[64,4224]{1,0:T(8,128)(2,1)S(1)} %concatenate.8.refs_0_, bf16[64,4224]{1,0:T(8,128)(2,1)} %collective-permute-done.10.refs_1_, bf16[64,4224]{1,0:T(8,128)(2,1)S(1)} %collective-permute-done.2.refs_2_, ...), custom_call_target="tpu_custom_call" | custom-call | tf_op jit(solution)/shard_map/gather_rows/pallas_call | solution.py:174
  52.1 2.9 %collective-permute-done.6.refs_3_ = bf16[48,4096]{1,0:T(8,128)(2,1)} collective-permute-done((bf16[48,4096]{1,0:T(8,128)(2,1)}, bf16[48,4096]{1,0:T(8,128)(2,1)}, u32[]{:S(2)}, u32[]{:S(2)}) %collective-permute-start.6) | collective-permute-done | bytes 393248 | tf_op jit(solution)/shard_map/ppermute | solution.py:80
  55.1 7.6 %collective-permute-done.7.refs_1_ = bf16[48,4096]{1,0:T(8,128)(2,1)} collective-permute-done((bf16[48,4096]{1,0:T(8,128)(2,1)}, bf16[48,4096]{1,0:T(8,128)(2,1)}, u32[]{:S(2)}, u32[]{:S(2)}) %collective-permute-start.7) | collective-permute-done | bytes 393248 | tf_op jit(solution)/shard_map/ppermute | solution.py:80
  62.7 3.5 %collective-permute-done.9.near = bf16[64,4224]{1,0:T(8,128)(2,1)S(1)} collective-permute-done((bf16[64,4224]{1,0:T(8,128)(2,1)S(1)}, bf16[64,4224]{1,0:T(8,128)(2,1)S(1)}, u32[]{:S(2)}, u32[]{:S(2)}) %collective-permute-start.9) | collective-permute-done | bytes 540704 | tf_op jit(solution)/shard_map/ppermute | solution.py:84
  66.2 1.9 collective-permute-done.14.far
  68.1 1.3 select_rows.3
  69.5 2.5 %collective-permute-start.15 = (bf16[48,4096]{1,0:T(8,128)(2,1)S(1)}, bf16[48,4096]{1,0:T(8,128)(2,1)S(1)}, u32[]{:S(2)}, u32[]{:S(2)}) collective-permute-start(bf16[48,4096]{1,0:T(8,128)(2,1)S(1)} %get-tuple-element.140), channel_id=1, source_target_pairs={{0,24},{4,28},{8,16},{12,20},{16,8},{20,12},{24,0},{28,4},{1,25},{... | collective-permute-start | bytes 1179656 | tf_op jit(solution)/shard_map/ppermute | solution.py:80
  72.0 0.5 collective-permute-start.16
  73.1 2.3 %copy-done.1 = bf16[1,12,12,128,128]{4,3,2,1,0:T(8,128)(2,1)S(1)} copy-done((bf16[1,12,12,128,128]{4,3,2,1,0:T(8,128)(2,1)S(1)}, bf16[1,12,12,128,128]{4,3,2,1,0:T(8,128)(2,1)}, u32[]{:S(2)}) %copy-start.1) | copy-done | bytes 4718616
  75.4 2.3 %copy-done.2 = bf16[1,12,12,128,128]{4,3,2,1,0:T(8,128)(2,1)S(1)} copy-done((bf16[1,12,12,128,128]{4,3,2,1,0:T(8,128)(2,1)S(1)}, bf16[1,12,12,128,128]{4,3,2,1,0:T(8,128)(2,1)}, u32[]{:S(2)}) %copy-start.2) | copy-done | bytes 4718616
  77.7 8.3 %expert_rows.4 = (bf16[48,4096]{1,0:T(8,128)(2,1)S(1)}, bf16[48,4096]{1,0:T(8,128)(2,1)S(1)}, bf16[48,4096]{1,0:T(8,128)(2,1)S(1)}, bf16[48,4096]{1,0:T(8,128)(2,1)S(1)}) custom-call(s32[12,12]{1,0:T(8,128)S(1)} %bitcast.9, bf16[48,4096]{1,0:T(8,128)(2,1)S(1)} %copy-done.8, bf16[48,4096]{1,0:T(8,128)(2,1)} %collective-permute-done.7.refs_1_, ...), custom_call_target="tpu_custom_call" | custom-call | tf_op jit(solution)/shard_map/expert_rows/pallas_call | solution.py:253
  86.0 4.1 %collective-permute-done.16.refs_1_ = bf16[48,4096]{1,0:T(8,128)(2,1)S(1)} collective-permute-done((bf16[48,4096]{1,0:T(8,128)(2,1)S(1)}, bf16[48,4096]{1,0:T(8,128)(2,1)S(1)}, u32[]{:S(2)}, u32[]{:S(2)}) %collective-permute-start.16) | collective-permute-done | bytes 393248 | tf_op jit(solution)/shard_map/ppermute | solution.py:80
  90.1 2.3 %collective-permute-start.18 = (bf16[48,4096]{1,0:T(8,128)(2,1)S(1)}, bf16[48,4096]{1,0:T(8,128)(2,1)S(1)}, u32[]{:S(2)}, u32[]{:S(2)}) collective-permute-start(bf16[48,4096]{1,0:T(8,128)(2,1)S(1)} %get-tuple-element.152), channel_id=1, source_target_pairs={{0,24},{4,28},{8,16},{12,20},{16,8},{20,12},{24,0},{28,4},{1,25},{... | collective-permute-start | bytes 1179656 | tf_op jit(solution)/shard_map/ppermute | solution.py:80
  92.5 0.5 collective-permute-start.19
  93.0 0.6 collective-permute-start.20
  93.6 7.7 %expert_rows.5 = (bf16[48,4096]{1,0:T(8,128)(2,1)S(1)}, bf16[48,4096]{1,0:T(8,128)(2,1)S(1)}, bf16[48,4096]{1,0:T(8,128)(2,1)S(1)}, bf16[48,4096]{1,0:T(8,128)(2,1)S(1)}) custom-call(s32[12,12]{1,0:T(8,128)S(1)} %bitcast.10, bf16[48,4096]{1,0:T(8,128)(2,1)S(1)} %get-tuple-element.156.refs_0_, bf16[48,4096]{1,0:T(8,128)(2,1)S(1)} %collective-permute-done.16.refs_1_, ...), custom_call_target="tpu_custom_call" | custom-call | tf_op jit(solution)/shard_map/expert_rows/pallas_call | solution.py:253
  101.3 1.8 collective-permute-done.18.refs_3_
  103.1 7.4 %collective-permute-done.19.refs_1_ = bf16[48,4096]{1,0:T(8,128)(2,1)S(1)} collective-permute-done((bf16[48,4096]{1,0:T(8,128)(2,1)S(1)}, bf16[48,4096]{1,0:T(8,128)(2,1)S(1)}, u32[]{:S(2)}, u32[]{:S(2)}) %collective-permute-start.19) | collective-permute-done | bytes 393248 | tf_op jit(solution)/shard_map/ppermute | solution.py:80
  110.5 2.3 %collective-permute-start.21 = (bf16[48,4096]{1,0:T(8,128)(2,1)S(1)}, bf16[48,4096]{1,0:T(8,128)(2,1)S(1)}, u32[]{:S(2)}, u32[]{:S(2)}) collective-permute-start(bf16[48,4096]{1,0:T(8,128)(2,1)S(1)} %get-tuple-element.164), channel_id=1, source_target_pairs={{0,24},{4,28},{8,16},{12,20},{16,8},{20,12},{24,0},{28,4},{1,25},{... | collective-permute-start | bytes 1179656 | tf_op jit(solution)/shard_map/ppermute | solution.py:80
  112.9 0.5 collective-permute-start.22
  113.4 0.6 collective-permute-start.23
  114.0 7.7 %expert_rows.6 = (bf16[48,4096]{1,0:T(8,128)(2,1)S(1)}, bf16[48,4096]{1,0:T(8,128)(2,1)S(1)}, bf16[48,4096]{1,0:T(8,128)(2,1)S(1)}, bf16[48,4096]{1,0:T(8,128)(2,1)S(1)}) custom-call(s32[12,12]{1,0:T(8,128)S(1)} %bitcast.11, bf16[192,4096]{1,0:T(8,128)(2,1)S(1)} %get-tuple-element.180.refs_0_, bf16[1,12,12,128,128]{4,3,2,1,0:T(8,128)(2,1)S(1)} %copy-done, ...), custom_call_target="tpu_custom_call" | custom-call | tf_op jit(solution)/shard_map/expert_rows/pallas_call | solution.py:253
  121.7 1.8 collective-permute-done.21.refs_3_
  123.4 1.8 combine_rows.4
  125.2 7.9 %expert_rows.7 = (bf16[48,4096]{1,0:T(8,128)(2,1)S(1)}, bf16[48,4096]{1,0:T(8,128)(2,1)S(1)}, bf16[48,4096]{1,0:T(8,128)(2,1)S(1)}, bf16[48,4096]{1,0:T(8,128)(2,1)S(1)}) custom-call(s32[12,12]{1,0:T(8,128)S(1)} %bitcast.12, bf16[192,4096]{1,0:T(8,128)(2,1)S(1)} %collective-permute-done.24.refs_0_, bf16[1,12,12,128,128]{4,3,2,1,0:T(8,128)(2,1)S(1)} %copy-done, ...), custom_call_target="tpu_custom_call" | custom-call | tf_op jit(solution)/shard_map/expert_rows/pallas_call | solution.py:253
  133.2 1.8 combine_rows.5
  135.0 0.6 collective-permute-start.30
  135.6 1.7 collective-permute-start.29
  137.9 2.3 %collective-permute-start.25 = (bf16[48,4096]{1,0:T(8,128)(2,1)S(1)}, bf16[48,4096]{1,0:T(8,128)(2,1)S(1)}, u32[]{:S(2)}, u32[]{:S(2)}) collective-permute-start(bf16[48,4096]{1,0:T(8,128)(2,1)S(1)} %get-tuple-element.190), channel_id=1, source_target_pairs={{0,24},{4,28},{8,16},{12,20},{16,8},{20,12},{24,0},{28,4},{1,25},{... | collective-permute-start | bytes 1179656 | tf_op jit(solution)/shard_map/ppermute | solution.py:80
  140.2 0.6 collective-permute-start.26
  140.8 9.2 %collective-permute-done.34.near = bf16[64,128]{1,0:T(8,128)(2,1)S(1)} collective-permute-done((bf16[64,128]{1,0:T(8,128)(2,1)S(1)}, bf16[64,128]{1,0:T(8,128)(2,1)S(1)}, u32[]{:S(2)}, u32[]{:S(2)}) %collective-permute-start.34) | collective-permute-done | bytes 16416 | tf_op jit(solution)/shard_map/ppermute | solution.py:84
  149.9 1.4 collective-permute-start.27
  151.3 6.3 %collective-permute-done.26.refs_1_ = bf16[48,4096]{1,0:T(8,128)(2,1)S(1)} collective-permute-done((bf16[48,4096]{1,0:T(8,128)(2,1)S(1)}, bf16[48,4096]{1,0:T(8,128)(2,1)S(1)}, u32[]{:S(2)}, u32[]{:S(2)}) %collective-permute-start.26) | collective-permute-done | bytes 393248 | tf_op jit(solution)/shard_map/ppermute | solution.py:80
  157.6 2.5 %collective-permute-done.27.refs_2_ = bf16[48,4096]{1,0:T(8,128)(2,1)S(1)} collective-permute-done((bf16[48,4096]{1,0:T(8,128)(2,1)S(1)}, bf16[48,4096]{1,0:T(8,128)(2,1)S(1)}, u32[]{:S(2)}, u32[]{:S(2)}) %collective-permute-start.27) | collective-permute-done | bytes 393248 | tf_op jit(solution)/shard_map/ppermute | solution.py:80
  160.1 1.8 combine_rows.6
  162.1 2.2 %collective-permute-start.38 = (bf16[64,4096]{1,0:T(8,128)(2,1)S(1)}, bf16[64,4096]{1,0:T(8,128)(2,1)S(1)}, u32[]{:S(2)}, u32[]{:S(2)}) collective-permute-start(bf16[64,4096]{1,0:T(8,128)(2,1)S(1)} %add_convert_fusion.1), channel_id=1, source_target_pairs={{0,2},{1,3},{2,0},{3,1},{4,6},{5,7},{6,4},{7,5},{8,10},{9,11},{10,... | collective-permute-start | bytes 1572872 | tf_op jit(solution)/shard_map/ppermute | solution.py:84
  164.4 1.3 collective-permute-start.37
  165.7 2.4 %collective-permute-start.31 = (bf16[48,4096]{1,0:T(8,128)(2,1)S(1)}, bf16[48,4096]{1,0:T(8,128)(2,1)S(1)}, u32[]{:S(2)}, u32[]{:S(2)}) collective-permute-start(bf16[48,4096]{1,0:T(8,128)(2,1)S(1)} %get-tuple-element.206), channel_id=1, source_target_pairs={{0,24},{4,28},{8,16},{12,20},{16,8},{20,12},{24,0},{28,4},{1,25},{... | collective-permute-start | bytes 1179656 | tf_op jit(solution)/shard_map/ppermute | solution.py:80
  168.0 0.5 collective-permute-start.32
  168.6 0.6 collective-permute-start.33
  169.2 9.5 %collective-permute-done.31.refs_3_ = bf16[48,4096]{1,0:T(8,128)(2,1)S(1)} collective-permute-done((bf16[48,4096]{1,0:T(8,128)(2,1)S(1)}, bf16[48,4096]{1,0:T(8,128)(2,1)S(1)}, u32[]{:S(2)}, u32[]{:S(2)}) %collective-permute-start.31) | collective-permute-done | bytes 393248 | tf_op jit(solution)/shard_map/ppermute | solution.py:80
  178.6 7.3 %collective-permute-done.32.refs_1_ = bf16[48,4096]{1,0:T(8,128)(2,1)S(1)} collective-permute-done((bf16[48,4096]{1,0:T(8,128)(2,1)S(1)}, bf16[48,4096]{1,0:T(8,128)(2,1)S(1)}, u32[]{:S(2)}, u32[]{:S(2)}) %collective-permute-start.32) | collective-permute-done | bytes 393248 | tf_op jit(solution)/shard_map/ppermute | solution.py:80
  185.9 2.8 %collective-permute-done.38 = bf16[64,4096]{1,0:T(8,128)(2,1)S(1)} collective-permute-done((bf16[64,4096]{1,0:T(8,128)(2,1)S(1)}, bf16[64,4096]{1,0:T(8,128)(2,1)S(1)}, u32[]{:S(2)}, u32[]{:S(2)}) %collective-permute-start.38) | collective-permute-done | bytes 524320 | tf_op jit(solution)/shard_map/ppermute | solution.py:84
  188.7 1.8 combine_rows.7
  190.5 1.9 collective-permute-done.39
  192.4 1.1 add_convert_fusion
  (65 shorter events, 4.2 us)
Async XLA Ops:
  0.0 73.1 %copy-start.9 = (s32[1,12,12]{2,0,1:T(1,128)S(1)}, s32[1,12,12]{2,0,1:T(1,128)}, u32[]{:S(2)}) copy-start(s32[1,12,12]{2,0,1:T(1,128)} %param.10) | copy-start | bytes 1732
  3.1 17.1 %collective-permute-start.1 = (bf16[64,4224]{1,0:T(8,128)(2,1)S(1)}, bf16[64,4224]{1,0:T(8,128)(2,1)S(1)}, u32[]{:S(2)}, u32[]{:S(2)}) collective-permute-start(bf16[64,4224]{1,0:T(8,128)(2,1)S(1)} %concatenate.8.refs_0_), channel_id=1, source_target_pairs={{0,24},{4,28},{8,16},{12,20},{16,8},{20,12},{24,0},{28,4},{1,25},{... | collective-permute-start | bytes 1622024 | tf_op jit(solution)/shard_map/ppermute | solution.py:80
  7.1 24.2 %collective-permute-start.2 = (bf16[64,4224]{1,0:T(8,128)(2,1)S(1)}, bf16[64,4224]{1,0:T(8,128)(2,1)S(1)}, u32[]{:S(2)}, u32[]{:S(2)}) collective-permute-start(bf16[64,4224]{1,0:T(8,128)(2,1)S(1)} %concatenate.8.refs_0_), channel_id=1, source_target_pairs={{0,8},{4,12},{8,0},{12,4},{16,24},{20,28},{24,16},{28,20},{1,9},{5... | collective-permute-start | bytes 1622024 | tf_op jit(solution)/shard_map/ppermute | solution.py:80
  7.6 23.6 %collective-permute-start.3 = (bf16[64,4224]{1,0:T(8,128)(2,1)S(1)}, bf16[64,4224]{1,0:T(8,128)(2,1)}, u32[]{:S(2)}, u32[]{:S(2)}) collective-permute-start(bf16[64,4224]{1,0:T(8,128)(2,1)S(1)} %concatenate.8.refs_0_), channel_id=1, source_target_pairs={{0,16},{4,20},{8,24},{12,28},{16,0},{20,4},{24,8},{28,12},{1,17},{... | collective-permute-start | bytes 1622024 | tf_op jit(solution)/shard_map/ppermute | solution.py:80
  7.7 23.5 %collective-permute-start.4 = (bf16[64,4224]{1,0:T(8,128)(2,1)S(1)}, bf16[64,4224]{1,0:T(8,128)(2,1)S(1)}, u32[]{:S(2)}, u32[]{:S(2)}) collective-permute-start(bf16[64,4224]{1,0:T(8,128)(2,1)S(1)} %concatenate.8.refs_0_), channel_id=1, source_target_pairs={{0,3},{1,2},{2,1},{3,0},{4,7},{5,6},{6,5},{7,4},{8,11},{9,10},{10,... | collective-permute-start | bytes 1622024 | tf_op jit(solution)/shard_map/ppermute | solution.py:84
  31.2 2.0 %collective-permute-start.5 = (bf16[64,4224]{1,0:T(8,128)(2,1)S(1)}, bf16[64,4224]{1,0:T(8,128)(2,1)S(1)}, u32[]{:S(2)}, u32[]{:S(2)}) collective-permute-start(bf16[64,4224]{1,0:T(8,128)(2,1)S(1)} %collective-permute-done.4.near), channel_id=1, source_target_pairs={{0,4},{4,0},{8,12},{12,8},{16,20},{20,16},{24,28},{28,24},{1,5},{5... | collective-permute-start | bytes 1622024 | tf_op jit(solution)/shard_map/ppermute | solution.py:80
  31.2 10.6 %collective-permute-start.10 = (bf16[64,4224]{1,0:T(8,128)(2,1)S(1)}, bf16[64,4224]{1,0:T(8,128)(2,1)}, u32[]{:S(2)}, u32[]{:S(2)}) collective-permute-start(bf16[64,4224]{1,0:T(8,128)(2,1)S(1)} %concatenate.8.refs_0_), channel_id=1, source_target_pairs={{0,4},{4,0},{8,12},{12,8},{16,20},{20,16},{24,28},{28,24},{1,5},{5... | collective-permute-start | bytes 1622024 | tf_op jit(solution)/shard_map/ppermute | solution.py:80
  35.5 0.8 copy-start.7
  36.2 8.0 %collective-permute-start.11 = (bf16[64,4224]{1,0:T(8,128)(2,1)S(1)}, bf16[64,4224]{1,0:T(8,128)(2,1)S(1)}, u32[]{:S(2)}, u32[]{:S(2)}) collective-permute-start(bf16[64,4224]{1,0:T(8,128)(2,1)S(1)} %collective-permute-done.2.refs_2_), channel_id=1, source_target_pairs={{0,4},{4,0},{8,12},{12,8},{16,20},{20,16},{24,28},{28,24},{1,5},{5... | collective-permute-start | bytes 1622024 | tf_op jit(solution)/shard_map/ppermute | solution.py:80
  36.4 9.3 %collective-permute-start.12 = (bf16[64,4224]{1,0:T(8,128)(2,1)}, bf16[64,4224]{1,0:T(8,128)(2,1)S(1)}, u32[]{:S(2)}, u32[]{:S(2)}) collective-permute-start(bf16[64,4224]{1,0:T(8,128)(2,1)} %collective-permute-done.3.refs_4_), channel_id=1, source_target_pairs={{0,4},{4,0},{8,12},{12,8},{16,20},{20,16},{24,28},{28,24},{1,5},{5... | collective-permute-start | bytes 1622024 | tf_op jit(solution)/shard_map/ppermute | solution.py:80
  36.7 10.3 %collective-permute-start.13 = (bf16[64,4224]{1,0:T(8,128)(2,1)S(1)}, bf16[64,4224]{1,0:T(8,128)(2,1)}, u32[]{:S(2)}, u32[]{:S(2)}) collective-permute-start(bf16[64,4224]{1,0:T(8,128)(2,1)S(1)} %collective-permute-done.1.refs_6_), channel_id=1, source_target_pairs={{0,4},{4,0},{8,12},{12,8},{16,20},{20,16},{24,28},{28,24},{1,5},{5... | collective-permute-start | bytes 1622024 | tf_op jit(solution)/shard_map/ppermute | solution.py:80
  36.9 29.3 %collective-permute-start.9 = (bf16[64,4224]{1,0:T(8,128)(2,1)S(1)}, bf16[64,4224]{1,0:T(8,128)(2,1)S(1)}, u32[]{:S(2)}, u32[]{:S(2)}) collective-permute-start(bf16[64,4224]{1,0:T(8,128)(2,1)S(1)} %concatenate.8.refs_0_), channel_id=1, source_target_pairs={{0,2},{1,3},{2,0},{3,1},{4,6},{5,7},{6,4},{7,5},{8,10},{9,11},{10,... | collective-permute-start | bytes 1622024 | tf_op jit(solution)/shard_map/ppermute | solution.py:84
  41.8 13.2 %collective-permute-start.6 = (bf16[48,4096]{1,0:T(8,128)(2,1)}, bf16[48,4096]{1,0:T(8,128)(2,1)}, u32[]{:S(2)}, u32[]{:S(2)}) collective-permute-start(bf16[48,4096]{1,0:T(8,128)(2,1)} %get-tuple-element.124), channel_id=1, source_target_pairs={{0,24},{4,28},{8,16},{12,20},{16,8},{20,12},{24,0},{28,4},{1,25},{... | collective-permute-start | bytes 1179656 | tf_op jit(solution)/shard_map/ppermute | solution.py:80
  44.3 0.8 copy-start.3
  45.1 17.6 %collective-permute-start.7 = (bf16[48,4096]{1,0:T(8,128)(2,1)}, bf16[48,4096]{1,0:T(8,128)(2,1)}, u32[]{:S(2)}, u32[]{:S(2)}) collective-permute-start(bf16[48,4096]{1,0:T(8,128)(2,1)} %get-tuple-element.125), channel_id=1, source_target_pairs={{0,8},{4,12},{8,0},{12,4},{16,24},{20,28},{24,16},{28,20},{1,9},{5... | collective-permute-start | bytes 1179656 | tf_op jit(solution)/shard_map/ppermute | solution.py:80
  45.6 0.8 copy-start.5
  46.4 16.2 %collective-permute-start.8 = (bf16[48,4096]{1,0:T(8,128)(2,1)}, bf16[48,4096]{1,0:T(8,128)(2,1)}, u32[]{:S(2)}, u32[]{:S(2)}) collective-permute-start(bf16[48,4096]{1,0:T(8,128)(2,1)} %get-tuple-element.126), channel_id=1, source_target_pairs={{0,16},{4,20},{8,24},{12,28},{16,0},{20,4},{24,8},{28,12},{1,17},{... | collective-permute-start | bytes 1179656 | tf_op jit(solution)/shard_map/ppermute | solution.py:80
  46.9 26.1 %copy-start = (bf16[1,12,12,128,128]{4,3,2,1,0:T(8,128)(2,1)S(1)}, bf16[1,12,12,128,128]{4,3,2,1,0:T(8,128)(2,1)}, u32[]{:S(2)}) copy-start(bf16[1,12,12,128,128]{4,3,2,1,0:T(8,128)(2,1)} %refs_1_.3) | copy-start | bytes 14155780
  47.0 1.2 copy-start.4
  48.2 1.3 copy-start.6
  49.6 23.5 %copy-start.8 = (bf16[48,4096]{1,0:T(8,128)(2,1)S(1)}, bf16[48,4096]{1,0:T(8,128)(2,1)}, u32[]{:S(2)}) copy-start(bf16[48,4096]{1,0:T(8,128)(2,1)} %copy-done.7) | copy-start | bytes 1179652
  66.2 1.9 collective-permute-start.14
  69.4 55.8 %collective-permute-start.24 = (bf16[192,4096]{1,0:T(8,128)(2,1)S(1)}, bf16[192,4096]{1,0:T(8,128)(2,1)S(1)}, u32[]{:S(2)}, u32[]{:S(2)}) collective-permute-start(bf16[192,4096]{1,0:T(8,128)(2,1)S(1)} %get-tuple-element.179), channel_id=1, source_target_pairs={{0,1},{1,0},{2,3},{3,2},{4,5},{5,4},{6,7},{7,6},{8,9},{9,8},{10,11... | collective-permute-start | bytes 4718600 | tf_op jit(solution)/shard_map/ppermute | solution.py:84
  69.5 16.5 %collective-permute-start.15 = (bf16[48,4096]{1,0:T(8,128)(2,1)S(1)}, bf16[48,4096]{1,0:T(8,128)(2,1)S(1)}, u32[]{:S(2)}, u32[]{:S(2)}) collective-permute-start(bf16[48,4096]{1,0:T(8,128)(2,1)S(1)} %get-tuple-element.140), channel_id=1, source_target_pairs={{0,24},{4,28},{8,16},{12,20},{16,8},{20,12},{24,0},{28,4},{1,25},{... | collective-permute-start | bytes 1179656 | tf_op jit(solution)/shard_map/ppermute | solution.py:80
  72.0 18.1 %collective-permute-start.16 = (bf16[48,4096]{1,0:T(8,128)(2,1)S(1)}, bf16[48,4096]{1,0:T(8,128)(2,1)S(1)}, u32[]{:S(2)}, u32[]{:S(2)}) collective-permute-start(bf16[48,4096]{1,0:T(8,128)(2,1)S(1)} %get-tuple-element.141), channel_id=1, source_target_pairs={{0,8},{4,12},{8,0},{12,4},{16,24},{20,28},{24,16},{28,20},{1,9},{5... | collective-permute-start | bytes 1179656 | tf_op jit(solution)/shard_map/ppermute | solution.py:80
  72.5 17.6 %collective-permute-start.17 = (bf16[48,4096]{1,0:T(8,128)(2,1)S(1)}, bf16[48,4096]{1,0:T(8,128)(2,1)S(1)}, u32[]{:S(2)}, u32[]{:S(2)}) collective-permute-start(bf16[48,4096]{1,0:T(8,128)(2,1)S(1)} %get-tuple-element.142), channel_id=1, source_target_pairs={{0,16},{4,20},{8,24},{12,28},{16,0},{20,4},{24,8},{28,12},{1,17},{... | collective-permute-start | bytes 1179656 | tf_op jit(solution)/shard_map/ppermute | solution.py:80
  73.1 2.3 %copy-start.1 = (bf16[1,12,12,128,128]{4,3,2,1,0:T(8,128)(2,1)S(1)}, bf16[1,12,12,128,128]{4,3,2,1,0:T(8,128)(2,1)}, u32[]{:S(2)}) copy-start(bf16[1,12,12,128,128]{4,3,2,1,0:T(8,128)(2,1)} %refs_2_.3) | copy-start | bytes 14155780
  75.4 2.3 %copy-start.2 = (bf16[1,12,12,128,128]{4,3,2,1,0:T(8,128)(2,1)S(1)}, bf16[1,12,12,128,128]{4,3,2,1,0:T(8,128)(2,1)}, u32[]{:S(2)}) copy-start(bf16[1,12,12,128,128]{4,3,2,1,0:T(8,128)(2,1)} %refs_3_.3) | copy-start | bytes 14155780
  90.1 12.9 %collective-permute-start.18 = (bf16[48,4096]{1,0:T(8,128)(2,1)S(1)}, bf16[48,4096]{1,0:T(8,128)(2,1)S(1)}, u32[]{:S(2)}, u32[]{:S(2)}) collective-permute-start(bf16[48,4096]{1,0:T(8,128)(2,1)S(1)} %get-tuple-element.152), channel_id=1, source_target_pairs={{0,24},{4,28},{8,16},{12,20},{16,8},{20,12},{24,0},{28,4},{1,25},{... | collective-permute-start | bytes 1179656 | tf_op jit(solution)/shard_map/ppermute | solution.py:80
  92.5 18.0 %collective-permute-start.19 = (bf16[48,4096]{1,0:T(8,128)(2,1)S(1)}, bf16[48,4096]{1,0:T(8,128)(2,1)S(1)}, u32[]{:S(2)}, u32[]{:S(2)}) collective-permute-start(bf16[48,4096]{1,0:T(8,128)(2,1)S(1)} %get-tuple-element.153), channel_id=1, source_target_pairs={{0,8},{4,12},{8,0},{12,4},{16,24},{20,28},{24,16},{28,20},{1,9},{5... | collective-permute-start | bytes 1179656 | tf_op jit(solution)/shard_map/ppermute | solution.py:80
  93.0 17.5 %collective-permute-start.20 = (bf16[48,4096]{1,0:T(8,128)(2,1)S(1)}, bf16[48,4096]{1,0:T(8,128)(2,1)S(1)}, u32[]{:S(2)}, u32[]{:S(2)}) collective-permute-start(bf16[48,4096]{1,0:T(8,128)(2,1)S(1)} %get-tuple-element.154), channel_id=1, source_target_pairs={{0,16},{4,20},{8,24},{12,28},{16,0},{20,4},{24,8},{28,12},{1,17},{... | collective-permute-start | bytes 1179656 | tf_op jit(solution)/shard_map/ppermute | solution.py:80
  110.5 12.9 %collective-permute-start.21 = (bf16[48,4096]{1,0:T(8,128)(2,1)S(1)}, bf16[48,4096]{1,0:T(8,128)(2,1)S(1)}, u32[]{:S(2)}, u32[]{:S(2)}) collective-permute-start(bf16[48,4096]{1,0:T(8,128)(2,1)S(1)} %get-tuple-element.164), channel_id=1, source_target_pairs={{0,24},{4,28},{8,16},{12,20},{16,8},{20,12},{24,0},{28,4},{1,25},{... | collective-permute-start | bytes 1179656 | tf_op jit(solution)/shard_map/ppermute | solution.py:80
  112.9 20.2 %collective-permute-start.22 = (bf16[48,4096]{1,0:T(8,128)(2,1)S(1)}, bf16[48,4096]{1,0:T(8,128)(2,1)S(1)}, u32[]{:S(2)}, u32[]{:S(2)}) collective-permute-start(bf16[48,4096]{1,0:T(8,128)(2,1)S(1)} %get-tuple-element.170), channel_id=1, source_target_pairs={{0,8},{4,12},{8,0},{12,4},{16,24},{20,28},{24,16},{28,20},{1,9},{5... | collective-permute-start | bytes 1179656 | tf_op jit(solution)/shard_map/ppermute | solution.py:80
  113.4 19.7 %collective-permute-start.23 = (bf16[48,4096]{1,0:T(8,128)(2,1)S(1)}, bf16[48,4096]{1,0:T(8,128)(2,1)S(1)}, u32[]{:S(2)}, u32[]{:S(2)}) collective-permute-start(bf16[48,4096]{1,0:T(8,128)(2,1)S(1)} %get-tuple-element.171), channel_id=1, source_target_pairs={{0,16},{4,20},{8,24},{12,28},{16,0},{20,4},{24,8},{28,12},{1,17},{... | collective-permute-start | bytes 1179656 | tf_op jit(solution)/shard_map/ppermute | solution.py:80
  133.1 2.4 %collective-permute-start.28 = (bf16[64,4096]{1,0:T(8,128)(2,1)S(1)}, bf16[64,4096]{1,0:T(8,128)(2,1)S(1)}, u32[]{:S(2)}, u32[]{:S(2)}) collective-permute-start(bf16[64,4096]{1,0:T(8,128)(2,1)S(1)} %get-tuple-element.195), channel_id=1, source_target_pairs={{0,4},{4,0},{8,12},{12,8},{16,20},{20,16},{24,28},{28,24},{1,5},{5... | collective-permute-start | bytes 1572872 | tf_op jit(solution)/shard_map/ppermute | solution.py:80
  135.0 25.2 %collective-permute-start.30 = (bf16[64,4096]{1,0:T(8,128)(2,1)S(1)}, bf16[64,4096]{1,0:T(8,128)(2,1)S(1)}, u32[]{:S(2)}, u32[]{:S(2)}) collective-permute-start(bf16[64,4096]{1,0:T(8,128)(2,1)S(1)} %get-tuple-element.201), channel_id=1, source_target_pairs={{0,4},{4,0},{8,12},{12,8},{16,20},{20,16},{24,28},{28,24},{1,5},{5... | collective-permute-start | bytes 1572872 | tf_op jit(solution)/shard_map/ppermute | solution.py:80
  135.6 24.5 %collective-permute-start.29 = (bf16[64,4096]{1,0:T(8,128)(2,1)S(1)}, bf16[64,4096]{1,0:T(8,128)(2,1)S(1)}, u32[]{:S(2)}, u32[]{:S(2)}) collective-permute-start(bf16[64,4096]{1,0:T(8,128)(2,1)S(1)} %add_convert_fusion.3), channel_id=1, source_target_pairs={{0,1},{1,0},{2,3},{3,2},{4,5},{5,4},{6,7},{7,6},{8,9},{9,8},{10,11... | collective-permute-start | bytes 1572872 | tf_op jit(solution)/shard_map/ppermute | solution.py:84
  137.4 12.5 %collective-permute-start.34 = (bf16[64,128]{1,0:T(8,128)(2,1)S(1)}, bf16[64,128]{1,0:T(8,128)(2,1)S(1)}, u32[]{:S(2)}, u32[]{:S(2)}) collective-permute-start(bf16[64,128]{1,0:T(8,128)(2,1)S(1)} %pad_maximum_fusion.near), channel_id=1, source_target_pairs={{0,1},{1,0},{2,3},{3,2},{4,5},{5,4},{6,7},{7,6},{8,9},{9,8},{10,11... | collective-permute-start | bytes 49160 | tf_op jit(solution)/shard_map/ppermute | solution.py:84
  137.9 13.4 %collective-permute-start.25 = (bf16[48,4096]{1,0:T(8,128)(2,1)S(1)}, bf16[48,4096]{1,0:T(8,128)(2,1)S(1)}, u32[]{:S(2)}, u32[]{:S(2)}) collective-permute-start(bf16[48,4096]{1,0:T(8,128)(2,1)S(1)} %get-tuple-element.190), channel_id=1, source_target_pairs={{0,24},{4,28},{8,16},{12,20},{16,8},{20,12},{24,0},{28,4},{1,25},{... | collective-permute-start | bytes 1179656 | tf_op jit(solution)/shard_map/ppermute | solution.py:80
  140.2 17.4 %collective-permute-start.26 = (bf16[48,4096]{1,0:T(8,128)(2,1)S(1)}, bf16[48,4096]{1,0:T(8,128)(2,1)S(1)}, u32[]{:S(2)}, u32[]{:S(2)}) collective-permute-start(bf16[48,4096]{1,0:T(8,128)(2,1)S(1)} %get-tuple-element.191), channel_id=1, source_target_pairs={{0,8},{4,12},{8,0},{12,4},{16,24},{20,28},{24,16},{28,20},{1,9},{5... | collective-permute-start | bytes 1179656 | tf_op jit(solution)/shard_map/ppermute | solution.py:80
  149.9 10.2 %collective-permute-start.27 = (bf16[48,4096]{1,0:T(8,128)(2,1)S(1)}, bf16[48,4096]{1,0:T(8,128)(2,1)S(1)}, u32[]{:S(2)}, u32[]{:S(2)}) collective-permute-start(bf16[48,4096]{1,0:T(8,128)(2,1)S(1)} %get-tuple-element.192), channel_id=1, source_target_pairs={{0,16},{4,20},{8,24},{12,28},{16,0},{20,4},{24,8},{28,12},{1,17},{... | collective-permute-start | bytes 1179656 | tf_op jit(solution)/shard_map/ppermute | solution.py:80
  151.3 8.8 %collective-permute-start.35 = (bf16[64,128]{1,0:T(8,128)(2,1)S(1)}, bf16[64,128]{1,0:T(8,128)(2,1)S(1)}, u32[]{:S(2)}, u32[]{:S(2)}) collective-permute-start(bf16[64,128]{1,0:T(8,128)(2,1)S(1)} %collective-permute-done.34.near), channel_id=1, source_target_pairs={{0,4},{4,0},{8,12},{12,8},{16,20},{20,16},{24,28},{28,24},{1,5},{5... | collective-permute-start | bytes 49160 | tf_op jit(solution)/shard_map/ppermute | solution.py:80
  161.9 2.4 %collective-permute-start.36 = (bf16[64,4096]{1,0:T(8,128)(2,1)S(1)}, bf16[64,4096]{1,0:T(8,128)(2,1)S(1)}, u32[]{:S(2)}, u32[]{:S(2)}) collective-permute-start(bf16[64,4096]{1,0:T(8,128)(2,1)S(1)} %get-tuple-element.215), channel_id=1, source_target_pairs={{0,4},{4,0},{8,12},{12,8},{16,20},{20,16},{24,28},{28,24},{1,5},{5... | collective-permute-start | bytes 1572872 | tf_op jit(solution)/shard_map/ppermute | solution.py:80
  162.1 26.5 %collective-permute-start.38 = (bf16[64,4096]{1,0:T(8,128)(2,1)S(1)}, bf16[64,4096]{1,0:T(8,128)(2,1)S(1)}, u32[]{:S(2)}, u32[]{:S(2)}) collective-permute-start(bf16[64,4096]{1,0:T(8,128)(2,1)S(1)} %add_convert_fusion.1), channel_id=1, source_target_pairs={{0,2},{1,3},{2,0},{3,1},{4,6},{5,7},{6,4},{7,5},{8,10},{9,11},{10,... | collective-permute-start | bytes 1572872 | tf_op jit(solution)/shard_map/ppermute | solution.py:84
  164.4 24.2 %collective-permute-start.37 = (bf16[64,4096]{1,0:T(8,128)(2,1)S(1)}, bf16[64,4096]{1,0:T(8,128)(2,1)S(1)}, u32[]{:S(2)}, u32[]{:S(2)}) collective-permute-start(bf16[64,4096]{1,0:T(8,128)(2,1)S(1)} %add_convert_fusion.2), channel_id=1, source_target_pairs={{0,1},{1,0},{2,3},{3,2},{4,5},{5,4},{6,7},{7,6},{8,9},{9,8},{10,11... | collective-permute-start | bytes 1572872 | tf_op jit(solution)/shard_map/ppermute | solution.py:84
  165.7 12.9 %collective-permute-start.31 = (bf16[48,4096]{1,0:T(8,128)(2,1)S(1)}, bf16[48,4096]{1,0:T(8,128)(2,1)S(1)}, u32[]{:S(2)}, u32[]{:S(2)}) collective-permute-start(bf16[48,4096]{1,0:T(8,128)(2,1)S(1)} %get-tuple-element.206), channel_id=1, source_target_pairs={{0,24},{4,28},{8,16},{12,20},{16,8},{20,12},{24,0},{28,4},{1,25},{... | collective-permute-start | bytes 1179656 | tf_op jit(solution)/shard_map/ppermute | solution.py:80
  168.0 17.9 %collective-permute-start.32 = (bf16[48,4096]{1,0:T(8,128)(2,1)S(1)}, bf16[48,4096]{1,0:T(8,128)(2,1)S(1)}, u32[]{:S(2)}, u32[]{:S(2)}) collective-permute-start(bf16[48,4096]{1,0:T(8,128)(2,1)S(1)} %get-tuple-element.207), channel_id=1, source_target_pairs={{0,8},{4,12},{8,0},{12,4},{16,24},{20,28},{24,16},{28,20},{1,9},{5... | collective-permute-start | bytes 1179656 | tf_op jit(solution)/shard_map/ppermute | solution.py:80
  168.6 17.3 %collective-permute-start.33 = (bf16[48,4096]{1,0:T(8,128)(2,1)S(1)}, bf16[48,4096]{1,0:T(8,128)(2,1)S(1)}, u32[]{:S(2)}, u32[]{:S(2)}) collective-permute-start(bf16[48,4096]{1,0:T(8,128)(2,1)S(1)} %get-tuple-element.208), channel_id=1, source_target_pairs={{0,16},{4,20},{8,24},{12,28},{16,0},{20,4},{24,8},{28,12},{1,17},{... | collective-permute-start | bytes 1179656 | tf_op jit(solution)/shard_map/ppermute | solution.py:80
  178.6 10.0 %collective-permute-start = (bf16[64,128]{1,0:T(8,128)(2,1)S(1)}, bf16[64,128]{1,0:T(8,128)(2,1)S(1)}, u32[]{:S(2)}, u32[]{:S(2)}) collective-permute-start(bf16[64,128]{1,0:T(8,128)(2,1)S(1)} %pad_maximum_fusion.near), channel_id=1, source_target_pairs={{0,4},{4,0},{8,12},{12,8},{16,20},{20,16},{24,28},{28,24},{1,5},{5... | collective-permute-start | bytes 49160 | tf_op jit(solution)/shard_map/ppermute | solution.py:80
  190.4 2.0 %collective-permute-start.39 = (bf16[64,4096]{1,0:T(8,128)(2,1)S(1)}, bf16[64,4096]{1,0:T(8,128)(2,1)S(1)}, u32[]{:S(2)}, u32[]{:S(2)}) collective-permute-start(bf16[64,4096]{1,0:T(8,128)(2,1)S(1)} %get-tuple-element.224), channel_id=1, source_target_pairs={{0,4},{4,0},{8,12},{12,8},{16,20},{20,16},{24,28},{28,24},{1,5},{5... | collective-permute-start | bytes 1572872 | tf_op jit(solution)/shard_map/ppermute | solution.py:80

commit v4 on v3

--- a/solution.py
+++ b/solution.py
@@ -300,11 +300,9 @@
     own_far = flip(own, CORE)
     third = along(own, XOR[3])
     layer = exchange([own] * 4)
-    layer, (third,) = both(layer, [third])
+    layer, (third, late) = both(layer, [third, own])
 
     pair3, out3 = chosen(third)
-    late, *rest = hold([own] + layer + out3, [])
-    layer, out3 = rest[:4], rest[4:]
     in3 = exchange(out3)
     second, first = along(late, XOR[2]), along(meta, XOR[1])
     halves = [own, own_far] + [half for near in layer[1:] for half in (near, flip(near, CORE))]

time: 194 us -> 191 us (0.985)
  waiting for transfers between devices: 91.4 us -> 97.4 us
  starting transfers between devices: 42.9 us -> 37.8 us
  local copies, waits for them, and re-layouts: 11 us -> 6.83 us
    ppermute x7, waiting for transfers between devices: 15.5 us -> 37 us  [along(): return lax.ppermute(value, 'expert', pairs)]
    ppermute x33, waiting for transfers between devices: 75.9 us -> 60.5 us  [flip(): lax.ppermute(value, 'dp', [(i, i ^ bit) for i in range(lax.axis_size('dp'...]
    unnamed x21 -> x13, local copies, waits for them, and re-layouts: 9.62 us -> 5.43 us
    ppermute x7, starting transfers between devices: 14.6 us -> 10.6 us  [along(): return lax.ppermute(value, 'expert', pairs)]
  transfers between devices with their start and end apart: 40 -> 40, of which waited for: 18 -> 19; matrix products, arithmetic and copies ran while one was open for 0% -> 0% of each run, Pallas kernels for 21% -> 21%
where the time goes in v4:
time: 191 us
  waiting for transfers between devices  97.4 us (51%)
  Pallas kernels  45 us (24%)
  starting transfers between devices  37.8 us (20%)
  local copies, waits for them, and re-layouts  6.83 us (4%)
  other arithmetic  3.17 us (2%)
    ppermute x33, waiting for transfers between devices, flip(): lax.ppermute(value, 'dp', [(i, i ^ bit) for i in range(lax.axis_size('dp'...  60.5 us
    ppermute x7, waiting for transfers between devices, along(): return lax.ppermute(value, 'expert', pairs)  37 us
    pallas_call x4, Pallas kernels, expert(): pl.pallas_call(functools.partial(expert_kernel, count), grid=(blocks // e...  31.4 us
    ppermute x33, starting transfers between devices, flip(): lax.ppermute(value, 'dp', [(i, i ^ bit) for i in range(lax.axis_size('dp'...  27.1 us
    ppermute x7, starting transfers between devices, along(): return lax.ppermute(value, 'expert', pairs)  10.6 us
    pallas_call x4, Pallas kernels, combine(): pl.pallas_call(functools.partial(combine_kernel, width, experts, cap), ou...  7.02 us
    unnamed x13, local copies, waits for them, and re-layouts  5.43 us
  transfers between devices with their start and end apart: 40, of which 19 were waited for; matrix products, arithmetic and copies ran while one was open for 0% of the time, Pallas kernels for 21%

profile of v4, /device:TPU:0, one launch (start us, length us, event | category | flops | bytes accessed | tf_op | source)
XLA Modules:
  0.0 190.6 jit_solution(11602714248050927254)
XLA Ops:
  0.0 0.7 fusion.1
  0.7 0.7 select_reduce_fusion
  1.9 1.2 concatenate.8.refs_0_
  3.1 5.1 %collective-permute-start.4 = (bf16[64,4224]{1,0:T(8,128)(2,1)S(1)}, bf16[64,4224]{1,0:T(8,128)(2,1)S(1)}, u32[]{:S(2)}, u32[]{:S(2)}) collective-permute-start(bf16[64,4224]{1,0:T(8,128)(2,1)S(1)} %concatenate.8.refs_0_), channel_id=1, source_target_pairs={{0,3},{1,2},{2,1},{3,0},{4,7},{5,6},{6,5},{7,4},{8,11},{9,10},{10,... | collective-permute-start | bytes 1622024 | tf_op jit(solution)/shard_map/ppermute | solution.py:84
  8.2 1.5 collective-permute-start.3
  9.7 1.5 collective-permute-start.2
  11.2 0.5 collective-permute-start.1
  11.7 8.9 %collective-permute-done.4.near = bf16[64,4224]{1,0:T(8,128)(2,1)S(1)} collective-permute-done((bf16[64,4224]{1,0:T(8,128)(2,1)S(1)}, bf16[64,4224]{1,0:T(8,128)(2,1)S(1)}, u32[]{:S(2)}, u32[]{:S(2)}) %collective-permute-start.4) | collective-permute-done | bytes 540704 | tf_op jit(solution)/shard_map/ppermute | solution.py:84
  20.6 1.9 %collective-permute-done.3.refs_4_ = bf16[64,4224]{1,0:T(8,128)(2,1)S(1)} collective-permute-done((bf16[64,4224]{1,0:T(8,128)(2,1)S(1)}, bf16[64,4224]{1,0:T(8,128)(2,1)S(1)}, u32[]{:S(2)}, u32[]{:S(2)}) %collective-permute-start.3) | collective-permute-done | bytes 540704 | tf_op jit(solution)/shard_map/ppermute | solution.py:80
  22.5 2.4 %collective-permute-done.2.refs_2_ = bf16[64,4224]{1,0:T(8,128)(2,1)S(1)} collective-permute-done((bf16[64,4224]{1,0:T(8,128)(2,1)S(1)}, bf16[64,4224]{1,0:T(8,128)(2,1)S(1)}, u32[]{:S(2)}, u32[]{:S(2)}) %collective-permute-start.2) | collective-permute-done | bytes 540704 | tf_op jit(solution)/shard_map/ppermute | solution.py:80
  25.0 9.9 %collective-permute-done.1.refs_6_ = bf16[64,4224]{1,0:T(8,128)(2,1)} collective-permute-done((bf16[64,4224]{1,0:T(8,128)(2,1)S(1)}, bf16[64,4224]{1,0:T(8,128)(2,1)}, u32[]{:S(2)}, u32[]{:S(2)}) %collective-permute-start.1) | collective-permute-done | bytes 540704 | tf_op jit(solution)/shard_map/ppermute | solution.py:80
  34.8 0.5 collective-permute-start.10
  35.3 0.5 collective-permute-start.12
  35.9 1.6 collective-permute-done.5.far
  37.6 2.3 %select_rows.2 = (bf16[48,4096]{1,0:T(8,128)(2,1)S(1)}, bf16[48,4096]{1,0:T(8,128)(2,1)}, bf16[48,4096]{1,0:T(8,128)(2,1)}, bf16[48,4096]{1,0:T(8,128)(2,1)}) custom-call(s32[4]{0:T(128)S(1)} %pad_add_fusion.ids, bf16[64,4224]{1,0:T(8,128)(2,1)S(1)} %collective-permute-done.4.near, bf16[64,4224]{1,0:T(8,128)(2,1)S(1)} %collective-permute-done.5.far), custom_call_target="tpu_custom_call" | custom-call | tf_op jit(solution)/shard_map/select_rows/pallas_call | solution.py:137
  39.8 0.7 copy-done.3
  40.6 2.4 %collective-permute-start.6 = (bf16[48,4096]{1,0:T(8,128)(2,1)}, bf16[48,4096]{1,0:T(8,128)(2,1)}, u32[]{:S(2)}, u32[]{:S(2)}) collective-permute-start(bf16[48,4096]{1,0:T(8,128)(2,1)} %get-tuple-element.110), channel_id=1, source_target_pairs={{0,24},{4,28},{8,16},{12,20},{16,8},{20,12},{24,0},{28,4},{1,25},{... | collective-permute-start | bytes 1179656 | tf_op jit(solution)/shard_map/ppermute | solution.py:80
  43.0 0.5 collective-permute-start.7
  43.6 0.5 collective-permute-start.8
  44.2 3.0 %gather_rows.1 = (bf16[192,4096]{1,0:T(8,128)(2,1)S(1)}, bf16[192,4096]{1,0:T(8,128)(2,1)S(1)}) custom-call(s32[2]{0:T(128)S(1)} %pad_add_fusion.1.ids, bf16[64,4224]{1,0:T(8,128)(2,1)S(1)} %concatenate.8.refs_0_, bf16[64,4224]{1,0:T(8,128)(2,1)} %collective-permute-done.10.refs_1_, bf16[64,4224]{1,0:T(8,128)(2,1)S(1)} %collective-permute-done.2.refs_2_, ...), custom_call_target="tpu_custom_call" | custom-call | tf_op jit(solution)/shard_map/gather_rows/pallas_call | solution.py:174
  47.2 16.1 %collective-permute-done.9.near = bf16[64,4224]{1,0:T(8,128)(2,1)S(1)} collective-permute-done((bf16[64,4224]{1,0:T(8,128)(2,1)S(1)}, bf16[64,4224]{1,0:T(8,128)(2,1)S(1)}, u32[]{:S(2)}, u32[]{:S(2)}) %collective-permute-start.9) | collective-permute-done | bytes 540704 | tf_op jit(solution)/shard_map/ppermute | solution.py:84
  63.4 1.9 collective-permute-done.14.far
  65.3 1.3 select_rows.3
  66.7 2.5 %collective-permute-start.15 = (bf16[48,4096]{1,0:T(8,128)(2,1)S(1)}, bf16[48,4096]{1,0:T(8,128)(2,1)S(1)}, u32[]{:S(2)}, u32[]{:S(2)}) collective-permute-start(bf16[48,4096]{1,0:T(8,128)(2,1)S(1)} %get-tuple-element.126), channel_id=1, source_target_pairs={{0,24},{4,28},{8,16},{12,20},{16,8},{20,12},{24,0},{28,4},{1,25},{... | collective-permute-start | bytes 1179656 | tf_op jit(solution)/shard_map/ppermute | solution.py:80
  69.2 0.5 collective-permute-start.16
  69.7 0.5 collective-permute-start.17
  70.2 2.3 %copy-done.1 = bf16[1,12,12,128,128]{4,3,2,1,0:T(8,128)(2,1)S(1)} copy-done((bf16[1,12,12,128,128]{4,3,2,1,0:T(8,128)(2,1)S(1)}, bf16[1,12,12,128,128]{4,3,2,1,0:T(8,128)(2,1)}, u32[]{:S(2)}) %copy-start.1) | copy-done | bytes 4718616
  72.6 2.3 %copy-done.2 = bf16[1,12,12,128,128]{4,3,2,1,0:T(8,128)(2,1)S(1)} copy-done((bf16[1,12,12,128,128]{4,3,2,1,0:T(8,128)(2,1)S(1)}, bf16[1,12,12,128,128]{4,3,2,1,0:T(8,128)(2,1)}, u32[]{:S(2)}) %copy-start.2) | copy-done | bytes 4718616
  74.9 8.3 %expert_rows.4 = (bf16[48,4096]{1,0:T(8,128)(2,1)S(1)}, bf16[48,4096]{1,0:T(8,128)(2,1)S(1)}, bf16[48,4096]{1,0:T(8,128)(2,1)S(1)}, bf16[48,4096]{1,0:T(8,128)(2,1)S(1)}) custom-call(s32[12,12]{1,0:T(8,128)S(1)} %bitcast.9, bf16[48,4096]{1,0:T(8,128)(2,1)S(1)} %copy-done.4, bf16[48,4096]{1,0:T(8,128)(2,1)} %collective-permute-done.7.refs_1_, ...), custom_call_target="tpu_custom_call" | custom-call | tf_op jit(solution)/shard_map/expert_rows/pallas_call | solution.py:253
  83.2 4.1 %collective-permute-done.16.refs_1_ = bf16[48,4096]{1,0:T(8,128)(2,1)S(1)} collective-permute-done((bf16[48,4096]{1,0:T(8,128)(2,1)S(1)}, bf16[48,4096]{1,0:T(8,128)(2,1)S(1)}, u32[]{:S(2)}, u32[]{:S(2)}) %collective-permute-start.16) | collective-permute-done | bytes 393248 | tf_op jit(solution)/shard_map/ppermute | solution.py:80
  87.3 2.3 %collective-permute-start.18 = (bf16[48,4096]{1,0:T(8,128)(2,1)S(1)}, bf16[48,4096]{1,0:T(8,128)(2,1)S(1)}, u32[]{:S(2)}, u32[]{:S(2)}) collective-permute-start(bf16[48,4096]{1,0:T(8,128)(2,1)S(1)} %get-tuple-element.138), channel_id=1, source_target_pairs={{0,24},{4,28},{8,16},{12,20},{16,8},{20,12},{24,0},{28,4},{1,25},{... | collective-permute-start | bytes 1179656 | tf_op jit(solution)/shard_map/ppermute | solution.py:80
  89.7 0.5 collective-permute-start.19
  90.2 0.6 collective-permute-start.20
  90.8 7.7 %expert_rows.5 = (bf16[48,4096]{1,0:T(8,128)(2,1)S(1)}, bf16[48,4096]{1,0:T(8,128)(2,1)S(1)}, bf16[48,4096]{1,0:T(8,128)(2,1)S(1)}, bf16[48,4096]{1,0:T(8,128)(2,1)S(1)}) custom-call(s32[12,12]{1,0:T(8,128)S(1)} %bitcast.10, bf16[48,4096]{1,0:T(8,128)(2,1)S(1)} %get-tuple-element.142.refs_0_, bf16[48,4096]{1,0:T(8,128)(2,1)S(1)} %collective-permute-done.16.refs_1_, ...), custom_call_target="tpu_custom_call" | custom-call | tf_op jit(solution)/shard_map/expert_rows/pallas_call | solution.py:253
  98.5 1.8 collective-permute-done.18.refs_3_
  100.2 7.4 %collective-permute-done.19.refs_1_ = bf16[48,4096]{1,0:T(8,128)(2,1)S(1)} collective-permute-done((bf16[48,4096]{1,0:T(8,128)(2,1)S(1)}, bf16[48,4096]{1,0:T(8,128)(2,1)S(1)}, u32[]{:S(2)}, u32[]{:S(2)}) %collective-permute-start.19) | collective-permute-done | bytes 393248 | tf_op jit(solution)/shard_map/ppermute | solution.py:80
  107.7 2.3 %collective-permute-start.21 = (bf16[48,4096]{1,0:T(8,128)(2,1)S(1)}, bf16[48,4096]{1,0:T(8,128)(2,1)S(1)}, u32[]{:S(2)}, u32[]{:S(2)}) collective-permute-start(bf16[48,4096]{1,0:T(8,128)(2,1)S(1)} %get-tuple-element.150), channel_id=1, source_target_pairs={{0,24},{4,28},{8,16},{12,20},{16,8},{20,12},{24,0},{28,4},{1,25},{... | collective-permute-start | bytes 1179656 | tf_op jit(solution)/shard_map/ppermute | solution.py:80
  110.0 0.5 collective-permute-start.22
  110.6 0.6 collective-permute-start.23
  111.2 7.7 %expert_rows.6 = (bf16[48,4096]{1,0:T(8,128)(2,1)S(1)}, bf16[48,4096]{1,0:T(8,128)(2,1)S(1)}, bf16[48,4096]{1,0:T(8,128)(2,1)S(1)}, bf16[48,4096]{1,0:T(8,128)(2,1)S(1)}) custom-call(s32[12,12]{1,0:T(8,128)S(1)} %bitcast.11, bf16[192,4096]{1,0:T(8,128)(2,1)S(1)} %get-tuple-element.166.refs_0_, bf16[1,12,12,128,128]{4,3,2,1,0:T(8,128)(2,1)S(1)} %copy-done, ...), custom_call_target="tpu_custom_call" | custom-call | tf_op jit(solution)/shard_map/expert_rows/pallas_call | solution.py:253
  118.8 1.8 collective-permute-done.21.refs_3_
  120.6 1.8 combine_rows.4
  122.4 7.9 %expert_rows.7 = (bf16[48,4096]{1,0:T(8,128)(2,1)S(1)}, bf16[48,4096]{1,0:T(8,128)(2,1)S(1)}, bf16[48,4096]{1,0:T(8,128)(2,1)S(1)}, bf16[48,4096]{1,0:T(8,128)(2,1)S(1)}) custom-call(s32[12,12]{1,0:T(8,128)S(1)} %bitcast.12, bf16[192,4096]{1,0:T(8,128)(2,1)S(1)} %collective-permute-done.24.refs_0_, bf16[1,12,12,128,128]{4,3,2,1,0:T(8,128)(2,1)S(1)} %copy-done, ...), custom_call_target="tpu_custom_call" | custom-call | tf_op jit(solution)/shard_map/expert_rows/pallas_call | solution.py:253
  130.4 1.8 combine_rows.5
  132.1 0.6 collective-permute-start.30
  132.8 1.7 collective-permute-start.29
  135.1 2.3 %collective-permute-start.25 = (bf16[48,4096]{1,0:T(8,128)(2,1)S(1)}, bf16[48,4096]{1,0:T(8,128)(2,1)S(1)}, u32[]{:S(2)}, u32[]{:S(2)}) collective-permute-start(bf16[48,4096]{1,0:T(8,128)(2,1)S(1)} %get-tuple-element.176), channel_id=1, source_target_pairs={{0,24},{4,28},{8,16},{12,20},{16,8},{20,12},{24,0},{28,4},{1,25},{... | collective-permute-start | bytes 1179656 | tf_op jit(solution)/shard_map/ppermute | solution.py:80
  137.3 0.6 collective-permute-start.26
  137.9 9.2 %collective-permute-done.34.near = bf16[64,128]{1,0:T(8,128)(2,1)S(1)} collective-permute-done((bf16[64,128]{1,0:T(8,128)(2,1)S(1)}, bf16[64,128]{1,0:T(8,128)(2,1)S(1)}, u32[]{:S(2)}, u32[]{:S(2)}) %collective-permute-start.34) | collective-permute-done | bytes 16416 | tf_op jit(solution)/shard_map/ppermute | solution.py:84
  147.1 1.4 collective-permute-start.27
  148.5 6.3 %collective-permute-done.26.refs_1_ = bf16[48,4096]{1,0:T(8,128)(2,1)S(1)} collective-permute-done((bf16[48,4096]{1,0:T(8,128)(2,1)S(1)}, bf16[48,4096]{1,0:T(8,128)(2,1)S(1)}, u32[]{:S(2)}, u32[]{:S(2)}) %collective-permute-start.26) | collective-permute-done | bytes 393248 | tf_op jit(solution)/shard_map/ppermute | solution.py:80
  154.8 2.5 %collective-permute-done.27.refs_2_ = bf16[48,4096]{1,0:T(8,128)(2,1)S(1)} collective-permute-done((bf16[48,4096]{1,0:T(8,128)(2,1)S(1)}, bf16[48,4096]{1,0:T(8,128)(2,1)S(1)}, u32[]{:S(2)}, u32[]{:S(2)}) %collective-permute-start.27) | collective-permute-done | bytes 393248 | tf_op jit(solution)/shard_map/ppermute | solution.py:80
  157.3 1.8 combine_rows.6
  159.3 1.6 collective-permute-start.38
  161.1 1.7 collective-permute-start.37
  162.8 2.4 %collective-permute-start.31 = (bf16[48,4096]{1,0:T(8,128)(2,1)S(1)}, bf16[48,4096]{1,0:T(8,128)(2,1)S(1)}, u32[]{:S(2)}, u32[]{:S(2)}) collective-permute-start(bf16[48,4096]{1,0:T(8,128)(2,1)S(1)} %get-tuple-element.192), channel_id=1, source_target_pairs={{0,24},{4,28},{8,16},{12,20},{16,8},{20,12},{24,0},{28,4},{1,25},{... | collective-permute-start | bytes 1179656 | tf_op jit(solution)/shard_map/ppermute | solution.py:80
  165.2 0.5 collective-permute-start.32
  165.7 0.6 collective-permute-start.33
  166.3 9.5 %collective-permute-done.31.refs_3_ = bf16[48,4096]{1,0:T(8,128)(2,1)S(1)} collective-permute-done((bf16[48,4096]{1,0:T(8,128)(2,1)S(1)}, bf16[48,4096]{1,0:T(8,128)(2,1)S(1)}, u32[]{:S(2)}, u32[]{:S(2)}) %collective-permute-start.31) | collective-permute-done | bytes 393248 | tf_op jit(solution)/shard_map/ppermute | solution.py:80
  175.8 7.3 %collective-permute-done.32.refs_1_ = bf16[48,4096]{1,0:T(8,128)(2,1)S(1)} collective-permute-done((bf16[48,4096]{1,0:T(8,128)(2,1)S(1)}, bf16[48,4096]{1,0:T(8,128)(2,1)S(1)}, u32[]{:S(2)}, u32[]{:S(2)}) %collective-permute-start.32) | collective-permute-done | bytes 393248 | tf_op jit(solution)/shard_map/ppermute | solution.py:80
  183.0 2.8 %collective-permute-done.38 = bf16[64,4096]{1,0:T(8,128)(2,1)S(1)} collective-permute-done((bf16[64,4096]{1,0:T(8,128)(2,1)S(1)}, bf16[64,4096]{1,0:T(8,128)(2,1)S(1)}, u32[]{:S(2)}, u32[]{:S(2)}) %collective-permute-start.38) | collective-permute-done | bytes 524320 | tf_op jit(solution)/shard_map/ppermute | solution.py:84
  185.8 1.8 combine_rows.7
  187.7 1.9 collective-permute-done.39
  189.5 1.1 add_convert_fusion
  (57 shorter events, 2.2 us)
Async XLA Ops:
  0.0 70.2 %copy-start.5 = (s32[1,12,12]{2,0,1:T(1,128)S(1)}, s32[1,12,12]{2,0,1:T(1,128)}, u32[]{:S(2)}) copy-start(s32[1,12,12]{2,0,1:T(1,128)} %param.10) | copy-start | bytes 1732
  3.1 17.5 %collective-permute-start.4 = (bf16[64,4224]{1,0:T(8,128)(2,1)S(1)}, bf16[64,4224]{1,0:T(8,128)(2,1)S(1)}, u32[]{:S(2)}, u32[]{:S(2)}) collective-permute-start(bf16[64,4224]{1,0:T(8,128)(2,1)S(1)} %concatenate.8.refs_0_), channel_id=1, source_target_pairs={{0,3},{1,2},{2,1},{3,0},{4,7},{5,6},{6,5},{7,4},{8,11},{9,10},{10,... | collective-permute-start | bytes 1622024 | tf_op jit(solution)/shard_map/ppermute | solution.py:84
  8.2 14.3 %collective-permute-start.3 = (bf16[64,4224]{1,0:T(8,128)(2,1)S(1)}, bf16[64,4224]{1,0:T(8,128)(2,1)S(1)}, u32[]{:S(2)}, u32[]{:S(2)}) collective-permute-start(bf16[64,4224]{1,0:T(8,128)(2,1)S(1)} %concatenate.8.refs_0_), channel_id=1, source_target_pairs={{0,16},{4,20},{8,24},{12,28},{16,0},{20,4},{24,8},{28,12},{1,17},{... | collective-permute-start | bytes 1622024 | tf_op jit(solution)/shard_map/ppermute | solution.py:80
  9.7 15.2 %collective-permute-start.2 = (bf16[64,4224]{1,0:T(8,128)(2,1)S(1)}, bf16[64,4224]{1,0:T(8,128)(2,1)S(1)}, u32[]{:S(2)}, u32[]{:S(2)}) collective-permute-start(bf16[64,4224]{1,0:T(8,128)(2,1)S(1)} %concatenate.8.refs_0_), channel_id=1, source_target_pairs={{0,8},{4,12},{8,0},{12,4},{16,24},{20,28},{24,16},{28,20},{1,9},{5... | collective-permute-start | bytes 1622024 | tf_op jit(solution)/shard_map/ppermute | solution.py:80
  11.2 23.6 %collective-permute-start.1 = (bf16[64,4224]{1,0:T(8,128)(2,1)S(1)}, bf16[64,4224]{1,0:T(8,128)(2,1)}, u32[]{:S(2)}, u32[]{:S(2)}) collective-permute-start(bf16[64,4224]{1,0:T(8,128)(2,1)S(1)} %concatenate.8.refs_0_), channel_id=1, source_target_pairs={{0,24},{4,28},{8,16},{12,20},{16,8},{20,12},{24,0},{28,4},{1,25},{... | collective-permute-start | bytes 1622024 | tf_op jit(solution)/shard_map/ppermute | solution.py:80
  34.8 2.7 %collective-permute-start.5 = (bf16[64,4224]{1,0:T(8,128)(2,1)S(1)}, bf16[64,4224]{1,0:T(8,128)(2,1)S(1)}, u32[]{:S(2)}, u32[]{:S(2)}) collective-permute-start(bf16[64,4224]{1,0:T(8,128)(2,1)S(1)} %collective-permute-done.4.near), channel_id=1, source_target_pairs={{0,4},{4,0},{8,12},{12,8},{16,20},{20,16},{24,28},{28,24},{1,5},{5... | collective-permute-start | bytes 1622024 | tf_op jit(solution)/shard_map/ppermute | solution.py:80
  34.8 5.8 %collective-permute-start.10 = (bf16[64,4224]{1,0:T(8,128)(2,1)S(1)}, bf16[64,4224]{1,0:T(8,128)(2,1)}, u32[]{:S(2)}, u32[]{:S(2)}) collective-permute-start(bf16[64,4224]{1,0:T(8,128)(2,1)S(1)} %concatenate.8.refs_0_), channel_id=1, source_target_pairs={{0,4},{4,0},{8,12},{12,8},{16,20},{20,16},{24,28},{28,24},{1,5},{5... | collective-permute-start | bytes 1622024 | tf_op jit(solution)/shard_map/ppermute | solution.py:80
  35.3 7.7 %collective-permute-start.11 = (bf16[64,4224]{1,0:T(8,128)(2,1)S(1)}, bf16[64,4224]{1,0:T(8,128)(2,1)}, u32[]{:S(2)}, u32[]{:S(2)}) collective-permute-start(bf16[64,4224]{1,0:T(8,128)(2,1)S(1)} %collective-permute-done.2.refs_2_), channel_id=1, source_target_pairs={{0,4},{4,0},{8,12},{12,8},{16,20},{20,16},{24,28},{28,24},{1,5},{5... | collective-permute-start | bytes 1622024 | tf_op jit(solution)/shard_map/ppermute | solution.py:80
  35.3 8.2 %collective-permute-start.12 = (bf16[64,4224]{1,0:T(8,128)(2,1)S(1)}, bf16[64,4224]{1,0:T(8,128)(2,1)}, u32[]{:S(2)}, u32[]{:S(2)}) collective-permute-start(bf16[64,4224]{1,0:T(8,128)(2,1)S(1)} %collective-permute-done.3.refs_4_), channel_id=1, source_target_pairs={{0,4},{4,0},{8,12},{12,8},{16,20},{20,16},{24,28},{28,24},{1,5},{5... | collective-permute-start | bytes 1622024 | tf_op jit(solution)/shard_map/ppermute | solution.py:80
  35.9 8.3 %collective-permute-start.13 = (bf16[64,4224]{1,0:T(8,128)(2,1)}, bf16[64,4224]{1,0:T(8,128)(2,1)}, u32[]{:S(2)}, u32[]{:S(2)}) collective-permute-start(bf16[64,4224]{1,0:T(8,128)(2,1)} %collective-permute-done.1.refs_6_), channel_id=1, source_target_pairs={{0,4},{4,0},{8,12},{12,8},{16,20},{20,16},{24,28},{28,24},{1,5},{5... | collective-permute-start | bytes 1622024 | tf_op jit(solution)/shard_map/ppermute | solution.py:80
  37.5 25.8 %collective-permute-start.9 = (bf16[64,4224]{1,0:T(8,128)(2,1)S(1)}, bf16[64,4224]{1,0:T(8,128)(2,1)S(1)}, u32[]{:S(2)}, u32[]{:S(2)}) collective-permute-start(bf16[64,4224]{1,0:T(8,128)(2,1)S(1)} %concatenate.8.refs_0_), channel_id=1, source_target_pairs={{0,2},{1,3},{2,0},{3,1},{4,6},{5,7},{6,4},{7,5},{8,10},{9,11},{10,... | collective-permute-start | bytes 1622024 | tf_op jit(solution)/shard_map/ppermute | solution.py:84
  39.8 0.8 copy-start.3
  40.6 22.7 %collective-permute-start.6 = (bf16[48,4096]{1,0:T(8,128)(2,1)}, bf16[48,4096]{1,0:T(8,128)(2,1)}, u32[]{:S(2)}, u32[]{:S(2)}) collective-permute-start(bf16[48,4096]{1,0:T(8,128)(2,1)} %get-tuple-element.110), channel_id=1, source_target_pairs={{0,24},{4,28},{8,16},{12,20},{16,8},{20,12},{24,0},{28,4},{1,25},{... | collective-permute-start | bytes 1179656 | tf_op jit(solution)/shard_map/ppermute | solution.py:80
  43.0 20.2 %collective-permute-start.7 = (bf16[48,4096]{1,0:T(8,128)(2,1)}, bf16[48,4096]{1,0:T(8,128)(2,1)}, u32[]{:S(2)}, u32[]{:S(2)}) collective-permute-start(bf16[48,4096]{1,0:T(8,128)(2,1)} %get-tuple-element.111), channel_id=1, source_target_pairs={{0,8},{4,12},{8,0},{12,4},{16,24},{20,28},{24,16},{28,20},{1,9},{5... | collective-permute-start | bytes 1179656 | tf_op jit(solution)/shard_map/ppermute | solution.py:80
  43.6 19.7 %collective-permute-start.8 = (bf16[48,4096]{1,0:T(8,128)(2,1)}, bf16[48,4096]{1,0:T(8,128)(2,1)}, u32[]{:S(2)}, u32[]{:S(2)}) collective-permute-start(bf16[48,4096]{1,0:T(8,128)(2,1)} %get-tuple-element.112), channel_id=1, source_target_pairs={{0,16},{4,20},{8,24},{12,28},{16,0},{20,4},{24,8},{28,12},{1,17},{... | collective-permute-start | bytes 1179656 | tf_op jit(solution)/shard_map/ppermute | solution.py:80
  44.1 26.1 %copy-start = (bf16[1,12,12,128,128]{4,3,2,1,0:T(8,128)(2,1)S(1)}, bf16[1,12,12,128,128]{4,3,2,1,0:T(8,128)(2,1)}, u32[]{:S(2)}) copy-start(bf16[1,12,12,128,128]{4,3,2,1,0:T(8,128)(2,1)} %refs_1_.3) | copy-start | bytes 14155780
  44.1 26.1 %copy-start.4 = (bf16[48,4096]{1,0:T(8,128)(2,1)S(1)}, bf16[48,4096]{1,0:T(8,128)(2,1)}, u32[]{:S(2)}) copy-start(bf16[48,4096]{1,0:T(8,128)(2,1)} %copy-done.3) | copy-start | bytes 1179652
  63.3 2.0 %collective-permute-start.14 = (bf16[64,4224]{1,0:T(8,128)(2,1)S(1)}, bf16[64,4224]{1,0:T(8,128)(2,1)S(1)}, u32[]{:S(2)}, u32[]{:S(2)}) collective-permute-start(bf16[64,4224]{1,0:T(8,128)(2,1)S(1)} %collective-permute-done.9.near), channel_id=1, source_target_pairs={{0,4},{4,0},{8,12},{12,8},{16,20},{20,16},{24,28},{28,24},{1,5},{5... | collective-permute-start | bytes 1622024 | tf_op jit(solution)/shard_map/ppermute | solution.py:80
  66.6 55.8 %collective-permute-start.24 = (bf16[192,4096]{1,0:T(8,128)(2,1)S(1)}, bf16[192,4096]{1,0:T(8,128)(2,1)S(1)}, u32[]{:S(2)}, u32[]{:S(2)}) collective-permute-start(bf16[192,4096]{1,0:T(8,128)(2,1)S(1)} %get-tuple-element.165), channel_id=1, source_target_pairs={{0,1},{1,0},{2,3},{3,2},{4,5},{5,4},{6,7},{7,6},{8,9},{9,8},{10,11... | collective-permute-start | bytes 4718600 | tf_op jit(solution)/shard_map/ppermute | solution.py:84
  66.7 16.5 %collective-permute-start.15 = (bf16[48,4096]{1,0:T(8,128)(2,1)S(1)}, bf16[48,4096]{1,0:T(8,128)(2,1)S(1)}, u32[]{:S(2)}, u32[]{:S(2)}) collective-permute-start(bf16[48,4096]{1,0:T(8,128)(2,1)S(1)} %get-tuple-element.126), channel_id=1, source_target_pairs={{0,24},{4,28},{8,16},{12,20},{16,8},{20,12},{24,0},{28,4},{1,25},{... | collective-permute-start | bytes 1179656 | tf_op jit(solution)/shard_map/ppermute | solution.py:80
  69.2 18.1 %collective-permute-start.16 = (bf16[48,4096]{1,0:T(8,128)(2,1)S(1)}, bf16[48,4096]{1,0:T(8,128)(2,1)S(1)}, u32[]{:S(2)}, u32[]{:S(2)}) collective-permute-start(bf16[48,4096]{1,0:T(8,128)(2,1)S(1)} %get-tuple-element.127), channel_id=1, source_target_pairs={{0,8},{4,12},{8,0},{12,4},{16,24},{20,28},{24,16},{28,20},{1,9},{5... | collective-permute-start | bytes 1179656 | tf_op jit(solution)/shard_map/ppermute | solution.py:80
  69.7 17.6 %collective-permute-start.17 = (bf16[48,4096]{1,0:T(8,128)(2,1)S(1)}, bf16[48,4096]{1,0:T(8,128)(2,1)S(1)}, u32[]{:S(2)}, u32[]{:S(2)}) collective-permute-start(bf16[48,4096]{1,0:T(8,128)(2,1)S(1)} %get-tuple-element.128), channel_id=1, source_target_pairs={{0,16},{4,20},{8,24},{12,28},{16,0},{20,4},{24,8},{28,12},{1,17},{... | collective-permute-start | bytes 1179656 | tf_op jit(solution)/shard_map/ppermute | solution.py:80
  70.2 2.3 %copy-start.1 = (bf16[1,12,12,128,128]{4,3,2,1,0:T(8,128)(2,1)S(1)}, bf16[1,12,12,128,128]{4,3,2,1,0:T(8,128)(2,1)}, u32[]{:S(2)}) copy-start(bf16[1,12,12,128,128]{4,3,2,1,0:T(8,128)(2,1)} %refs_2_.3) | copy-start | bytes 14155780
  72.6 2.3 %copy-start.2 = (bf16[1,12,12,128,128]{4,3,2,1,0:T(8,128)(2,1)S(1)}, bf16[1,12,12,128,128]{4,3,2,1,0:T(8,128)(2,1)}, u32[]{:S(2)}) copy-start(bf16[1,12,12,128,128]{4,3,2,1,0:T(8,128)(2,1)} %refs_3_.3) | copy-start | bytes 14155780
  87.3 12.9 %collective-permute-start.18 = (bf16[48,4096]{1,0:T(8,128)(2,1)S(1)}, bf16[48,4096]{1,0:T(8,128)(2,1)S(1)}, u32[]{:S(2)}, u32[]{:S(2)}) collective-permute-start(bf16[48,4096]{1,0:T(8,128)(2,1)S(1)} %get-tuple-element.138), channel_id=1, source_target_pairs={{0,24},{4,28},{8,16},{12,20},{16,8},{20,12},{24,0},{28,4},{1,25},{... | collective-permute-start | bytes 1179656 | tf_op jit(solution)/shard_map/ppermute | solution.py:80
  89.7 18.0 %collective-permute-start.19 = (bf16[48,4096]{1,0:T(8,128)(2,1)S(1)}, bf16[48,4096]{1,0:T(8,128)(2,1)S(1)}, u32[]{:S(2)}, u32[]{:S(2)}) collective-permute-start(bf16[48,4096]{1,0:T(8,128)(2,1)S(1)} %get-tuple-element.139), channel_id=1, source_target_pairs={{0,8},{4,12},{8,0},{12,4},{16,24},{20,28},{24,16},{28,20},{1,9},{5... | collective-permute-start | bytes 1179656 | tf_op jit(solution)/shard_map/ppermute | solution.py:80
  90.2 17.5 %collective-permute-start.20 = (bf16[48,4096]{1,0:T(8,128)(2,1)S(1)}, bf16[48,4096]{1,0:T(8,128)(2,1)S(1)}, u32[]{:S(2)}, u32[]{:S(2)}) collective-permute-start(bf16[48,4096]{1,0:T(8,128)(2,1)S(1)} %get-tuple-element.140), channel_id=1, source_target_pairs={{0,16},{4,20},{8,24},{12,28},{16,0},{20,4},{24,8},{28,12},{1,17},{... | collective-permute-start | bytes 1179656 | tf_op jit(solution)/shard_map/ppermute | solution.py:80
  107.7 12.9 %collective-permute-start.21 = (bf16[48,4096]{1,0:T(8,128)(2,1)S(1)}, bf16[48,4096]{1,0:T(8,128)(2,1)S(1)}, u32[]{:S(2)}, u32[]{:S(2)}) collective-permute-start(bf16[48,4096]{1,0:T(8,128)(2,1)S(1)} %get-tuple-element.150), channel_id=1, source_target_pairs={{0,24},{4,28},{8,16},{12,20},{16,8},{20,12},{24,0},{28,4},{1,25},{... | collective-permute-start | bytes 1179656 | tf_op jit(solution)/shard_map/ppermute | solution.py:80
  110.0 20.2 %collective-permute-start.22 = (bf16[48,4096]{1,0:T(8,128)(2,1)S(1)}, bf16[48,4096]{1,0:T(8,128)(2,1)S(1)}, u32[]{:S(2)}, u32[]{:S(2)}) collective-permute-start(bf16[48,4096]{1,0:T(8,128)(2,1)S(1)} %get-tuple-element.156), channel_id=1, source_target_pairs={{0,8},{4,12},{8,0},{12,4},{16,24},{20,28},{24,16},{28,20},{1,9},{5... | collective-permute-start | bytes 1179656 | tf_op jit(solution)/shard_map/ppermute | solution.py:80
  110.6 19.7 %collective-permute-start.23 = (bf16[48,4096]{1,0:T(8,128)(2,1)S(1)}, bf16[48,4096]{1,0:T(8,128)(2,1)S(1)}, u32[]{:S(2)}, u32[]{:S(2)}) collective-permute-start(bf16[48,4096]{1,0:T(8,128)(2,1)S(1)} %get-tuple-element.157), channel_id=1, source_target_pairs={{0,16},{4,20},{8,24},{12,28},{16,0},{20,4},{24,8},{28,12},{1,17},{... | collective-permute-start | bytes 1179656 | tf_op jit(solution)/shard_map/ppermute | solution.py:80
  130.3 2.4 %collective-permute-start.28 = (bf16[64,4096]{1,0:T(8,128)(2,1)S(1)}, bf16[64,4096]{1,0:T(8,128)(2,1)S(1)}, u32[]{:S(2)}, u32[]{:S(2)}) collective-permute-start(bf16[64,4096]{1,0:T(8,128)(2,1)S(1)} %get-tuple-element.181), channel_id=1, source_target_pairs={{0,4},{4,0},{8,12},{12,8},{16,20},{20,16},{24,28},{28,24},{1,5},{5... | collective-permute-start | bytes 1572872 | tf_op jit(solution)/shard_map/ppermute | solution.py:80
  132.1 25.2 %collective-permute-start.30 = (bf16[64,4096]{1,0:T(8,128)(2,1)S(1)}, bf16[64,4096]{1,0:T(8,128)(2,1)S(1)}, u32[]{:S(2)}, u32[]{:S(2)}) collective-permute-start(bf16[64,4096]{1,0:T(8,128)(2,1)S(1)} %get-tuple-element.187), channel_id=1, source_target_pairs={{0,4},{4,0},{8,12},{12,8},{16,20},{20,16},{24,28},{28,24},{1,5},{5... | collective-permute-start | bytes 1572872 | tf_op jit(solution)/shard_map/ppermute | solution.py:80
  132.8 24.5 %collective-permute-start.29 = (bf16[64,4096]{1,0:T(8,128)(2,1)S(1)}, bf16[64,4096]{1,0:T(8,128)(2,1)S(1)}, u32[]{:S(2)}, u32[]{:S(2)}) collective-permute-start(bf16[64,4096]{1,0:T(8,128)(2,1)S(1)} %add_convert_fusion.3), channel_id=1, source_target_pairs={{0,1},{1,0},{2,3},{3,2},{4,5},{5,4},{6,7},{7,6},{8,9},{9,8},{10,11... | collective-permute-start | bytes 1572872 | tf_op jit(solution)/shard_map/ppermute | solution.py:84
  134.6 12.5 %collective-permute-start.34 = (bf16[64,128]{1,0:T(8,128)(2,1)S(1)}, bf16[64,128]{1,0:T(8,128)(2,1)S(1)}, u32[]{:S(2)}, u32[]{:S(2)}) collective-permute-start(bf16[64,128]{1,0:T(8,128)(2,1)S(1)} %pad_maximum_fusion.near), channel_id=1, source_target_pairs={{0,1},{1,0},{2,3},{3,2},{4,5},{5,4},{6,7},{7,6},{8,9},{9,8},{10,11... | collective-permute-start | bytes 49160 | tf_op jit(solution)/shard_map/ppermute | solution.py:84
  135.1 13.4 %collective-permute-start.25 = (bf16[48,4096]{1,0:T(8,128)(2,1)S(1)}, bf16[48,4096]{1,0:T(8,128)(2,1)S(1)}, u32[]{:S(2)}, u32[]{:S(2)}) collective-permute-start(bf16[48,4096]{1,0:T(8,128)(2,1)S(1)} %get-tuple-element.176), channel_id=1, source_target_pairs={{0,24},{4,28},{8,16},{12,20},{16,8},{20,12},{24,0},{28,4},{1,25},{... | collective-permute-start | bytes 1179656 | tf_op jit(solution)/shard_map/ppermute | solution.py:80
  137.3 17.4 %collective-permute-start.26 = (bf16[48,4096]{1,0:T(8,128)(2,1)S(1)}, bf16[48,4096]{1,0:T(8,128)(2,1)S(1)}, u32[]{:S(2)}, u32[]{:S(2)}) collective-permute-start(bf16[48,4096]{1,0:T(8,128)(2,1)S(1)} %get-tuple-element.177), channel_id=1, source_target_pairs={{0,8},{4,12},{8,0},{12,4},{16,24},{20,28},{24,16},{28,20},{1,9},{5... | collective-permute-start | bytes 1179656 | tf_op jit(solution)/shard_map/ppermute | solution.py:80
  147.1 10.2 %collective-permute-start.27 = (bf16[48,4096]{1,0:T(8,128)(2,1)S(1)}, bf16[48,4096]{1,0:T(8,128)(2,1)S(1)}, u32[]{:S(2)}, u32[]{:S(2)}) collective-permute-start(bf16[48,4096]{1,0:T(8,128)(2,1)S(1)} %get-tuple-element.178), channel_id=1, source_target_pairs={{0,16},{4,20},{8,24},{12,28},{16,0},{20,4},{24,8},{28,12},{1,17},{... | collective-permute-start | bytes 1179656 | tf_op jit(solution)/shard_map/ppermute | solution.py:80
  148.5 8.8 %collective-permute-start.35 = (bf16[64,128]{1,0:T(8,128)(2,1)S(1)}, bf16[64,128]{1,0:T(8,128)(2,1)S(1)}, u32[]{:S(2)}, u32[]{:S(2)}) collective-permute-start(bf16[64,128]{1,0:T(8,128)(2,1)S(1)} %collective-permute-done.34.near), channel_id=1, source_target_pairs={{0,4},{4,0},{8,12},{12,8},{16,20},{20,16},{24,28},{28,24},{1,5},{5... | collective-permute-start | bytes 49160 | tf_op jit(solution)/shard_map/ppermute | solution.py:80
  159.0 2.0 %collective-permute-start.36 = (bf16[64,4096]{1,0:T(8,128)(2,1)S(1)}, bf16[64,4096]{1,0:T(8,128)(2,1)S(1)}, u32[]{:S(2)}, u32[]{:S(2)}) collective-permute-start(bf16[64,4096]{1,0:T(8,128)(2,1)S(1)} %get-tuple-element.201), channel_id=1, source_target_pairs={{0,4},{4,0},{8,12},{12,8},{16,20},{20,16},{24,28},{28,24},{1,5},{5... | collective-permute-start | bytes 1572872 | tf_op jit(solution)/shard_map/ppermute | solution.py:80
  159.3 26.5 %collective-permute-start.38 = (bf16[64,4096]{1,0:T(8,128)(2,1)S(1)}, bf16[64,4096]{1,0:T(8,128)(2,1)S(1)}, u32[]{:S(2)}, u32[]{:S(2)}) collective-permute-start(bf16[64,4096]{1,0:T(8,128)(2,1)S(1)} %add_convert_fusion.1), channel_id=1, source_target_pairs={{0,2},{1,3},{2,0},{3,1},{4,6},{5,7},{6,4},{7,5},{8,10},{9,11},{10,... | collective-permute-start | bytes 1572872 | tf_op jit(solution)/shard_map/ppermute | solution.py:84
  161.1 24.7 %collective-permute-start.37 = (bf16[64,4096]{1,0:T(8,128)(2,1)S(1)}, bf16[64,4096]{1,0:T(8,128)(2,1)S(1)}, u32[]{:S(2)}, u32[]{:S(2)}) collective-permute-start(bf16[64,4096]{1,0:T(8,128)(2,1)S(1)} %add_convert_fusion.2), channel_id=1, source_target_pairs={{0,1},{1,0},{2,3},{3,2},{4,5},{5,4},{6,7},{7,6},{8,9},{9,8},{10,11... | collective-permute-start | bytes 1572872 | tf_op jit(solution)/shard_map/ppermute | solution.py:84
  162.8 12.9 %collective-permute-start.31 = (bf16[48,4096]{1,0:T(8,128)(2,1)S(1)}, bf16[48,4096]{1,0:T(8,128)(2,1)S(1)}, u32[]{:S(2)}, u32[]{:S(2)}) collective-permute-start(bf16[48,4096]{1,0:T(8,128)(2,1)S(1)} %get-tuple-element.192), channel_id=1, source_target_pairs={{0,24},{4,28},{8,16},{12,20},{16,8},{20,12},{24,0},{28,4},{1,25},{... | collective-permute-start | bytes 1179656 | tf_op jit(solution)/shard_map/ppermute | solution.py:80
  165.2 17.8 %collective-permute-start.32 = (bf16[48,4096]{1,0:T(8,128)(2,1)S(1)}, bf16[48,4096]{1,0:T(8,128)(2,1)S(1)}, u32[]{:S(2)}, u32[]{:S(2)}) collective-permute-start(bf16[48,4096]{1,0:T(8,128)(2,1)S(1)} %get-tuple-element.193), channel_id=1, source_target_pairs={{0,8},{4,12},{8,0},{12,4},{16,24},{20,28},{24,16},{28,20},{1,9},{5... | collective-permute-start | bytes 1179656 | tf_op jit(solution)/shard_map/ppermute | solution.py:80
  165.7 17.3 %collective-permute-start.33 = (bf16[48,4096]{1,0:T(8,128)(2,1)S(1)}, bf16[48,4096]{1,0:T(8,128)(2,1)S(1)}, u32[]{:S(2)}, u32[]{:S(2)}) collective-permute-start(bf16[48,4096]{1,0:T(8,128)(2,1)S(1)} %get-tuple-element.194), channel_id=1, source_target_pairs={{0,16},{4,20},{8,24},{12,28},{16,0},{20,4},{24,8},{28,12},{1,17},{... | collective-permute-start | bytes 1179656 | tf_op jit(solution)/shard_map/ppermute | solution.py:80
  175.8 10.0 %collective-permute-start = (bf16[64,128]{1,0:T(8,128)(2,1)S(1)}, bf16[64,128]{1,0:T(8,128)(2,1)S(1)}, u32[]{:S(2)}, u32[]{:S(2)}) collective-permute-start(bf16[64,128]{1,0:T(8,128)(2,1)S(1)} %pad_maximum_fusion.near), channel_id=1, source_target_pairs={{0,4},{4,0},{8,12},{12,8},{16,20},{20,16},{24,28},{28,24},{1,5},{5... | collective-permute-start | bytes 49160 | tf_op jit(solution)/shard_map/ppermute | solution.py:80
  187.6 2.0 %collective-permute-start.39 = (bf16[64,4096]{1,0:T(8,128)(2,1)S(1)}, bf16[64,4096]{1,0:T(8,128)(2,1)S(1)}, u32[]{:S(2)}, u32[]{:S(2)}) collective-permute-start(bf16[64,4096]{1,0:T(8,128)(2,1)S(1)} %get-tuple-element.210), channel_id=1, source_target_pairs={{0,4},{4,0},{8,12},{12,8},{16,20},{20,16},{24,28},{28,24},{1,5},{5... | collective-permute-start | bytes 1572872 | tf_op jit(solution)/shard_map/ppermute | solution.py:80

commit v5 on v4

--- a/solution.py
+++ b/solution.py
@@ -319,7 +319,8 @@
 
     got3 = exchange(back3)
     back2 = expert(topo, in2, weights)
-    got3, back2 = both(got3, list(back2))
+    got3, held = both(got3, list(pair1) + list(back2))
+    pair1, back2 = held[:2], held[2:]
 
     got2 = exchange(back2)
     back0 = expert(topo, [in0], weights)
@@ -331,8 +332,9 @@
 
     got1 = exchange(back1)
     far3 = along(add(mine3, flip(theirs3, CORE)), XOR[1])
-    mine2, theirs2 = joined(pair2, got2)
+    mine2, theirs2 = combine(ids, *pair2, got2, width, experts, cap)
     got1, (far3, mine2, theirs2, *back0) = both(got1, [far3, mine2, theirs2] + back0)
+    theirs2 = flip(theirs2, CORE)
 
     got0 = exchange(back0)
     far2 = along(add(mine2, theirs2, far3), XOR[2])

time: 191 us -> 190 us (level)
  transfers between devices with their start and end apart: 40 -> 40, of which waited for: 19 -> 17; matrix products, arithmetic and copies ran while one was open for 0% -> 0% of each run, Pallas kernels for 21% -> 22%
where the time goes in v5:
time: 190 us
  waiting for transfers between devices  97.7 us (51%)
  Pallas kernels  44.9 us (24%)
  starting transfers between devices  36.8 us (19%)
  local copies, waits for them, and re-layouts  6.83 us (4%)
  other arithmetic  3.16 us (2%)
    ppermute x33, waiting for transfers between devices, flip(): lax.ppermute(value, 'dp', [(i, i ^ bit) for i in range(lax.axis_size('dp'...  59.5 us
    ppermute x7, waiting for transfers between devices, along(): return lax.ppermute(value, 'expert', pairs)  38.2 us
    pallas_call x4, Pallas kernels, expert(): pl.pallas_call(functools.partial(expert_kernel, count), grid=(blocks // e...  31.4 us
    ppermute x33, starting transfers between devices, flip(): lax.ppermute(value, 'dp', [(i, i ^ bit) for i in range(lax.axis_size('dp'...  26.4 us
    ppermute x7, starting transfers between devices, along(): return lax.ppermute(value, 'expert', pairs)  10.4 us
    pallas_call x4, Pallas kernels, combine(): pl.pallas_call(functools.partial(combine_kernel, width, experts, cap), ou...  7.01 us
    unnamed x13, local copies, waits for them, and re-layouts  5.43 us
  transfers between devices with their start and end apart: 40, of which 17 were waited for; matrix products, arithmetic and copies ran while one was open for 0% of the time, Pallas kernels for 22%

profile of v5, /device:TPU:0, one launch (start us, length us, event | category | flops | bytes accessed | tf_op | source)
XLA Modules:
  0.0 189.9 jit_solution(12547738058704057803)
XLA Ops:
  0.0 0.7 fusion.1
  0.7 0.7 select_reduce_fusion
  1.9 1.2 concatenate.8.refs_0_
  3.1 5.1 %collective-permute-start.4 = (bf16[64,4224]{1,0:T(8,128)(2,1)S(1)}, bf16[64,4224]{1,0:T(8,128)(2,1)S(1)}, u32[]{:S(2)}, u32[]{:S(2)}) collective-permute-start(bf16[64,4224]{1,0:T(8,128)(2,1)S(1)} %concatenate.8.refs_0_), channel_id=1, source_target_pairs={{0,3},{1,2},{2,1},{3,0},{4,7},{5,6},{6,5},{7,4},{8,11},{9,10},{10,... | collective-permute-start | bytes 1622024 | tf_op jit(solution)/shard_map/ppermute | solution.py:84
  8.2 1.5 collective-permute-start.3
  9.7 1.5 collective-permute-start.2
  11.2 0.5 collective-permute-start.1
  11.7 8.9 %collective-permute-done.4.near = bf16[64,4224]{1,0:T(8,128)(2,1)S(1)} collective-permute-done((bf16[64,4224]{1,0:T(8,128)(2,1)S(1)}, bf16[64,4224]{1,0:T(8,128)(2,1)S(1)}, u32[]{:S(2)}, u32[]{:S(2)}) %collective-permute-start.4) | collective-permute-done | bytes 540704 | tf_op jit(solution)/shard_map/ppermute | solution.py:84
  20.6 1.9 %collective-permute-done.3.refs_4_ = bf16[64,4224]{1,0:T(8,128)(2,1)S(1)} collective-permute-done((bf16[64,4224]{1,0:T(8,128)(2,1)S(1)}, bf16[64,4224]{1,0:T(8,128)(2,1)S(1)}, u32[]{:S(2)}, u32[]{:S(2)}) %collective-permute-start.3) | collective-permute-done | bytes 540704 | tf_op jit(solution)/shard_map/ppermute | solution.py:80
  22.5 2.4 %collective-permute-done.2.refs_2_ = bf16[64,4224]{1,0:T(8,128)(2,1)S(1)} collective-permute-done((bf16[64,4224]{1,0:T(8,128)(2,1)S(1)}, bf16[64,4224]{1,0:T(8,128)(2,1)S(1)}, u32[]{:S(2)}, u32[]{:S(2)}) %collective-permute-start.2) | collective-permute-done | bytes 540704 | tf_op jit(solution)/shard_map/ppermute | solution.py:80
  25.0 9.9 %collective-permute-done.1.refs_6_ = bf16[64,4224]{1,0:T(8,128)(2,1)} collective-permute-done((bf16[64,4224]{1,0:T(8,128)(2,1)S(1)}, bf16[64,4224]{1,0:T(8,128)(2,1)}, u32[]{:S(2)}, u32[]{:S(2)}) %collective-permute-start.1) | collective-permute-done | bytes 540704 | tf_op jit(solution)/shard_map/ppermute | solution.py:80
  34.8 0.5 collective-permute-start.10
  35.3 0.5 collective-permute-start.12
  35.9 1.6 collective-permute-done.5.far
  37.6 2.3 %select_rows.2 = (bf16[48,4096]{1,0:T(8,128)(2,1)S(1)}, bf16[48,4096]{1,0:T(8,128)(2,1)}, bf16[48,4096]{1,0:T(8,128)(2,1)}, bf16[48,4096]{1,0:T(8,128)(2,1)}) custom-call(s32[4]{0:T(128)S(1)} %pad_add_fusion.ids, bf16[64,4224]{1,0:T(8,128)(2,1)S(1)} %collective-permute-done.4.near, bf16[64,4224]{1,0:T(8,128)(2,1)S(1)} %collective-permute-done.5.far), custom_call_target="tpu_custom_call" | custom-call | tf_op jit(solution)/shard_map/select_rows/pallas_call | solution.py:137
  39.8 0.7 copy-done.3
  40.6 2.4 %collective-permute-start.6 = (bf16[48,4096]{1,0:T(8,128)(2,1)}, bf16[48,4096]{1,0:T(8,128)(2,1)}, u32[]{:S(2)}, u32[]{:S(2)}) collective-permute-start(bf16[48,4096]{1,0:T(8,128)(2,1)} %get-tuple-element.112), channel_id=1, source_target_pairs={{0,24},{4,28},{8,16},{12,20},{16,8},{20,12},{24,0},{28,4},{1,25},{... | collective-permute-start | bytes 1179656 | tf_op jit(solution)/shard_map/ppermute | solution.py:80
  43.0 0.5 collective-permute-start.7
  43.6 0.5 collective-permute-start.8
  44.2 3.0 %gather_rows.1 = (bf16[192,4096]{1,0:T(8,128)(2,1)S(1)}, bf16[192,4096]{1,0:T(8,128)(2,1)S(1)}) custom-call(s32[2]{0:T(128)S(1)} %pad_add_fusion.1.ids, bf16[64,4224]{1,0:T(8,128)(2,1)S(1)} %concatenate.8.refs_0_, bf16[64,4224]{1,0:T(8,128)(2,1)} %collective-permute-done.10.refs_1_, bf16[64,4224]{1,0:T(8,128)(2,1)S(1)} %collective-permute-done.2.refs_2_, ...), custom_call_target="tpu_custom_call" | custom-call | tf_op jit(solution)/shard_map/gather_rows/pallas_call | solution.py:174
  47.2 16.1 %collective-permute-done.9.near = bf16[64,4224]{1,0:T(8,128)(2,1)S(1)} collective-permute-done((bf16[64,4224]{1,0:T(8,128)(2,1)S(1)}, bf16[64,4224]{1,0:T(8,128)(2,1)S(1)}, u32[]{:S(2)}, u32[]{:S(2)}) %collective-permute-start.9) | collective-permute-done | bytes 540704 | tf_op jit(solution)/shard_map/ppermute | solution.py:84
  63.4 1.9 %collective-permute-done.14.far = bf16[64,4224]{1,0:T(8,128)(2,1)S(1)} collective-permute-done((bf16[64,4224]{1,0:T(8,128)(2,1)S(1)}, bf16[64,4224]{1,0:T(8,128)(2,1)S(1)}, u32[]{:S(2)}, u32[]{:S(2)}) %collective-permute-start.14) | collective-permute-done | bytes 540704 | tf_op jit(solution)/shard_map/ppermute | solution.py:80
  65.3 1.3 select_rows.3
  66.7 2.5 %collective-permute-start.15 = (bf16[48,4096]{1,0:T(8,128)(2,1)S(1)}, bf16[48,4096]{1,0:T(8,128)(2,1)S(1)}, u32[]{:S(2)}, u32[]{:S(2)}) collective-permute-start(bf16[48,4096]{1,0:T(8,128)(2,1)S(1)} %get-tuple-element.128), channel_id=1, source_target_pairs={{0,24},{4,28},{8,16},{12,20},{16,8},{20,12},{24,0},{28,4},{1,25},{... | collective-permute-start | bytes 1179656 | tf_op jit(solution)/shard_map/ppermute | solution.py:80
  69.2 0.5 collective-permute-start.16
  69.7 0.5 collective-permute-start.17
  70.2 2.3 %copy-done.1 = bf16[1,12,12,128,128]{4,3,2,1,0:T(8,128)(2,1)S(1)} copy-done((bf16[1,12,12,128,128]{4,3,2,1,0:T(8,128)(2,1)S(1)}, bf16[1,12,12,128,128]{4,3,2,1,0:T(8,128)(2,1)}, u32[]{:S(2)}) %copy-start.1) | copy-done | bytes 4718616
  72.6 2.3 %copy-done.2 = bf16[1,12,12,128,128]{4,3,2,1,0:T(8,128)(2,1)S(1)} copy-done((bf16[1,12,12,128,128]{4,3,2,1,0:T(8,128)(2,1)S(1)}, bf16[1,12,12,128,128]{4,3,2,1,0:T(8,128)(2,1)}, u32[]{:S(2)}) %copy-start.2) | copy-done | bytes 4718616
  74.9 8.2 %expert_rows.4 = (bf16[48,4096]{1,0:T(8,128)(2,1)S(1)}, bf16[48,4096]{1,0:T(8,128)(2,1)S(1)}, bf16[48,4096]{1,0:T(8,128)(2,1)S(1)}, bf16[48,4096]{1,0:T(8,128)(2,1)S(1)}) custom-call(s32[12,12]{1,0:T(8,128)S(1)} %bitcast.9, bf16[48,4096]{1,0:T(8,128)(2,1)S(1)} %copy-done.4, bf16[48,4096]{1,0:T(8,128)(2,1)} %collective-permute-done.7.refs_1_, ...), custom_call_target="tpu_custom_call" | custom-call | tf_op jit(solution)/shard_map/expert_rows/pallas_call | solution.py:253
  83.2 4.1 %collective-permute-done.16.refs_1_ = bf16[48,4096]{1,0:T(8,128)(2,1)S(1)} collective-permute-done((bf16[48,4096]{1,0:T(8,128)(2,1)S(1)}, bf16[48,4096]{1,0:T(8,128)(2,1)S(1)}, u32[]{:S(2)}, u32[]{:S(2)}) %collective-permute-start.16) | collective-permute-done | bytes 393248 | tf_op jit(solution)/shard_map/ppermute | solution.py:80
  87.3 2.3 %collective-permute-start.18 = (bf16[48,4096]{1,0:T(8,128)(2,1)S(1)}, bf16[48,4096]{1,0:T(8,128)(2,1)S(1)}, u32[]{:S(2)}, u32[]{:S(2)}) collective-permute-start(bf16[48,4096]{1,0:T(8,128)(2,1)S(1)} %get-tuple-element.140), channel_id=1, source_target_pairs={{0,24},{4,28},{8,16},{12,20},{16,8},{20,12},{24,0},{28,4},{1,25},{... | collective-permute-start | bytes 1179656 | tf_op jit(solution)/shard_map/ppermute | solution.py:80
  89.7 0.5 collective-permute-start.19
  90.2 0.6 collective-permute-start.20
  90.9 1.7 collective-permute-start.21
  92.6 10.8 %collective-permute-done.21.near = bf16[64,128]{1,0:T(8,128)(2,1)S(1)} collective-permute-done((bf16[64,128]{1,0:T(8,128)(2,1)S(1)}, bf16[64,128]{1,0:T(8,128)(2,1)S(1)}, u32[]{:S(2)}, u32[]{:S(2)}) %collective-permute-start.21) | collective-permute-done | bytes 16416 | tf_op jit(solution)/shard_map/ppermute | solution.py:84
  103.4 7.6 %expert_rows.5 = (bf16[48,4096]{1,0:T(8,128)(2,1)S(1)}, bf16[48,4096]{1,0:T(8,128)(2,1)S(1)}, bf16[48,4096]{1,0:T(8,128)(2,1)S(1)}, bf16[48,4096]{1,0:T(8,128)(2,1)S(1)}) custom-call(s32[12,12]{1,0:T(8,128)S(1)} %bitcast.10, bf16[48,4096]{1,0:T(8,128)(2,1)S(1)} %get-tuple-element.144.refs_0_, bf16[48,4096]{1,0:T(8,128)(2,1)S(1)} %collective-permute-done.16.refs_1_, ...), custom_call_target="tpu_custom_call" | custom-call | tf_op jit(solution)/shard_map/expert_rows/pallas_call | solution.py:253
  111.1 2.5 %collective-permute-start.23 = (bf16[48,4096]{1,0:T(8,128)(2,1)S(1)}, bf16[48,4096]{1,0:T(8,128)(2,1)S(1)}, u32[]{:S(2)}, u32[]{:S(2)}) collective-permute-start(bf16[48,4096]{1,0:T(8,128)(2,1)S(1)} %get-tuple-element.152), channel_id=1, source_target_pairs={{0,24},{4,28},{8,16},{12,20},{16,8},{20,12},{24,0},{28,4},{1,25},{... | collective-permute-start | bytes 1179656 | tf_op jit(solution)/shard_map/ppermute | solution.py:80
  113.6 0.5 collective-permute-start.24
  114.2 0.5 collective-permute-start.25
  114.7 7.6 %expert_rows.6 = (bf16[48,4096]{1,0:T(8,128)(2,1)S(1)}, bf16[48,4096]{1,0:T(8,128)(2,1)S(1)}, bf16[48,4096]{1,0:T(8,128)(2,1)S(1)}, bf16[48,4096]{1,0:T(8,128)(2,1)S(1)}) custom-call(s32[12,12]{1,0:T(8,128)S(1)} %bitcast.11, bf16[192,4096]{1,0:T(8,128)(2,1)S(1)} %get-tuple-element.168.refs_0_, bf16[1,12,12,128,128]{4,3,2,1,0:T(8,128)(2,1)S(1)} %copy-done, ...), custom_call_target="tpu_custom_call" | custom-call | tf_op jit(solution)/shard_map/expert_rows/pallas_call | solution.py:253
  122.3 1.7 collective-permute-done.23.refs_3_
  124.0 1.8 combine_rows.4
  125.8 7.8 %expert_rows.7 = (bf16[48,4096]{1,0:T(8,128)(2,1)S(1)}, bf16[48,4096]{1,0:T(8,128)(2,1)S(1)}, bf16[48,4096]{1,0:T(8,128)(2,1)S(1)}, bf16[48,4096]{1,0:T(8,128)(2,1)S(1)}) custom-call(s32[12,12]{1,0:T(8,128)S(1)} %bitcast.12, bf16[192,4096]{1,0:T(8,128)(2,1)S(1)} %collective-permute-done.26.refs_0_, bf16[1,12,12,128,128]{4,3,2,1,0:T(8,128)(2,1)S(1)} %copy-done, ...), custom_call_target="tpu_custom_call" | custom-call | tf_op jit(solution)/shard_map/expert_rows/pallas_call | solution.py:253
  133.8 1.9 collective-permute-done.30
  135.8 0.4 collective-permute-start.31
  136.1 2.4 %collective-permute-start.27 = (bf16[48,4096]{1,0:T(8,128)(2,1)S(1)}, bf16[48,4096]{1,0:T(8,128)(2,1)S(1)}, u32[]{:S(2)}, u32[]{:S(2)}) collective-permute-start(bf16[48,4096]{1,0:T(8,128)(2,1)S(1)} %get-tuple-element.178), channel_id=1, source_target_pairs={{0,24},{4,28},{8,16},{12,20},{16,8},{20,12},{24,0},{28,4},{1,25},{... | collective-permute-start | bytes 1179656 | tf_op jit(solution)/shard_map/ppermute | solution.py:80
  138.6 0.6 collective-permute-start.28
  139.1 0.5 collective-permute-start.29
  139.6 1.7 combine_rows.5
  141.4 7.7 %collective-permute-done.27.refs_3_ = bf16[48,4096]{1,0:T(8,128)(2,1)S(1)} collective-permute-done((bf16[48,4096]{1,0:T(8,128)(2,1)S(1)}, bf16[48,4096]{1,0:T(8,128)(2,1)S(1)}, u32[]{:S(2)}, u32[]{:S(2)}) %collective-permute-start.27) | collective-permute-done | bytes 393248 | tf_op jit(solution)/shard_map/ppermute | solution.py:80
  149.1 7.4 %collective-permute-done.28.refs_1_ = bf16[48,4096]{1,0:T(8,128)(2,1)S(1)} collective-permute-done((bf16[48,4096]{1,0:T(8,128)(2,1)S(1)}, bf16[48,4096]{1,0:T(8,128)(2,1)S(1)}, u32[]{:S(2)}, u32[]{:S(2)}) %collective-permute-start.28) | collective-permute-done | bytes 393248 | tf_op jit(solution)/shard_map/ppermute | solution.py:80
  156.5 1.8 combine_rows.6
  158.3 0.6 collective-permute-start.35
  159.0 1.7 collective-permute-start.38
  160.8 1.4 collective-permute-start.36
  162.3 2.3 %collective-permute-start.32 = (bf16[48,4096]{1,0:T(8,128)(2,1)S(1)}, bf16[48,4096]{1,0:T(8,128)(2,1)S(1)}, u32[]{:S(2)}, u32[]{:S(2)}) collective-permute-start(bf16[48,4096]{1,0:T(8,128)(2,1)S(1)} %get-tuple-element.194), channel_id=1, source_target_pairs={{0,24},{4,28},{8,16},{12,20},{16,8},{20,12},{24,0},{28,4},{1,25},{... | collective-permute-start | bytes 1179656 | tf_op jit(solution)/shard_map/ppermute | solution.py:80
  164.6 0.6 collective-permute-start.33
  165.1 0.6 collective-permute-start.34
  165.7 9.4 %collective-permute-done.32.refs_3_ = bf16[48,4096]{1,0:T(8,128)(2,1)S(1)} collective-permute-done((bf16[48,4096]{1,0:T(8,128)(2,1)S(1)}, bf16[48,4096]{1,0:T(8,128)(2,1)S(1)}, u32[]{:S(2)}, u32[]{:S(2)}) %collective-permute-start.32) | collective-permute-done | bytes 393248 | tf_op jit(solution)/shard_map/ppermute | solution.py:80
  175.2 7.5 %collective-permute-done.33.refs_1_ = bf16[48,4096]{1,0:T(8,128)(2,1)S(1)} collective-permute-done((bf16[48,4096]{1,0:T(8,128)(2,1)S(1)}, bf16[48,4096]{1,0:T(8,128)(2,1)S(1)}, u32[]{:S(2)}, u32[]{:S(2)}) %collective-permute-start.33) | collective-permute-done | bytes 393248 | tf_op jit(solution)/shard_map/ppermute | solution.py:80
  182.7 2.4 %collective-permute-done.38 = bf16[64,4096]{1,0:T(8,128)(2,1)S(1)} collective-permute-done((bf16[64,4096]{1,0:T(8,128)(2,1)S(1)}, bf16[64,4096]{1,0:T(8,128)(2,1)S(1)}, u32[]{:S(2)}, u32[]{:S(2)}) %collective-permute-start.38) | collective-permute-done | bytes 524320 | tf_op jit(solution)/shard_map/ppermute | solution.py:84
  185.1 1.8 combine_rows.7
  186.9 1.9 collective-permute-done.39
  188.8 1.0 add_convert_fusion
  (57 shorter events, 1.5 us)
Async XLA Ops:
  0.0 70.2 %copy-start.5 = (s32[1,12,12]{2,0,1:T(1,128)S(1)}, s32[1,12,12]{2,0,1:T(1,128)}, u32[]{:S(2)}) copy-start(s32[1,12,12]{2,0,1:T(1,128)} %param.10) | copy-start | bytes 1732
  3.1 17.5 %collective-permute-start.4 = (bf16[64,4224]{1,0:T(8,128)(2,1)S(1)}, bf16[64,4224]{1,0:T(8,128)(2,1)S(1)}, u32[]{:S(2)}, u32[]{:S(2)}) collective-permute-start(bf16[64,4224]{1,0:T(8,128)(2,1)S(1)} %concatenate.8.refs_0_), channel_id=1, source_target_pairs={{0,3},{1,2},{2,1},{3,0},{4,7},{5,6},{6,5},{7,4},{8,11},{9,10},{10,... | collective-permute-start | bytes 1622024 | tf_op jit(solution)/shard_map/ppermute | solution.py:84
  8.2 14.3 %collective-permute-start.3 = (bf16[64,4224]{1,0:T(8,128)(2,1)S(1)}, bf16[64,4224]{1,0:T(8,128)(2,1)S(1)}, u32[]{:S(2)}, u32[]{:S(2)}) collective-permute-start(bf16[64,4224]{1,0:T(8,128)(2,1)S(1)} %concatenate.8.refs_0_), channel_id=1, source_target_pairs={{0,16},{4,20},{8,24},{12,28},{16,0},{20,4},{24,8},{28,12},{1,17},{... | collective-permute-start | bytes 1622024 | tf_op jit(solution)/shard_map/ppermute | solution.py:80
  9.7 15.2 %collective-permute-start.2 = (bf16[64,4224]{1,0:T(8,128)(2,1)S(1)}, bf16[64,4224]{1,0:T(8,128)(2,1)S(1)}, u32[]{:S(2)}, u32[]{:S(2)}) collective-permute-start(bf16[64,4224]{1,0:T(8,128)(2,1)S(1)} %concatenate.8.refs_0_), channel_id=1, source_target_pairs={{0,8},{4,12},{8,0},{12,4},{16,24},{20,28},{24,16},{28,20},{1,9},{5... | collective-permute-start | bytes 1622024 | tf_op jit(solution)/shard_map/ppermute | solution.py:80
  11.2 23.6 %collective-permute-start.1 = (bf16[64,4224]{1,0:T(8,128)(2,1)S(1)}, bf16[64,4224]{1,0:T(8,128)(2,1)}, u32[]{:S(2)}, u32[]{:S(2)}) collective-permute-start(bf16[64,4224]{1,0:T(8,128)(2,1)S(1)} %concatenate.8.refs_0_), channel_id=1, source_target_pairs={{0,24},{4,28},{8,16},{12,20},{16,8},{20,12},{24,0},{28,4},{1,25},{... | collective-permute-start | bytes 1622024 | tf_op jit(solution)/shard_map/ppermute | solution.py:80
  34.8 2.7 %collective-permute-start.5 = (bf16[64,4224]{1,0:T(8,128)(2,1)S(1)}, bf16[64,4224]{1,0:T(8,128)(2,1)S(1)}, u32[]{:S(2)}, u32[]{:S(2)}) collective-permute-start(bf16[64,4224]{1,0:T(8,128)(2,1)S(1)} %collective-permute-done.4.near), channel_id=1, source_target_pairs={{0,4},{4,0},{8,12},{12,8},{16,20},{20,16},{24,28},{28,24},{1,5},{5... | collective-permute-start | bytes 1622024 | tf_op jit(solution)/shard_map/ppermute | solution.py:80
  34.8 5.8 %collective-permute-start.10 = (bf16[64,4224]{1,0:T(8,128)(2,1)S(1)}, bf16[64,4224]{1,0:T(8,128)(2,1)}, u32[]{:S(2)}, u32[]{:S(2)}) collective-permute-start(bf16[64,4224]{1,0:T(8,128)(2,1)S(1)} %concatenate.8.refs_0_), channel_id=1, source_target_pairs={{0,4},{4,0},{8,12},{12,8},{16,20},{20,16},{24,28},{28,24},{1,5},{5... | collective-permute-start | bytes 1622024 | tf_op jit(solution)/shard_map/ppermute | solution.py:80
  35.3 7.7 %collective-permute-start.11 = (bf16[64,4224]{1,0:T(8,128)(2,1)S(1)}, bf16[64,4224]{1,0:T(8,128)(2,1)}, u32[]{:S(2)}, u32[]{:S(2)}) collective-permute-start(bf16[64,4224]{1,0:T(8,128)(2,1)S(1)} %collective-permute-done.2.refs_2_), channel_id=1, source_target_pairs={{0,4},{4,0},{8,12},{12,8},{16,20},{20,16},{24,28},{28,24},{1,5},{5... | collective-permute-start | bytes 1622024 | tf_op jit(solution)/shard_map/ppermute | solution.py:80
  35.3 8.2 %collective-permute-start.12 = (bf16[64,4224]{1,0:T(8,128)(2,1)S(1)}, bf16[64,4224]{1,0:T(8,128)(2,1)}, u32[]{:S(2)}, u32[]{:S(2)}) collective-permute-start(bf16[64,4224]{1,0:T(8,128)(2,1)S(1)} %collective-permute-done.3.refs_4_), channel_id=1, source_target_pairs={{0,4},{4,0},{8,12},{12,8},{16,20},{20,16},{24,28},{28,24},{1,5},{5... | collective-permute-start | bytes 1622024 | tf_op jit(solution)/shard_map/ppermute | solution.py:80
  35.9 8.3 %collective-permute-start.13 = (bf16[64,4224]{1,0:T(8,128)(2,1)}, bf16[64,4224]{1,0:T(8,128)(2,1)}, u32[]{:S(2)}, u32[]{:S(2)}) collective-permute-start(bf16[64,4224]{1,0:T(8,128)(2,1)} %collective-permute-done.1.refs_6_), channel_id=1, source_target_pairs={{0,4},{4,0},{8,12},{12,8},{16,20},{20,16},{24,28},{28,24},{1,5},{5... | collective-permute-start | bytes 1622024 | tf_op jit(solution)/shard_map/ppermute | solution.py:80
  37.5 25.8 %collective-permute-start.9 = (bf16[64,4224]{1,0:T(8,128)(2,1)S(1)}, bf16[64,4224]{1,0:T(8,128)(2,1)S(1)}, u32[]{:S(2)}, u32[]{:S(2)}) collective-permute-start(bf16[64,4224]{1,0:T(8,128)(2,1)S(1)} %concatenate.8.refs_0_), channel_id=1, source_target_pairs={{0,2},{1,3},{2,0},{3,1},{4,6},{5,7},{6,4},{7,5},{8,10},{9,11},{10,... | collective-permute-start | bytes 1622024 | tf_op jit(solution)/shard_map/ppermute | solution.py:84
  39.8 0.8 copy-start.3
  40.6 22.7 %collective-permute-start.6 = (bf16[48,4096]{1,0:T(8,128)(2,1)}, bf16[48,4096]{1,0:T(8,128)(2,1)}, u32[]{:S(2)}, u32[]{:S(2)}) collective-permute-start(bf16[48,4096]{1,0:T(8,128)(2,1)} %get-tuple-element.112), channel_id=1, source_target_pairs={{0,24},{4,28},{8,16},{12,20},{16,8},{20,12},{24,0},{28,4},{1,25},{... | collective-permute-start | bytes 1179656 | tf_op jit(solution)/shard_map/ppermute | solution.py:80
  43.0 20.2 %collective-permute-start.7 = (bf16[48,4096]{1,0:T(8,128)(2,1)}, bf16[48,4096]{1,0:T(8,128)(2,1)}, u32[]{:S(2)}, u32[]{:S(2)}) collective-permute-start(bf16[48,4096]{1,0:T(8,128)(2,1)} %get-tuple-element.113), channel_id=1, source_target_pairs={{0,8},{4,12},{8,0},{12,4},{16,24},{20,28},{24,16},{28,20},{1,9},{5... | collective-permute-start | bytes 1179656 | tf_op jit(solution)/shard_map/ppermute | solution.py:80
  43.6 19.7 %collective-permute-start.8 = (bf16[48,4096]{1,0:T(8,128)(2,1)}, bf16[48,4096]{1,0:T(8,128)(2,1)}, u32[]{:S(2)}, u32[]{:S(2)}) collective-permute-start(bf16[48,4096]{1,0:T(8,128)(2,1)} %get-tuple-element.114), channel_id=1, source_target_pairs={{0,16},{4,20},{8,24},{12,28},{16,0},{20,4},{24,8},{28,12},{1,17},{... | collective-permute-start | bytes 1179656 | tf_op jit(solution)/shard_map/ppermute | solution.py:80
  44.1 26.1 %copy-start = (bf16[1,12,12,128,128]{4,3,2,1,0:T(8,128)(2,1)S(1)}, bf16[1,12,12,128,128]{4,3,2,1,0:T(8,128)(2,1)}, u32[]{:S(2)}) copy-start(bf16[1,12,12,128,128]{4,3,2,1,0:T(8,128)(2,1)} %refs_1_.3) | copy-start | bytes 14155780
  44.1 26.1 %copy-start.4 = (bf16[48,4096]{1,0:T(8,128)(2,1)S(1)}, bf16[48,4096]{1,0:T(8,128)(2,1)}, u32[]{:S(2)}) copy-start(bf16[48,4096]{1,0:T(8,128)(2,1)} %copy-done.3) | copy-start | bytes 1179652
  63.3 2.0 %collective-permute-start.14 = (bf16[64,4224]{1,0:T(8,128)(2,1)S(1)}, bf16[64,4224]{1,0:T(8,128)(2,1)S(1)}, u32[]{:S(2)}, u32[]{:S(2)}) collective-permute-start(bf16[64,4224]{1,0:T(8,128)(2,1)S(1)} %collective-permute-done.9.near), channel_id=1, source_target_pairs={{0,4},{4,0},{8,12},{12,8},{16,20},{20,16},{24,28},{28,24},{1,5},{5... | collective-permute-start | bytes 1622024 | tf_op jit(solution)/shard_map/ppermute | solution.py:80
  66.6 59.2 %collective-permute-start.26 = (bf16[192,4096]{1,0:T(8,128)(2,1)S(1)}, bf16[192,4096]{1,0:T(8,128)(2,1)S(1)}, u32[]{:S(2)}, u32[]{:S(2)}) collective-permute-start(bf16[192,4096]{1,0:T(8,128)(2,1)S(1)} %get-tuple-element.167), channel_id=1, source_target_pairs={{0,1},{1,0},{2,3},{3,2},{4,5},{5,4},{6,7},{7,6},{8,9},{9,8},{10,11... | collective-permute-start | bytes 4718600 | tf_op jit(solution)/shard_map/ppermute | solution.py:84
  66.7 16.5 %collective-permute-start.15 = (bf16[48,4096]{1,0:T(8,128)(2,1)S(1)}, bf16[48,4096]{1,0:T(8,128)(2,1)S(1)}, u32[]{:S(2)}, u32[]{:S(2)}) collective-permute-start(bf16[48,4096]{1,0:T(8,128)(2,1)S(1)} %get-tuple-element.128), channel_id=1, source_target_pairs={{0,24},{4,28},{8,16},{12,20},{16,8},{20,12},{24,0},{28,4},{1,25},{... | collective-permute-start | bytes 1179656 | tf_op jit(solution)/shard_map/ppermute | solution.py:80
  69.2 18.1 %collective-permute-start.16 = (bf16[48,4096]{1,0:T(8,128)(2,1)S(1)}, bf16[48,4096]{1,0:T(8,128)(2,1)S(1)}, u32[]{:S(2)}, u32[]{:S(2)}) collective-permute-start(bf16[48,4096]{1,0:T(8,128)(2,1)S(1)} %get-tuple-element.129), channel_id=1, source_target_pairs={{0,8},{4,12},{8,0},{12,4},{16,24},{20,28},{24,16},{28,20},{1,9},{5... | collective-permute-start | bytes 1179656 | tf_op jit(solution)/shard_map/ppermute | solution.py:80
  69.7 17.6 %collective-permute-start.17 = (bf16[48,4096]{1,0:T(8,128)(2,1)S(1)}, bf16[48,4096]{1,0:T(8,128)(2,1)S(1)}, u32[]{:S(2)}, u32[]{:S(2)}) collective-permute-start(bf16[48,4096]{1,0:T(8,128)(2,1)S(1)} %get-tuple-element.130), channel_id=1, source_target_pairs={{0,16},{4,20},{8,24},{12,28},{16,0},{20,4},{24,8},{28,12},{1,17},{... | collective-permute-start | bytes 1179656 | tf_op jit(solution)/shard_map/ppermute | solution.py:80
  70.2 2.3 %copy-start.1 = (bf16[1,12,12,128,128]{4,3,2,1,0:T(8,128)(2,1)S(1)}, bf16[1,12,12,128,128]{4,3,2,1,0:T(8,128)(2,1)}, u32[]{:S(2)}) copy-start(bf16[1,12,12,128,128]{4,3,2,1,0:T(8,128)(2,1)} %refs_2_.3) | copy-start | bytes 14155780
  72.6 2.3 %copy-start.2 = (bf16[1,12,12,128,128]{4,3,2,1,0:T(8,128)(2,1)S(1)}, bf16[1,12,12,128,128]{4,3,2,1,0:T(8,128)(2,1)}, u32[]{:S(2)}) copy-start(bf16[1,12,12,128,128]{4,3,2,1,0:T(8,128)(2,1)} %refs_3_.3) | copy-start | bytes 14155780
  87.3 23.8 %collective-permute-start.18 = (bf16[48,4096]{1,0:T(8,128)(2,1)S(1)}, bf16[48,4096]{1,0:T(8,128)(2,1)S(1)}, u32[]{:S(2)}, u32[]{:S(2)}) collective-permute-start(bf16[48,4096]{1,0:T(8,128)(2,1)S(1)} %get-tuple-element.140), channel_id=1, source_target_pairs={{0,24},{4,28},{8,16},{12,20},{16,8},{20,12},{24,0},{28,4},{1,25},{... | collective-permute-start | bytes 1179656 | tf_op jit(solution)/shard_map/ppermute | solution.py:80
  89.7 21.5 %collective-permute-start.19 = (bf16[48,4096]{1,0:T(8,128)(2,1)S(1)}, bf16[48,4096]{1,0:T(8,128)(2,1)S(1)}, u32[]{:S(2)}, u32[]{:S(2)}) collective-permute-start(bf16[48,4096]{1,0:T(8,128)(2,1)S(1)} %get-tuple-element.141), channel_id=1, source_target_pairs={{0,8},{4,12},{8,0},{12,4},{16,24},{20,28},{24,16},{28,20},{1,9},{5... | collective-permute-start | bytes 1179656 | tf_op jit(solution)/shard_map/ppermute | solution.py:80
  90.2 20.9 %collective-permute-start.20 = (bf16[48,4096]{1,0:T(8,128)(2,1)S(1)}, bf16[48,4096]{1,0:T(8,128)(2,1)S(1)}, u32[]{:S(2)}, u32[]{:S(2)}) collective-permute-start(bf16[48,4096]{1,0:T(8,128)(2,1)S(1)} %get-tuple-element.142), channel_id=1, source_target_pairs={{0,16},{4,20},{8,24},{12,28},{16,0},{20,4},{24,8},{28,12},{1,17},{... | collective-permute-start | bytes 1179656 | tf_op jit(solution)/shard_map/ppermute | solution.py:80
  90.9 12.5 %collective-permute-start.21 = (bf16[64,128]{1,0:T(8,128)(2,1)S(1)}, bf16[64,128]{1,0:T(8,128)(2,1)S(1)}, u32[]{:S(2)}, u32[]{:S(2)}) collective-permute-start(bf16[64,128]{1,0:T(8,128)(2,1)S(1)} %pad_maximum_fusion.near), channel_id=1, source_target_pairs={{0,1},{1,0},{2,3},{3,2},{4,5},{5,4},{6,7},{7,6},{8,9},{9,8},{10,11... | collective-permute-start | bytes 49160 | tf_op jit(solution)/shard_map/ppermute | solution.py:84
  103.4 7.7 %collective-permute-start.22 = (bf16[64,128]{1,0:T(8,128)(2,1)S(1)}, bf16[64,128]{1,0:T(8,128)(2,1)S(1)}, u32[]{:S(2)}, u32[]{:S(2)}) collective-permute-start(bf16[64,128]{1,0:T(8,128)(2,1)S(1)} %collective-permute-done.21.near), channel_id=1, source_target_pairs={{0,4},{4,0},{8,12},{12,8},{16,20},{20,16},{24,28},{28,24},{1,5},{5... | collective-permute-start | bytes 49160 | tf_op jit(solution)/shard_map/ppermute | solution.py:80
  111.1 12.9 %collective-permute-start.23 = (bf16[48,4096]{1,0:T(8,128)(2,1)S(1)}, bf16[48,4096]{1,0:T(8,128)(2,1)S(1)}, u32[]{:S(2)}, u32[]{:S(2)}) collective-permute-start(bf16[48,4096]{1,0:T(8,128)(2,1)S(1)} %get-tuple-element.152), channel_id=1, source_target_pairs={{0,24},{4,28},{8,16},{12,20},{16,8},{20,12},{24,0},{28,4},{1,25},{... | collective-permute-start | bytes 1179656 | tf_op jit(solution)/shard_map/ppermute | solution.py:80
  113.6 20.1 %collective-permute-start.24 = (bf16[48,4096]{1,0:T(8,128)(2,1)S(1)}, bf16[48,4096]{1,0:T(8,128)(2,1)S(1)}, u32[]{:S(2)}, u32[]{:S(2)}) collective-permute-start(bf16[48,4096]{1,0:T(8,128)(2,1)S(1)} %get-tuple-element.158), channel_id=1, source_target_pairs={{0,8},{4,12},{8,0},{12,4},{16,24},{20,28},{24,16},{28,20},{1,9},{5... | collective-permute-start | bytes 1179656 | tf_op jit(solution)/shard_map/ppermute | solution.py:80
  114.2 19.5 %collective-permute-start.25 = (bf16[48,4096]{1,0:T(8,128)(2,1)S(1)}, bf16[48,4096]{1,0:T(8,128)(2,1)S(1)}, u32[]{:S(2)}, u32[]{:S(2)}) collective-permute-start(bf16[48,4096]{1,0:T(8,128)(2,1)S(1)} %get-tuple-element.159), channel_id=1, source_target_pairs={{0,16},{4,20},{8,24},{12,28},{16,0},{20,4},{24,8},{28,12},{1,17},{... | collective-permute-start | bytes 1179656 | tf_op jit(solution)/shard_map/ppermute | solution.py:80
  133.7 2.0 %collective-permute-start.30 = (bf16[64,4096]{1,0:T(8,128)(2,1)S(1)}, bf16[64,4096]{1,0:T(8,128)(2,1)S(1)}, u32[]{:S(2)}, u32[]{:S(2)}) collective-permute-start(bf16[64,4096]{1,0:T(8,128)(2,1)S(1)} %get-tuple-element.183), channel_id=1, source_target_pairs={{0,4},{4,0},{8,12},{12,8},{16,20},{20,16},{24,28},{28,24},{1,5},{5... | collective-permute-start | bytes 1572872 | tf_op jit(solution)/shard_map/ppermute | solution.py:80
  135.8 20.7 %collective-permute-start.31 = (bf16[64,4096]{1,0:T(8,128)(2,1)S(1)}, bf16[64,4096]{1,0:T(8,128)(2,1)S(1)}, u32[]{:S(2)}, u32[]{:S(2)}) collective-permute-start(bf16[64,4096]{1,0:T(8,128)(2,1)S(1)} %add_convert_fusion.3), channel_id=1, source_target_pairs={{0,1},{1,0},{2,3},{3,2},{4,5},{5,4},{6,7},{7,6},{8,9},{9,8},{10,11... | collective-permute-start | bytes 1572872 | tf_op jit(solution)/shard_map/ppermute | solution.py:84
  136.1 12.9 %collective-permute-start.27 = (bf16[48,4096]{1,0:T(8,128)(2,1)S(1)}, bf16[48,4096]{1,0:T(8,128)(2,1)S(1)}, u32[]{:S(2)}, u32[]{:S(2)}) collective-permute-start(bf16[48,4096]{1,0:T(8,128)(2,1)S(1)} %get-tuple-element.178), channel_id=1, source_target_pairs={{0,24},{4,28},{8,16},{12,20},{16,8},{20,12},{24,0},{28,4},{1,25},{... | collective-permute-start | bytes 1179656 | tf_op jit(solution)/shard_map/ppermute | solution.py:80
  138.6 17.9 %collective-permute-start.28 = (bf16[48,4096]{1,0:T(8,128)(2,1)S(1)}, bf16[48,4096]{1,0:T(8,128)(2,1)S(1)}, u32[]{:S(2)}, u32[]{:S(2)}) collective-permute-start(bf16[48,4096]{1,0:T(8,128)(2,1)S(1)} %get-tuple-element.179), channel_id=1, source_target_pairs={{0,8},{4,12},{8,0},{12,4},{16,24},{20,28},{24,16},{28,20},{1,9},{5... | collective-permute-start | bytes 1179656 | tf_op jit(solution)/shard_map/ppermute | solution.py:80
  139.1 17.4 %collective-permute-start.29 = (bf16[48,4096]{1,0:T(8,128)(2,1)S(1)}, bf16[48,4096]{1,0:T(8,128)(2,1)S(1)}, u32[]{:S(2)}, u32[]{:S(2)}) collective-permute-start(bf16[48,4096]{1,0:T(8,128)(2,1)S(1)} %get-tuple-element.180), channel_id=1, source_target_pairs={{0,16},{4,20},{8,24},{12,28},{16,0},{20,4},{24,8},{28,12},{1,17},{... | collective-permute-start | bytes 1179656 | tf_op jit(solution)/shard_map/ppermute | solution.py:80
  156.5 2.3 %collective-permute-start.37 = (bf16[64,4096]{1,0:T(8,128)(2,1)S(1)}, bf16[64,4096]{1,0:T(8,128)(2,1)S(1)}, u32[]{:S(2)}, u32[]{:S(2)}) collective-permute-start(bf16[64,4096]{1,0:T(8,128)(2,1)S(1)} %get-tuple-element.207), channel_id=1, source_target_pairs={{0,4},{4,0},{8,12},{12,8},{16,20},{20,16},{24,28},{28,24},{1,5},{5... | collective-permute-start | bytes 1572872 | tf_op jit(solution)/shard_map/ppermute | solution.py:80
  158.3 2.4 %collective-permute-start.35 = (bf16[64,4096]{1,0:T(8,128)(2,1)S(1)}, bf16[64,4096]{1,0:T(8,128)(2,1)S(1)}, u32[]{:S(2)}, u32[]{:S(2)}) collective-permute-start(bf16[64,4096]{1,0:T(8,128)(2,1)S(1)} %get-tuple-element.205), channel_id=1, source_target_pairs={{0,4},{4,0},{8,12},{12,8},{16,20},{20,16},{24,28},{28,24},{1,5},{5... | collective-permute-start | bytes 1572872 | tf_op jit(solution)/shard_map/ppermute | solution.py:80
  159.0 26.1 %collective-permute-start.38 = (bf16[64,4096]{1,0:T(8,128)(2,1)S(1)}, bf16[64,4096]{1,0:T(8,128)(2,1)S(1)}, u32[]{:S(2)}, u32[]{:S(2)}) collective-permute-start(bf16[64,4096]{1,0:T(8,128)(2,1)S(1)} %add_convert_fusion.1), channel_id=1, source_target_pairs={{0,2},{1,3},{2,0},{3,1},{4,6},{5,7},{6,4},{7,5},{8,10},{9,11},{10,... | collective-permute-start | bytes 1572872 | tf_op jit(solution)/shard_map/ppermute | solution.py:84
  160.8 24.3 %collective-permute-start.36 = (bf16[64,4096]{1,0:T(8,128)(2,1)S(1)}, bf16[64,4096]{1,0:T(8,128)(2,1)S(1)}, u32[]{:S(2)}, u32[]{:S(2)}) collective-permute-start(bf16[64,4096]{1,0:T(8,128)(2,1)S(1)} %add_convert_fusion.2), channel_id=1, source_target_pairs={{0,1},{1,0},{2,3},{3,2},{4,5},{5,4},{6,7},{7,6},{8,9},{9,8},{10,11... | collective-permute-start | bytes 1572872 | tf_op jit(solution)/shard_map/ppermute | solution.py:84
  162.3 12.9 %collective-permute-start.32 = (bf16[48,4096]{1,0:T(8,128)(2,1)S(1)}, bf16[48,4096]{1,0:T(8,128)(2,1)S(1)}, u32[]{:S(2)}, u32[]{:S(2)}) collective-permute-start(bf16[48,4096]{1,0:T(8,128)(2,1)S(1)} %get-tuple-element.194), channel_id=1, source_target_pairs={{0,24},{4,28},{8,16},{12,20},{16,8},{20,12},{24,0},{28,4},{1,25},{... | collective-permute-start | bytes 1179656 | tf_op jit(solution)/shard_map/ppermute | solution.py:80
  164.6 18.1 %collective-permute-start.33 = (bf16[48,4096]{1,0:T(8,128)(2,1)S(1)}, bf16[48,4096]{1,0:T(8,128)(2,1)S(1)}, u32[]{:S(2)}, u32[]{:S(2)}) collective-permute-start(bf16[48,4096]{1,0:T(8,128)(2,1)S(1)} %get-tuple-element.195), channel_id=1, source_target_pairs={{0,8},{4,12},{8,0},{12,4},{16,24},{20,28},{24,16},{28,20},{1,9},{5... | collective-permute-start | bytes 1179656 | tf_op jit(solution)/shard_map/ppermute | solution.py:80
  165.1 17.6 %collective-permute-start.34 = (bf16[48,4096]{1,0:T(8,128)(2,1)S(1)}, bf16[48,4096]{1,0:T(8,128)(2,1)S(1)}, u32[]{:S(2)}, u32[]{:S(2)}) collective-permute-start(bf16[48,4096]{1,0:T(8,128)(2,1)S(1)} %get-tuple-element.196), channel_id=1, source_target_pairs={{0,16},{4,20},{8,24},{12,28},{16,0},{20,4},{24,8},{28,12},{1,17},{... | collective-permute-start | bytes 1179656 | tf_op jit(solution)/shard_map/ppermute | solution.py:80
  175.2 9.9 %collective-permute-start = (bf16[64,128]{1,0:T(8,128)(2,1)S(1)}, bf16[64,128]{1,0:T(8,128)(2,1)S(1)}, u32[]{:S(2)}, u32[]{:S(2)}) collective-permute-start(bf16[64,128]{1,0:T(8,128)(2,1)S(1)} %pad_maximum_fusion.near), channel_id=1, source_target_pairs={{0,4},{4,0},{8,12},{12,8},{16,20},{20,16},{24,28},{28,24},{1,5},{5... | collective-permute-start | bytes 49160 | tf_op jit(solution)/shard_map/ppermute | solution.py:80
  186.8 2.0 %collective-permute-start.39 = (bf16[64,4096]{1,0:T(8,128)(2,1)S(1)}, bf16[64,4096]{1,0:T(8,128)(2,1)S(1)}, u32[]{:S(2)}, u32[]{:S(2)}) collective-permute-start(bf16[64,4096]{1,0:T(8,128)(2,1)S(1)} %get-tuple-element.214), channel_id=1, source_target_pairs={{0,4},{4,0},{8,12},{12,8},{16,20},{20,16},{24,28},{28,24},{1,5},{5... | collective-permute-start | bytes 1572872 | tf_op jit(solution)/shard_map/ppermute | solution.py:80
